TPU v7x, 32 devices: a whole 2x2x4 slice. The times are simulated.
32 devices in a mesh: ctx: 8 (over z, x), fsdp: 4 (over y, core).
Axes of the slice: x: 2, y: 2, z: 4, core: 2. Of those that a mesh axis runs over, the one named last changes fastest.
Arguments:
- tokens: bfloat16 [4, 1024, 1536], P('fsdp', 'ctx'), may hold values from -6 to 6
- query_key_value_weight: bfloat16 [1536, 2560], P('fsdp'), may hold values from -0.15625 to 0.15625
- output_weight: bfloat16 [1536, 1536], P('fsdp'), may hold values from -0.75 to 0.75
- routing_weight: bfloat16 [1536, 8], P('fsdp'), may hold values from -0.109375 to 0.109375
- gain_attn: bfloat16 [1536], P('fsdp'), may hold values from 0.5 to 1.5
- gain_moe: bfloat16 [1536], P('fsdp'), may hold values from 0.5 to 1.5
- w_experts: bfloat16 [8, 1536, 3072], P('fsdp'), may hold values from -0.15625 to 0.15625
- doc_starts: int32 [4, 8], P('fsdp'), may hold values from 0 to 1023, as said below
- routes: int32 [4, 1024, 2], P('fsdp', 'ctx'), may hold values from 0 to 7, all different within a row; in each aligned block of 128 rows (0 to 127, 128 to 255, ..., all dimensions but the last counted through in order) at most 64 rows name the same one
- cotangent: bfloat16 [4, 1024, 1536], P('fsdp', 'ctx'), may hold values from -6 to 6
Outputs:
- output: bfloat16 [4, 1024, 1536], P('fsdp', 'ctx')
- d_tokens: bfloat16 [4, 1024, 1536], P('fsdp', 'ctx')
- d_w_qkv: float32 [1536, 2560], P('fsdp')
- d_w_out: float32 [1536, 1536], P('fsdp')
- d_w_router: float32 [1536, 8], P('fsdp')
- d_gain_attn: float32 [1536], P('fsdp')
- d_gain_moe: float32 [1536], P('fsdp')
- d_w_experts: float32 [8, 1536, 3072], P('fsdp')
Inputs may be any that keep to these rules, and one draw needn't show every extreme that they name: `doc_starts`: in each stream the starts begin with 0 and rise strictly; one document begins within the first 128 positions and ends within the last 128. `routes`: A token's two experts differ. Among the 128 tokens of one device each expert is named at most 64 times, a bound that some block reaches.
All inputs are finite; a program needn't handle non-finite values.
Results may differ from a plain program's by a relative error of at most 0.025.
Values may be sent and summed in bfloat16 or wider, within the bound.
No kernel may reach another device: no remote copies, remote signals or barrier semaphores. Data moves between devices by JAX's collectives and lax.ppermute only.
A program may use at most 640 MiB of HBM per device.

v0:
```python
import math

import jax
import jax.numpy as jnp
from jax import lax
from jax.sharding import PartitionSpec as P

D = 1536
HQ = 24
HK = 8
HD = 64
FF = 1024
EXPERTS = 8
TOP = 2
CAP = 64


NORM_EPS = 1e-05
MASK_NEG = -1e30


def shifted(block, axis, distance):
    devices = range(lax.axis_size(axis))
    route = [(i - distance, i) for i in devices if i - distance in devices]
    return lax.ppermute(block, axis, route)


def passed_along(value, axis, steps):
    count = lax.axis_size(axis)
    pairs = [(source, (source + steps) % count) for source in range(count)]
    return lax.ppermute(value, axis, pairs)


def rms_forward(values, gain_vec):
    factor = lax.rsqrt(jnp.mean(values * values, axis=-1, keepdims=True) + NORM_EPS)
    return (values * factor * gain_vec, factor)


def rms_backward(values, factor, gain_vec, incoming):
    inner = incoming * gain_vec
    d_gain = jnp.sum(incoming * values * factor, axis=0)
    cubed = factor * factor * factor
    d_values = factor * inner - values * cubed * jnp.mean(inner * values, axis=-1, keepdims=True)
    return (d_values, d_gain)


def doc_index(doc_bounds, positions):
    hits = (positions[:, None] >= doc_bounds[None, :]).astype(jnp.int32)
    return jnp.sum(hits, axis=1)


def visible_mask(query_pos, query_doc, key_pos, doc_bounds):
    key_doc = doc_index(doc_bounds, key_pos)
    return (key_pos[None, :] <= query_pos[:, None]) & (key_doc[None, :] == query_doc[:, None])


def route_slots(choices):
    flat_ids = choices.reshape(-1)
    one_hot = (flat_ids[:, None] == jnp.arange(EXPERTS, dtype=jnp.int32)[None, :]).astype(jnp.int32)
    ranking = jnp.sum((jnp.cumsum(one_hot, axis=0) - 1) * one_hot, axis=1)
    return flat_ids * CAP + ranking


def slot_owner(route_slot):
    route_total = route_slot.shape[0]
    slot_source = (
        jnp.zeros((EXPERTS * CAP,), jnp.int32)
        .at[route_slot]
        .set(jnp.arange(route_total, dtype=jnp.int32))
    )
    slot_filled = (
        jnp.zeros((EXPERTS * CAP,), jnp.int32)
        .at[route_slot]
        .set(jnp.ones((route_total,), jnp.int32))
    )
    return (slot_source, slot_filled)


def expert_apply(rows_in, kernel):
    both = jnp.einsum(
        "...ecd,edf->...ecf", rows_in, kernel[:, :, : 2 * FF], preferred_element_type=jnp.float32
    )
    hidden = (jax.nn.silu(both[..., :FF]) * both[..., FF:]).astype(jnp.bfloat16)
    result = jnp.einsum(
        "...ecf,edf->...ecd", hidden, kernel[:, :, 2 * FF :], preferred_element_type=jnp.float32
    )
    return result.astype(jnp.bfloat16)


def expert_grad(rows_in, grad_out, kernel):
    both = jnp.einsum(
        "...ecd,edf->...ecf", rows_in, kernel[:, :, : 2 * FF], preferred_element_type=jnp.float32
    )
    gate_part = both[..., :FF]
    up_part = both[..., FF:]
    sigma = jax.nn.sigmoid(gate_part)
    hidden = (jax.nn.silu(gate_part) * up_part).astype(jnp.bfloat16)
    d_hidden = jnp.einsum(
        "...ecd,edf->...ecf", grad_out, kernel[:, :, 2 * FF :], preferred_element_type=jnp.float32
    )
    d_gate = d_hidden * up_part * sigma * (1.0 + gate_part * (1.0 - sigma))
    d_up = d_hidden * gate_part * sigma
    d_both = jnp.concatenate([d_gate, d_up], axis=-1).astype(jnp.bfloat16)
    d_rows = jnp.einsum(
        "...ecf,edf->...ecd", d_both, kernel[:, :, : 2 * FF], preferred_element_type=jnp.float32
    )
    return (d_rows.astype(jnp.bfloat16), d_both, hidden)


def expert_kernel_grad(leading, rows_in, d_both, grad_out, hidden):
    d_inward = jnp.einsum(
        leading + "ecd," + leading + "ecf->edf", rows_in, d_both, preferred_element_type=jnp.float32
    )
    d_down = jnp.einsum(
        leading + "ecd," + leading + "ecf->edf",
        grad_out,
        hidden,
        preferred_element_type=jnp.float32,
    )
    return jnp.concatenate([d_inward, d_down], axis=-1)


def per_device(
    tokens,
    query_key_value_weight,
    output_weight,
    routing_weight,
    gain_attn,
    gain_moe,
    w_experts,
    doc_starts,
    routes,
    cotangent,
):
    input_rows = tokens[0].astype(jnp.float32)
    tok_count = input_rows.shape[0]
    head_group = HQ // HK
    kv_width = HK * HD
    q_scale = HD ** (-0.5)
    cycle_size = lax.axis_size("ctx")
    my_index = lax.axis_index("ctx")
    doc_bounds = doc_starts[0]
    choices = routes[0]
    qkv_w, out_w, router_w, attn_gain, moe_gain = (
        lax.all_gather(query_key_value_weight, "fsdp", axis=0, tiled=True),
        lax.all_gather(output_weight, "fsdp", axis=0, tiled=True),
        lax.all_gather(routing_weight, "fsdp", axis=0, tiled=True),
        lax.all_gather(gain_attn, "fsdp", axis=0, tiled=True),
        lax.all_gather(gain_moe, "fsdp", axis=0, tiled=True),
    )
    attn_g = attn_gain.astype(jnp.float32)
    moe_g = moe_gain.astype(jnp.float32)
    first_f, first_factor = rms_forward(input_rows, attn_g)
    normalized_rows = first_f.astype(jnp.bfloat16)
    projected = jnp.dot(normalized_rows, qkv_w, preferred_element_type=jnp.float32).astype(
        jnp.bfloat16
    )
    queries = projected[:, : HQ * HD].reshape(tok_count, HK, head_group, HD)
    kv_pairs = projected[:, HQ * HD :]
    query_pos = my_index * tok_count + jnp.arange(tok_count, dtype=jnp.int32)
    query_doc = doc_index(doc_bounds, query_pos)
    start_state = (
        jnp.full((HK, head_group, tok_count), MASK_NEG, jnp.float32),
        jnp.zeros((HK, head_group, tok_count), jnp.float32),
        jnp.zeros((HK, head_group, tok_count, HD), jnp.float32),
    )
    shard_pairs = lax.all_gather(kv_pairs, "ctx", axis=0, tiled=True)
    span = shard_pairs.shape[0]
    k_block = math.gcd(span, 512)
    blocks = shard_pairs.reshape(span // k_block, k_block, 2 * kv_width)
    offsets = k_block * jnp.arange(span // k_block, dtype=jnp.int32)

    def one_block(state, item):
        run_max, run_sum, run_out = state
        block_pairs, offset = item
        key_rows = block_pairs[:, :kv_width].reshape(k_block, HK, HD)
        value_rows = block_pairs[:, kv_width:].reshape(k_block, HK, HD)
        key_pos = offset + jnp.arange(k_block, dtype=jnp.int32)
        allowed = visible_mask(query_pos, query_doc, key_pos, doc_bounds)
        scores = (
            jnp.einsum("tkgd,skd->kgts", queries, key_rows, preferred_element_type=jnp.float32)
            * q_scale
        )
        new_max = jnp.maximum(run_max, jnp.max(jnp.where(allowed, scores, MASK_NEG), axis=-1))
        prob_block = jnp.where(allowed, jnp.exp(scores - new_max[..., None]), 0.0)
        shrink = jnp.exp(run_max - new_max)
        run_sum = run_sum * shrink + jnp.sum(prob_block, axis=-1)
        run_out = run_out * shrink[..., None] + jnp.einsum(
            "kgts,skd->kgtd",
            prob_block.astype(jnp.bfloat16),
            value_rows,
            preferred_element_type=jnp.float32,
        )
        return ((new_max, run_sum, run_out), None)

    state_out, unused = lax.scan(one_block, start_state, (blocks, offsets))
    run_max, run_sum, run_out = state_out
    log_norm = run_max + jnp.log(run_sum)
    attention_result = (
        (run_out / run_sum[..., None]).transpose(2, 0, 1, 3).reshape(tok_count, HQ * HD)
    )
    attended_low = attention_result.astype(jnp.bfloat16)
    midway_state = input_rows + jnp.dot(attended_low, out_w, preferred_element_type=jnp.float32)
    second_f, second_factor = rms_forward(midway_state, moe_g)
    second_branch = second_f.astype(jnp.bfloat16)
    router_scores = jnp.dot(second_branch, router_w, preferred_element_type=jnp.float32)
    gates = jax.nn.softmax(jnp.take_along_axis(router_scores, choices, axis=1), axis=-1)
    route_slot = route_slots(choices)
    slot_source, slot_filled = slot_owner(route_slot)
    empty_row = jnp.zeros((), jnp.bfloat16)
    expert_in = jnp.where(
        slot_filled[:, None] > 0, second_branch[slot_source // TOP], empty_row
    ).reshape(EXPERTS, CAP, D)
    rows_in = expert_in
    expert_out = expert_apply(rows_in, lax.all_gather(w_experts, "fsdp", axis=0, tiled=True))
    route_out = (
        expert_out.reshape(EXPERTS * CAP, D)[route_slot]
        .astype(jnp.float32)
        .reshape(tok_count, TOP, D)
    )
    output = (midway_state + jnp.sum(gates[:, :, None] * route_out, axis=1)).astype(jnp.bfloat16)
    grad_y = cotangent[0].astype(jnp.float32)
    d_gates = jnp.sum(grad_y[:, None, :] * route_out, axis=-1)
    route_grad = (
        (gates[:, :, None] * grad_y[:, None, :]).astype(jnp.bfloat16).reshape(tok_count * TOP, D)
    )
    grad_buffer = jnp.where(slot_filled[:, None] > 0, route_grad[slot_source], empty_row).reshape(
        EXPERTS, CAP, D
    )
    d_picked = gates * (d_gates - jnp.sum(gates * d_gates, axis=-1, keepdims=True))
    expert_hot = (
        choices[:, :, None] == jnp.arange(EXPERTS, dtype=jnp.int32)[None, None, :]
    ).astype(jnp.float32)
    d_logits = jnp.sum(expert_hot * d_picked[:, :, None], axis=1).astype(jnp.bfloat16)
    d_router = jnp.einsum("td,te->de", second_branch, d_logits, preferred_element_type=jnp.float32)
    d_second = jnp.einsum("te,de->td", d_logits, router_w, preferred_element_type=jnp.float32)
    rows_in = expert_in
    d_rows, d_both, hidden = expert_grad(
        rows_in, grad_buffer, lax.all_gather(w_experts, "fsdp", axis=0, tiled=True)
    )
    joined_back = jnp.concatenate([d_rows, d_both, hidden], axis=-1)
    d_expert_in = joined_back[..., :D]
    d_both_all = joined_back[..., D : D + 2 * FF]
    hidden_all = joined_back[..., D + 2 * FF :]
    d_experts = lax.psum_scatter(
        expert_kernel_grad("", expert_in, d_both_all, grad_buffer, hidden_all).astype(jnp.bfloat16),
        "fsdp",
        scatter_dimension=0,
        tiled=True,
    )
    d_routes = (
        d_expert_in.reshape(EXPERTS * CAP, D)[route_slot]
        .astype(jnp.float32)
        .reshape(tok_count, TOP, D)
    )
    d_second = d_second + jnp.sum(d_routes, axis=1)
    d_middle_norm, d_moe_gain = rms_backward(midway_state, second_factor, moe_g, d_second)
    d_middle = grad_y + d_middle_norm
    d_proj = d_middle.astype(jnp.bfloat16)
    d_out_w = jnp.einsum("te,td->ed", attended_low, d_proj, preferred_element_type=jnp.float32)
    d_attended = jnp.einsum("td,ed->te", d_proj, out_w, preferred_element_type=jnp.float32).astype(
        jnp.bfloat16
    )
    grad_heads = d_attended.reshape(tok_count, HK, head_group, HD)
    attended_heads = attention_result.reshape(tok_count, HK, head_group, HD)
    row_delta = jnp.sum(grad_heads.astype(jnp.float32) * attended_heads, axis=-1).transpose(1, 2, 0)
    key_rows = kv_pairs[:, :kv_width].reshape(tok_count, HK, HD)
    value_rows = kv_pairs[:, kv_width:].reshape(tok_count, HK, HD)
    key_pos = query_pos
    step_rows = jnp.arange(tok_count, dtype=jnp.int32)

    def cycle_step(step, state):
        q_rows, g_rows, lse_rows, delta_rows, d_query, pair_grads = state
        source = (my_index + step) % cycle_size
        source_pos = source * tok_count + step_rows
        source_doc = doc_index(doc_bounds, source_pos)
        allowed = visible_mask(source_pos, source_doc, key_pos, doc_bounds)
        scores = (
            jnp.einsum("tkgd,skd->kgts", q_rows, key_rows, preferred_element_type=jnp.float32)
            * q_scale
        )
        prob_block = jnp.where(allowed, jnp.exp(scores - lse_rows[..., None]), 0.0)
        d_probs = jnp.einsum(
            "tkgd,skd->kgts", g_rows, value_rows, preferred_element_type=jnp.float32
        )
        d_scores = (prob_block * (d_probs - delta_rows[..., None])).astype(jnp.bfloat16)
        d_query = (
            d_query
            + jnp.einsum("kgts,skd->tkgd", d_scores, key_rows, preferred_element_type=jnp.float32)
            * q_scale
        )
        d_keys = (
            jnp.einsum("kgts,tkgd->skd", d_scores, q_rows, preferred_element_type=jnp.float32)
            * q_scale
        )
        d_values = jnp.einsum(
            "kgts,tkgd->skd",
            prob_block.astype(jnp.bfloat16),
            g_rows,
            preferred_element_type=jnp.float32,
        )
        pair_grads = pair_grads + jnp.concatenate(
            [d_keys.reshape(tok_count, kv_width), d_values.reshape(tok_count, kv_width)], axis=1
        )
        q_rows, g_rows = shifted((q_rows, g_rows), "ctx", -1)
        lse_rows, delta_rows, d_query = (
            passed_along(lse_rows.astype(jnp.bfloat16), "ctx", -1).astype(lse_rows.dtype),
            passed_along(delta_rows.astype(jnp.bfloat16), "ctx", -1).astype(delta_rows.dtype),
            passed_along(d_query.astype(jnp.bfloat16), "ctx", -1).astype(d_query.dtype),
        )
        return (q_rows, g_rows, lse_rows, delta_rows, d_query, pair_grads)

    cycle_start = (
        queries,
        grad_heads,
        log_norm,
        row_delta,
        jnp.zeros((tok_count, HK, head_group, HD), jnp.float32),
        jnp.zeros((tok_count, 2 * kv_width), jnp.float32),
    )
    cycle_end = lax.fori_loop(0, cycle_size, cycle_step, cycle_start)
    d_query = cycle_end[4]
    pair_grads = cycle_end[5]
    d_mixed = jnp.concatenate([d_query.reshape(tok_count, HQ * HD), pair_grads], axis=1).astype(
        jnp.bfloat16
    )
    d_qkv_w = jnp.einsum("td,te->de", normalized_rows, d_mixed, preferred_element_type=jnp.float32)
    d_normed = jnp.einsum("te,de->td", d_mixed, qkv_w, preferred_element_type=jnp.float32)
    d_first, d_attn_gain = rms_backward(input_rows, first_factor, attn_g, d_normed)
    d_tokens = (d_middle + d_first).astype(jnp.bfloat16)
    qkv_part, out_part, router_part, attn_part, moe_part = (
        lax.psum_scatter(
            d_qkv_w.astype(jnp.bfloat16), "fsdp", scatter_dimension=0, tiled=True
        ).astype(jnp.float32),
        lax.psum_scatter(
            d_out_w.astype(jnp.bfloat16), "fsdp", scatter_dimension=0, tiled=True
        ).astype(jnp.float32),
        lax.psum_scatter(
            d_router.astype(jnp.bfloat16), "fsdp", scatter_dimension=0, tiled=True
        ).astype(jnp.float32),
        lax.psum_scatter(
            d_attn_gain.astype(jnp.bfloat16), "fsdp", scatter_dimension=0, tiled=True
        ).astype(jnp.float32),
        lax.psum_scatter(
            d_moe_gain.astype(jnp.bfloat16), "fsdp", scatter_dimension=0, tiled=True
        ).astype(jnp.float32),
    )
    qkv_sum, out_sum, router_sum, attn_sum, moe_sum, expert_sum = (
        lax.psum(qkv_part.astype(jnp.bfloat16), "ctx").astype(jnp.float32),
        lax.psum(out_part.astype(jnp.bfloat16), "ctx").astype(jnp.float32),
        lax.psum(router_part.astype(jnp.bfloat16), "ctx").astype(jnp.float32),
        lax.psum(attn_part.astype(jnp.bfloat16), "ctx").astype(jnp.float32),
        lax.psum(moe_part.astype(jnp.bfloat16), "ctx").astype(jnp.float32),
        lax.psum(d_experts, "ctx").astype(jnp.float32),
    )
    return (
        output[None],
        d_tokens[None],
        qkv_sum,
        out_sum,
        router_sum,
        attn_sum,
        moe_sum,
        expert_sum,
    )


def solution(mesh):
    placed = (
        P("fsdp", "ctx", None),
        P("fsdp", None),
        P("fsdp", None),
        P("fsdp", None),
        P("fsdp"),
        P("fsdp"),
        P("fsdp", None, None),
        P("fsdp", None),
        P("fsdp", "ctx", None),
        P("fsdp", "ctx", None),
    )
    return jax.shard_map(
        per_device,
        mesh=mesh,
        in_specs=placed,
        out_specs=(
            P("fsdp", "ctx", None),
            P("fsdp", "ctx", None),
            P("fsdp", None),
            P("fsdp", None),
            P("fsdp", None),
            P("fsdp"),
            P("fsdp"),
            P("fsdp", None, None),
        ),
        check_vma=False,
    )
```

profile of v0, /device:TPU:0, one launch (start us, length us, event | category | flops | bytes accessed | tf_op | source)
XLA Modules:
  0.0 2282.3 jit_solution(1352900257678978116)
XLA Ops:
  8.6 6.1 all-gather
  15.6 52.1 %all-gather.7.cloned.1.call-done = bf16[1536,2560]{1,0:T(8,128)(2,1)} async-done(((bf16[384,2560]{1,0:T(8,128)(2,1)}), bf16[1536,2560]{1,0:T(8,128)(2,1)}) %all-gather.7.cloned.1.call-update) | async-done | bytes 7864336 | tf_op jit(solution)/shard_map/all_gather | solution.py:145
  67.6 4.5 convolution_convert_fusion.4
  74.8 5.2 all-gather.1
  87.1 2.2 mul.360
  89.3 5.7 all_gather.27
  98.7 23.6 %all-gather.9.cloned.1.call-done = bf16[1024,1024]{1,0:T(8,128)(2,1)} async-done(((bf16[128,1024]{1,0:T(8,128)(2,1)}), bf16[1024,1024]{1,0:T(8,128)(2,1)}) %all-gather.9.cloned.1.call-update) | async-done | bytes 2097168 | tf_op jit(solution)/shard_map/all_gather | solution.py:167
  122.3 17.9 while.41
  141.5 18.4 all-gather.11.cloned.1.call-done
  159.9 3.3 multiply_reduce_fusion.4
  167.2 2.9 gather_fusion
  170.3 2.3 gather_fusion.2
  174.0 1.7 fusion.69
  175.7 427.3 %all-gather.13.cloned.1.call-done = bf16[8,1536,3072]{2,1,0:T(8,128)(2,1)} async-done(((bf16[2,1536,3072]{2,1,0:T(8,128)(2,1)}), bf16[8,1536,3072]{2,1,0:T(8,128)(2,1)}) %all-gather.13.cloned.1.call-update) | async-done | bytes 75497488 | tf_op jit(solution)/shard_map/all_gather | solution.py:215
  603.0 24.8 %fusion.35 = f32[8,64,2048]{2,1,0:T(8,128)} fusion(bf16[8,1536,3072]{2,1,0:T(8,128)(2,1)} %all-gather.13.cloned.1.call-done, bf16[8,64,1536]{2,1,0:T(8,128)(2,1)} %bitcast.225, pred[8,64]{1,0:T(8,128)(4,1)} %broadcast_in_dim.148), kind=kOutput, calls=%fused_computation.58 | convolution fusion | flops 3222011904 | bytes 56099840 | tf_op jit(solution)/shard_map/...ecd,edf->...ecf/dot_general | solution.py:80
  627.8 13.8 multiply_convert_fusion.1
  641.6 12.8 fusion.44
  654.4 2.1 gather_fusion.1
  656.5 22.1 fusion.41
  678.6 2.1 gather_fusion.3
  680.8 2.2 reshape.389
  683.0 2.9 reshape.387
  685.9 5.0 multiply_reduce_fusion
  693.3 3.0 reduce_sum.197
  697.0 2.2 multiply_reduce_fusion.2
  700.4 3.6 convolution_convert_fusion.3
  704.0 4.0 convolution_convert_fusion.5
  709.5 251.3 %while.42 = (s32[]{:T(128)}, bf16[128,8,3,64]{0,3,2,1:T(8,128)(2,1)S(1)}, bf16[128,8,3,64]{0,3,2,1:T(8,128)(2,1)S(1)}, f32[8,3,128]{2,1,0:T(4,128)}, f32[8,3,128...) while((s32[]{:T(128)}, ...), condition=%wide.region_25.26_spmd.clone, body=%wide.region_22.25_spmd.clone.sunk | while | flops 255920144 | bytes 19977756 | solution.py:321
  711.1 4.3 collective-permute-start.2
  722.0 4.7 collective-permute-start.4
  729.8 16.2 collective-permute-done.4
  749.1 2.0 collective-permute-start.3
  756.6 5.6 collective-permute-start.4
  765.3 13.9 collective-permute-done.4
  782.5 2.6 collective-permute-start.3
  790.5 8.6 collective-permute-start.4
  802.2 9.9 collective-permute-done.4
  816.1 3.4 collective-permute-start.3
  824.9 6.3 collective-permute-start.4
  834.3 10.6 collective-permute-done.4
  848.9 2.6 collective-permute-start.3
  856.9 5.3 collective-permute-start.4
  865.3 10.7 collective-permute-done.4
  880.1 2.6 collective-permute-start.3
  888.2 4.4 collective-permute-start.4
  895.7 10.7 collective-permute-done.4
  909.5 2.2 collective-permute-start.3
  917.2 4.7 collective-permute-start.4
  924.9 9.7 collective-permute-done.4
  944.2 7.5 collective-permute-start.4
  954.8 4.9 collective-permute-done.4
  961.8 6.2 convolution_convert_fusion.2
  969.4 15.4 convolution_convert_fusion.1
  984.8 22.5 convolution_convert_fusion
  1007.3 49.6 %pad_maximum_fusion = bf16[8,1536,3072]{2,1,0:T(8,128)(2,1)} fusion(bf16[8,1536,1024]{2,1,0:T(8,128)(2,1)} %convolution_convert_fusion.1, bf16[8,1536,2048]{2,1,0:T(8,128)(2,1)} %convolution_convert_fusion), kind=kLoop, calls=%fused_computation.55 | loop fusion | flops 150994944 | bytes 150994944 | tf_op jit(solution)/shard_map/concatenate | solution.py:120
  1059.5 503.5 %reduce-scatter.11.cloned.1.call-done = bf16[2,1536,3072]{2,1,0:T(8,128)(2,1)} async-done(((bf16[8,1536,3072]{2,1,0:T(8,128)(2,1)}), bf16[2,1536,3072]{2,1,0:T(8,128)(2,1)}) %reduce-scatter.11.cloned.1.call-update) | async-done | bytes 18874384 | tf_op jit(solution)/shard_map/reduce_scatter | solution.py:245
  1564.9 6.1 fusion.56
  1571.1 5.9 all-reduce.4
  1578.2 8.8 reduce-scatter.13.cloned.1.call-done
  1588.0 22.0 all-reduce.2
  1611.8 636.7 %all-reduce.7.cloned.1.call-done = (bf16[384,2560]{1,0:T(8,128)(2,1)}, bf16[384,1536]{1,0:T(8,128)(2,1)}, bf16[2,1536,3072]{2,1,0:T(8,128)(2,1)}) async-done(((bf16[384,2560]{1,0:T(8,128)(2,1)}, bf16[384,1536]{1,0:T(8,128)(2,1)}, bf16[2,1536,3072]{2,1,0:T(8,128)(2,1)}), (bf16[384,2560]{1,0:T(8,128)(2,1)}, bf16[384,1536]{1,0:T(8,128)(2,1)}, bf16[2,1536,3072]{2,1,0:T(8,128)(2,1)})) %all-reduce.7.cloned.1.call-update) | async-done | bytes 22020112 | tf_op jit(solution)/shard_map/psum | solution.py:349
  2248.5 4.0 convert_element_type.276
  2252.5 1.7 convert_element_type.278
  2254.2 21.0 convert_element_type.285
  (445 shorter events, 151.9 us)
Async XLA Ops:
  7.2 7.6 copy-start.2
  7.2 60.4 %all-gather.7.cloned.1.call-start = ((), (), s32[]{:S(2)}) async-start(), calls=%async_computation.4 | async-start | bytes 9830400 | tf_op jit(solution)/shard_map/all_gather | solution.py:145
  7.9 114.4 %all-gather.9.cloned.1.call-start = ((), (), s32[]{:S(2)}) async-start(), calls=%async_computation.5 | async-start | bytes 2359296 | tf_op jit(solution)/shard_map/all_gather | solution.py:167
  14.8 57.3 %copy-start.30 = (f32[1536]{0:T(1024)}, f32[1536]{0:T(1024)S(1)}, u32[]{:S(2)}) copy-start(f32[1536]{0:T(1024)S(1)} %reshape.451) | copy-start | bytes 18436
  15.5 56.6 %copy-start.39 = (f32[128]{0:T(128)}, f32[128]{0:T(128)S(1)}, u32[]{:S(2)}) copy-start(f32[128]{0:T(128)S(1)} %get-tuple-element.585) | copy-start | bytes 1540
  72.9 87.0 %all-gather.11.cloned.1.call-start = ((), (), s32[]{:S(2)}) async-start(), calls=%async_computation.6 | async-start | bytes 5898240 | tf_op jit(solution)/shard_map/all_gather | solution.py:146
  73.7 11.9 copy-start.23
  73.7 529.3 %all-gather.13.cloned.1.call-start = ((), (), s32[]{:S(2)}) async-start(), calls=%async_computation.7 | async-start | bytes 94371840 | tf_op jit(solution)/shard_map/all_gather | solution.py:215
  74.3 985.2 %reduce-scatter.9.cloned.1.call-start = ((), (), s32[]{:S(2)}) async-start(), calls=%async_computation.9 | async-start | bytes 5898240 | tf_op jit(solution)/shard_map/reduce_scatter | solution.py:335
  74.5 91.9 %copy-start.18 = (s32[1,128,2]{2,1,0:T(8,128)}, s32[1,128,2]{2,1,0:T(8,128)S(1)}, u32[]{:S(2)}) copy-start(s32[1,128,2]{2,1,0:T(8,128)S(1)} %copy.69) | copy-start | bytes 3076
  74.6 14.7 copy-start.43
  80.0 83.8 %copy-start.35 = (f32[1536]{0:T(1024)}, f32[1536]{0:T(1024)S(1)}, u32[]{:S(2)}) copy-start(f32[1536]{0:T(1024)S(1)} %reshape.452) | copy-start | bytes 18436
  95.0 69.3 %copy-start.32 = (bf16[1536,8]{0,1:T(8,128)(2,1)}, bf16[1536,8]{0,1:T(8,128)(2,1)S(1)}, u32[]{:S(2)}) copy-start(bf16[1536,8]{0,1:T(8,128)(2,1)S(1)} %all_gather.27) | copy-start | bytes 73732
  140.3 22.9 %copy-start.26 = (f32[8,3,128]{2,1,0:T(4,128)}, f32[8,3,128]{2,1,0:T(4,128)S(1)}, u32[]{:S(2)}) copy-start(f32[8,3,128]{2,1,0:T(4,128)S(1)} %get-tuple-element.373) | copy-start | bytes 36868
  141.5 21.7 copy-start.14
  172.6 455.2 %copy-start.9 = (bf16[512,1536]{1,0:T(8,128)(2,1)}, bf16[512,1536]{1,0:T(8,128)(2,1)S(1)}, u32[]{:S(2)}) copy-start(bf16[512,1536]{1,0:T(8,128)(2,1)S(1)} %gather_fusion.2) | copy-start | bytes 4718596
  603.0 24.8 %copy-start.33 = (pred[8,64]{1,0:T(8,128)(4,1)S(1)}, pred[8,64]{1,0:T(8,128)(4,1)}, u32[]{:S(2)}) copy-start(pred[8,64]{1,0:T(8,128)(4,1)} %broadcast_in_dim.148) | copy-start | bytes 1540
  641.6 12.8 copy-start.46
  708.5 351.0 %reduce-scatter.7.cloned.1.call-start = ((), (), s32[]{:S(2)}) async-start(), calls=%async_computation.8 | async-start | bytes 9830400 | tf_op jit(solution)/shard_map/reduce_scatter | solution.py:332
  711.1 16.7 collective-permute-start.2
  715.9 13.2 collective-permute-start.3
  716.5 30.6 %collective-permute-start = (bf16[128,8,3,64]{0,3,2,1:T(8,128)(2,1)S(1)}, bf16[128,8,3,64]{0,3,2,1:T(8,128)(2,1)S(1)}, u32[]{:S(2)}, u32[]{:S(2)}) collective-permute-start(bf16[128,8,3,64]{0,3,2,1:T(8,128)(2,1)S(1)} %copy.116), channel_id=1, source_target_pairs={{4,0},{8,4},{12,8},{16,12},{20,16},{24,20},{28,24},{5,1},{9,5},{13... | collective-permute-start | bytes 1179656 | tf_op jit(solution)/shard_map/while/body/eval_jaxpr/ppermute | solution.py:25
  717.9 29.3 %collective-permute-start.1 = (bf16[128,8,3,64]{0,3,2,1:T(8,128)(2,1)S(1)}, bf16[128,8,3,64]{0,3,2,1:T(8,128)(2,1)S(1)}, u32[]{:S(2)}, u32[]{:S(2)}) collective-permute-start(bf16[128,8,3,64]{0,3,2,1:T(8,128)(2,1)S(1)} %copy.117), channel_id=1, source_target_pairs={{4,0},{8,4},{12,8},{16,12},{20,16},{24,20},{28,24},{5,1},{9,5},{13... | collective-permute-start | bytes 1179656 | tf_op jit(solution)/shard_map/while/body/eval_jaxpr/ppermute | solution.py:25
  722.0 24.1 %collective-permute-start.4 = (bf16[128,8,3,64]{0,3,2,1:T(8,128)(2,1)S(1)}, bf16[128,8,3,64]{0,3,2,1:T(8,128)(2,1)}, u32[]{:S(2)}, u32[]{:S(2)}) collective-permute-start(bf16[128,8,3,64]{0,3,2,1:T(8,128)(2,1)S(1)} %fusion.165), channel_id=1, source_target_pairs={{0,28},{4,0},{8,4},{12,8},{16,12},{20,16},{24,20},{28,24},{1,29},{... | collective-permute-start | bytes 1179656 | tf_op jit(solution)/shard_map/while/body/eval_jaxpr/ppermute | solution.py:31
  748.5 14.8 collective-permute-start.2
  749.1 15.5 collective-permute-start.3
  751.2 29.2 %collective-permute-start = (bf16[128,8,3,64]{0,3,2,1:T(8,128)(2,1)S(1)}, bf16[128,8,3,64]{0,3,2,1:T(8,128)(2,1)S(1)}, u32[]{:S(2)}, u32[]{:S(2)}) collective-permute-start(bf16[128,8,3,64]{0,3,2,1:T(8,128)(2,1)S(1)} %copy.116), channel_id=1, source_target_pairs={{4,0},{8,4},{12,8},{16,12},{20,16},{24,20},{28,24},{5,1},{9,5},{13... | collective-permute-start | bytes 1179656 | tf_op jit(solution)/shard_map/while/body/eval_jaxpr/ppermute | solution.py:25
  752.5 27.8 %collective-permute-start.1 = (bf16[128,8,3,64]{0,3,2,1:T(8,128)(2,1)S(1)}, bf16[128,8,3,64]{0,3,2,1:T(8,128)(2,1)S(1)}, u32[]{:S(2)}, u32[]{:S(2)}) collective-permute-start(bf16[128,8,3,64]{0,3,2,1:T(8,128)(2,1)S(1)} %copy.117), channel_id=1, source_target_pairs={{4,0},{8,4},{12,8},{16,12},{20,16},{24,20},{28,24},{5,1},{9,5},{13... | collective-permute-start | bytes 1179656 | tf_op jit(solution)/shard_map/while/body/eval_jaxpr/ppermute | solution.py:25
  756.6 22.6 collective-permute-start.4
  781.7 18.5 collective-permute-start.2
  782.5 19.1 collective-permute-start.3
  785.1 28.1 %collective-permute-start = (bf16[128,8,3,64]{0,3,2,1:T(8,128)(2,1)S(1)}, bf16[128,8,3,64]{0,3,2,1:T(8,128)(2,1)S(1)}, u32[]{:S(2)}, u32[]{:S(2)}) collective-permute-start(bf16[128,8,3,64]{0,3,2,1:T(8,128)(2,1)S(1)} %copy.116), channel_id=1, source_target_pairs={{4,0},{8,4},{12,8},{16,12},{20,16},{24,20},{28,24},{5,1},{9,5},{13... | collective-permute-start | bytes 1179656 | tf_op jit(solution)/shard_map/while/body/eval_jaxpr/ppermute | solution.py:25
  786.4 26.8 %collective-permute-start.1 = (bf16[128,8,3,64]{0,3,2,1:T(8,128)(2,1)S(1)}, bf16[128,8,3,64]{0,3,2,1:T(8,128)(2,1)S(1)}, u32[]{:S(2)}, u32[]{:S(2)}) collective-permute-start(bf16[128,8,3,64]{0,3,2,1:T(8,128)(2,1)S(1)} %copy.117), channel_id=1, source_target_pairs={{4,0},{8,4},{12,8},{16,12},{20,16},{24,20},{28,24},{5,1},{9,5},{13... | collective-permute-start | bytes 1179656 | tf_op jit(solution)/shard_map/while/body/eval_jaxpr/ppermute | solution.py:25
  790.5 21.6 collective-permute-start.4
  814.5 17.8 collective-permute-start.2
  816.1 17.6 collective-permute-start.3
  819.5 26.5 %collective-permute-start = (bf16[128,8,3,64]{0,3,2,1:T(8,128)(2,1)S(1)}, bf16[128,8,3,64]{0,3,2,1:T(8,128)(2,1)S(1)}, u32[]{:S(2)}, u32[]{:S(2)}) collective-permute-start(bf16[128,8,3,64]{0,3,2,1:T(8,128)(2,1)S(1)} %copy.116), channel_id=1, source_target_pairs={{4,0},{8,4},{12,8},{16,12},{20,16},{24,20},{28,24},{5,1},{9,5},{13... | collective-permute-start | bytes 1179656 | tf_op jit(solution)/shard_map/while/body/eval_jaxpr/ppermute | solution.py:25
  820.8 25.2 %collective-permute-start.1 = (bf16[128,8,3,64]{0,3,2,1:T(8,128)(2,1)S(1)}, bf16[128,8,3,64]{0,3,2,1:T(8,128)(2,1)S(1)}, u32[]{:S(2)}, u32[]{:S(2)}) collective-permute-start(bf16[128,8,3,64]{0,3,2,1:T(8,128)(2,1)S(1)} %copy.117), channel_id=1, source_target_pairs={{4,0},{8,4},{12,8},{16,12},{20,16},{24,20},{28,24},{5,1},{9,5},{13... | collective-permute-start | bytes 1179656 | tf_op jit(solution)/shard_map/while/body/eval_jaxpr/ppermute | solution.py:25
  824.9 20.0 collective-permute-start.4
  847.4 16.0 collective-permute-start.2
  848.9 15.8 collective-permute-start.3
  851.5 25.6 %collective-permute-start = (bf16[128,8,3,64]{0,3,2,1:T(8,128)(2,1)S(1)}, bf16[128,8,3,64]{0,3,2,1:T(8,128)(2,1)S(1)}, u32[]{:S(2)}, u32[]{:S(2)}) collective-permute-start(bf16[128,8,3,64]{0,3,2,1:T(8,128)(2,1)S(1)} %copy.116), channel_id=1, source_target_pairs={{4,0},{8,4},{12,8},{16,12},{20,16},{24,20},{28,24},{5,1},{9,5},{13... | collective-permute-start | bytes 1179656 | tf_op jit(solution)/shard_map/while/body/eval_jaxpr/ppermute | solution.py:25
  852.8 24.3 %collective-permute-start.1 = (bf16[128,8,3,64]{0,3,2,1:T(8,128)(2,1)S(1)}, bf16[128,8,3,64]{0,3,2,1:T(8,128)(2,1)S(1)}, u32[]{:S(2)}, u32[]{:S(2)}) collective-permute-start(bf16[128,8,3,64]{0,3,2,1:T(8,128)(2,1)S(1)} %copy.117), channel_id=1, source_target_pairs={{4,0},{8,4},{12,8},{16,12},{20,16},{24,20},{28,24},{5,1},{9,5},{13... | collective-permute-start | bytes 1179656 | tf_op jit(solution)/shard_map/while/body/eval_jaxpr/ppermute | solution.py:25
  856.9 19.1 collective-permute-start.4
  878.5 15.2 collective-permute-start.2
  880.1 14.9 collective-permute-start.3
  882.8 24.8 %collective-permute-start = (bf16[128,8,3,64]{0,3,2,1:T(8,128)(2,1)S(1)}, bf16[128,8,3,64]{0,3,2,1:T(8,128)(2,1)S(1)}, u32[]{:S(2)}, u32[]{:S(2)}) collective-permute-start(bf16[128,8,3,64]{0,3,2,1:T(8,128)(2,1)S(1)} %copy.116), channel_id=1, source_target_pairs={{4,0},{8,4},{12,8},{16,12},{20,16},{24,20},{28,24},{5,1},{9,5},{13... | collective-permute-start | bytes 1179656 | tf_op jit(solution)/shard_map/while/body/eval_jaxpr/ppermute | solution.py:25
  884.1 23.4 %collective-permute-start.1 = (bf16[128,8,3,64]{0,3,2,1:T(8,128)(2,1)S(1)}, bf16[128,8,3,64]{0,3,2,1:T(8,128)(2,1)S(1)}, u32[]{:S(2)}, u32[]{:S(2)}) collective-permute-start(bf16[128,8,3,64]{0,3,2,1:T(8,128)(2,1)S(1)} %copy.117), channel_id=1, source_target_pairs={{4,0},{8,4},{12,8},{16,12},{20,16},{24,20},{28,24},{5,1},{9,5},{13... | collective-permute-start | bytes 1179656 | tf_op jit(solution)/shard_map/while/body/eval_jaxpr/ppermute | solution.py:25
  888.2 18.3 collective-permute-start.4
  908.9 14.0 collective-permute-start.2
  909.5 14.7 collective-permute-start.3
  911.7 24.0 %collective-permute-start = (bf16[128,8,3,64]{0,3,2,1:T(8,128)(2,1)S(1)}, bf16[128,8,3,64]{0,3,2,1:T(8,128)(2,1)S(1)}, u32[]{:S(2)}, u32[]{:S(2)}) collective-permute-start(bf16[128,8,3,64]{0,3,2,1:T(8,128)(2,1)S(1)} %copy.116), channel_id=1, source_target_pairs={{4,0},{8,4},{12,8},{16,12},{20,16},{24,20},{28,24},{5,1},{9,5},{13... | collective-permute-start | bytes 1179656 | tf_op jit(solution)/shard_map/while/body/eval_jaxpr/ppermute | solution.py:25
  913.0 22.7 collective-permute-start.1
  917.2 17.5 collective-permute-start.4
  937.0 15.7 collective-permute-start.2
  937.7 16.4 collective-permute-start.3
  938.8 22.0 collective-permute-start
  940.1 20.7 collective-permute-start.1
  944.2 15.5 collective-permute-start.4
  968.0 595.0 %reduce-scatter.11.cloned.1.call-start = ((), (), s32[]{:S(2)}) async-start(), calls=%async_computation.10 | async-start | bytes 94371840 | tf_op jit(solution)/shard_map/reduce_scatter | solution.py:245
  1057.0 530.0 %reduce-scatter.13.cloned.1.call-start = ((), (), s32[]{:S(2)}) async-start(), calls=%async_computation.11 | async-start | bytes 491520
  1059.1 1189.4 %all-reduce.7.cloned.1.call-start = ((), (), s32[]{:S(2)}) async-start(), calls=%async_computation.12 | async-start | bytes 44040192 | tf_op jit(solution)/shard_map/psum | solution.py:349
  1564.9 12.2 copy-start.8
  1564.9 12.2 copy-start.54
  (44 other events, 108.0 us)
Sparse Core Ops, SparseCore 0:
  9.6 58.0 all-gather.6
  73.0 49.2 all-gather.8
  123.9 35.9 all-gather.10
  161.3 441.6 all-gather.12
  708.6 47.8 reduce-scatter.8
  968.1 68.5 reduce-scatter.6
  1057.1 505.7 reduce-scatter.10
  1566.2 20.8 reduce-scatter.12
  1592.3 656.1 all-reduce.6
where the time goes:
time: 2290 us; the launch traced here: 2280 us
  waiting for transfers between devices  1760 us (77%)
  matrix products  169 us (7%)
  other arithmetic  153 us (7%)
  starting transfers between devices  92.8 us (4%)
  local copies, waits for them, and re-layouts  45.7 us (2%)
  blocking collectives  44.8 us (2%)
    psum x1, waiting for transfers between devices, per_device(): lax.psum(qkv_part.astype(jnp.bfloat16), 'ctx').astype(jnp.float32)  637 us
    reduce_scatter x1, waiting for transfers between devices, per_device(): lax.psum_scatter(expert_kernel_grad('', expert_in, d_both_all, grad_buffe...  503 us
    all_gather x1, waiting for transfers between devices, per_device(): lax.all_gather(w_experts, 'fsdp', axis=0, tiled=True)  427 us
    ppermute x24, waiting for transfers between devices, passed_along(): return lax.ppermute(value, axis, pairs)  86.7 us
    ppermute x24, starting transfers between devices, passed_along(): return lax.ppermute(value, axis, pairs)  71.5 us
    all_gather x1, waiting for transfers between devices, per_device(): lax.all_gather(query_key_value_weight, 'fsdp', axis=0, tiled=True)  52.1 us
    concatenate x1, other arithmetic, expert_kernel_grad(): return jnp.concatenate([d_inward, d_down], axis=-1)  49.6 us
  transfers between devices with their start and end apart: 49, of which 15 were waited for; matrix products, arithmetic and copies ran while one was open for 10% of the time, Pallas kernels for 0%

commit v1 on v0

v1 whole, which is shorter than its diff:
```python
import jax
import jax.numpy as jnp
from jax import lax
from jax.sharding import PartitionSpec as P

HQ = 24
HK = 8
HD = 64
GROUP = HQ // HK
FF = 1024
EXPERTS = 8
CAP = 64
Q_COLS = HQ * HD
K_COLS = HK * HD
HEAD_COLS = GROUP * HD + 2 * HD
SMALL = 16

NORM_EPS = 1e-05
MASK_NEG = -1e30
BF = jnp.bfloat16
F32 = jnp.float32


def dot(a, b):
    return jnp.dot(a, b, preferred_element_type=F32)


def dot_t(a, b):
    return lax.dot_general(a, b, (((1,), (1,)), ((), ())), preferred_element_type=F32)


def t_dot(a, b):
    return lax.dot_general(a, b, (((0,), (0,)), ((), ())), preferred_element_type=F32)


def rms_factor(values):
    return lax.rsqrt(jnp.mean(values * values, axis=-1, keepdims=True) + NORM_EPS)


def rms_input_grad(values, factor, gain_vec, incoming):
    inner = incoming * gain_vec
    cubed = factor * factor * factor
    return factor * inner - values * cubed * jnp.mean(inner * values, axis=-1, keepdims=True)


def doc_index(doc_bounds, positions):
    hits = (positions[:, None] >= doc_bounds[None, :]).astype(jnp.int32)
    return jnp.sum(hits, axis=1)


def to_all(value, axis):
    return lax.all_to_all(value, axis, 0, 0, tiled=True)


def gathered(value, axis):
    return lax.all_gather(value, axis, axis=0, tiled=True)


def reduced(value, axis):
    return lax.psum_scatter(value, axis, scatter_dimension=0, tiled=True)


def route_tables(routes, first, count):
    ids = jnp.arange(EXPERTS, dtype=jnp.int32)
    picked = jnp.any(routes[..., None] == ids, axis=-2)
    mine = jnp.any(routes[..., None] == (first + jnp.arange(count, dtype=jnp.int32)), axis=-2)
    taken = mine.astype(jnp.int32)
    rank = jnp.cumsum(taken, axis=-2) - taken
    return picked, mine, rank


def slot_matrix(mine, rank):
    slots = jnp.arange(CAP, dtype=jnp.int32)[:, None]
    mine_t = jnp.swapaxes(mine, -1, -2)[:, :, None, :]
    rank_t = jnp.swapaxes(rank, -1, -2)[:, :, None, :]
    return (mine_t & (rank_t == slots)).astype(BF)


def gate_table(second, router, picked):
    logits = jnp.einsum("btd,de->bte", second, router, preferred_element_type=F32)
    logits = jnp.where(picked, logits, MASK_NEG)
    return jax.nn.softmax(logits, axis=-1)


def attention_forward(q, k, v, allowed):
    length = q.shape[0]
    scores = jnp.einsum(
        "tgd,sd->gts", q.reshape(length, GROUP, HD), k, preferred_element_type=F32
    ) * HD ** (-0.5)
    highest = jnp.max(jnp.where(allowed, scores, MASK_NEG), axis=-1, keepdims=True)
    weights = jnp.where(allowed, jnp.exp(scores - highest), 0.0)
    total = jnp.sum(weights, axis=-1, keepdims=True)
    total = jnp.where(total == 0.0, 1.0, total)
    log_norm = highest + jnp.log(total)
    probs = (weights / total).astype(BF)
    attended = jnp.einsum("gts,sd->tgd", probs, v, preferred_element_type=F32)
    return attended.reshape(length, GROUP * HD), log_norm


def attention_backward(q, k, v, allowed, log_norm, attended, grads):
    length = q.shape[0]
    scale = HD ** (-0.5)
    q3 = q.reshape(length, GROUP, HD)
    g3 = grads.reshape(length, GROUP, HD)
    delta = jnp.sum(g3.astype(F32) * attended.reshape(length, GROUP, HD), axis=-1).T
    scores = jnp.einsum("tgd,sd->gts", q3, k, preferred_element_type=F32) * scale
    probs = jnp.where(allowed, jnp.exp(scores - log_norm), 0.0)
    d_probs = jnp.einsum("tgd,sd->gts", g3, v, preferred_element_type=F32)
    d_scores = (probs * (d_probs - delta[..., None])).astype(BF)
    d_q = jnp.einsum("gts,sd->tgd", d_scores, k, preferred_element_type=F32) * scale
    d_k = jnp.einsum("gts,tgd->sd", d_scores, q3, preferred_element_type=F32) * scale
    d_v = jnp.einsum("gts,tgd->sd", probs.astype(BF), g3, preferred_element_type=F32)
    return jnp.concatenate([d_q.reshape(length, GROUP * HD), d_k, d_v], axis=1).astype(BF)


def expert_pass(rows, d_out, w_experts):
    both = jnp.einsum("erd,edf->erf", rows, w_experts[:, :, : 2 * FF], preferred_element_type=F32)
    gate, up = both[..., :FF], both[..., FF:]
    sigma = jax.nn.sigmoid(gate)
    hidden = (gate * sigma * up).astype(BF)
    out = jnp.einsum(
        "erf,edf->erd", hidden, w_experts[:, :, 2 * FF :], preferred_element_type=F32
    ).astype(BF)
    d_hidden = jnp.einsum(
        "erd,edf->erf", d_out, w_experts[:, :, 2 * FF :], preferred_element_type=F32
    )
    d_both = jnp.concatenate(
        [d_hidden * up * sigma * (1.0 + gate * (1.0 - sigma)), d_hidden * gate * sigma], axis=-1
    ).astype(BF)
    d_rows = jnp.einsum(
        "erf,edf->erd", d_both, w_experts[:, :, : 2 * FF], preferred_element_type=F32
    ).astype(BF)
    return out, d_rows


def expert_weight_grad(rows, d_out, w_experts):
    both = jnp.einsum("erd,edf->erf", rows, w_experts[:, :, : 2 * FF], preferred_element_type=F32)
    gate, up = both[..., :FF], both[..., FF:]
    sigma = jax.nn.sigmoid(gate)
    hidden = (gate * sigma * up).astype(BF)
    d_hidden = jnp.einsum(
        "erd,edf->erf", d_out, w_experts[:, :, 2 * FF :], preferred_element_type=F32
    )
    d_both = jnp.concatenate(
        [d_hidden * up * sigma * (1.0 + gate * (1.0 - sigma)), d_hidden * gate * sigma], axis=-1
    ).astype(BF)
    inward = jnp.einsum("erd,erf->edf", rows, d_both, preferred_element_type=F32)
    down = jnp.einsum("erd,erf->edf", d_out, hidden, preferred_element_type=F32)
    return jnp.concatenate([inward, down], axis=-1)


def per_device(
    tokens,
    query_key_value_weight,
    output_weight,
    routing_weight,
    gain_attn,
    gain_moe,
    w_experts,
    doc_starts,
    routes,
    cotangent,
):
    spans = lax.axis_size("ctx")
    shards = lax.axis_size("fsdp")
    here = lax.axis_index("ctx")
    shard = lax.axis_index("fsdp")
    tok_count, width = tokens.shape[1:]
    local_experts = w_experts.shape[0]
    copies = spans // HK
    head = here // copies
    length = spans * tok_count
    blocks = spans * shards
    everyone = ("ctx", "fsdp")

    shard_rows = query_key_value_weight.shape[0]
    head_w = jnp.concatenate(
        [
            lax.dynamic_slice_in_dim(query_key_value_weight, head * GROUP * HD, GROUP * HD, 1),
            lax.dynamic_slice_in_dim(query_key_value_weight, Q_COLS + head * HD, HD, 1),
            lax.dynamic_slice_in_dim(query_key_value_weight, Q_COLS + K_COLS + head * HD, HD, 1),
            routing_weight,
            gain_attn[:, None],
            gain_moe[:, None],
        ],
        axis=1,
    )
    head_w = gathered(head_w, "fsdp")
    router_w = head_w[:, HEAD_COLS : HEAD_COLS + EXPERTS]
    attn_g = head_w[:, HEAD_COLS + EXPERTS].astype(F32)
    moe_g = head_w[:, HEAD_COLS + EXPERTS + 1].astype(F32)
    head_w = head_w[:, :HEAD_COLS]
    out_w = gathered(output_weight, "fsdp")
    qkv_w = gathered(query_key_value_weight, "fsdp")

    route_cols = jnp.pad(routes[0].astype(BF), ((0, 0), (0, 126)))
    grads_all = gathered(jnp.concatenate([cotangent[0], route_cols], axis=1), everyone)
    routes_all = grads_all[:, width : width + 2].astype(jnp.int32).reshape(blocks, tok_count, 2)
    grads_all = grads_all[:, :width].reshape(blocks, tok_count, width)

    stream = gathered(tokens[0], "ctx")
    stream_f = stream.astype(F32)
    normed = (stream_f * rms_factor(stream_f) * attn_g).astype(BF)
    mixed = dot(normed, head_w).astype(BF)
    q = mixed[:, : GROUP * HD]
    k = mixed[:, GROUP * HD : GROUP * HD + HD]
    v = mixed[:, GROUP * HD + HD :]
    pos = jnp.arange(length, dtype=jnp.int32)
    docs = doc_index(doc_starts[0], pos)
    active = (pos // tok_count) % copies == here % copies
    allowed = (pos[None, :] <= pos[:, None]) & (docs[None, :] == docs[:, None]) & active[:, None]
    attended, log_norm = attention_forward(q, k, v, allowed)
    attended_low = attended.astype(BF)
    attended_all = gathered(attended_low, "ctx").reshape(HK, copies, length, GROUP * HD)
    if copies > 1:
        attended_all = jnp.sum(attended_all, axis=1)
    attended_all = attended_all.reshape(HK, length, GROUP * HD)

    own = to_all(attended_low, "ctx").reshape(HK, copies, tok_count, GROUP * HD)
    own = jnp.sum(own, axis=1) if copies > 1 else own[:, 0]
    own = own.transpose(1, 0, 2).reshape(tok_count, Q_COLS)
    x = tokens[0].astype(F32)
    middle = x + dot(own, out_w)
    second_factor = rms_factor(middle)
    second = (middle * second_factor * moe_g).astype(BF)

    second_near = gathered(second, "fsdp").reshape(shards, tok_count, width)
    first_expert = shard * local_experts
    picked, mine, rank = route_tables(routes_all, first_expert, local_experts)

    def near(table):
        return lax.dynamic_slice_in_dim(table, here * shards, shards, 0)

    hot = slot_matrix(mine, rank)
    hot_near = near(hot)
    grads_near = near(grads_all)
    gates_near = lax.dynamic_slice_in_dim(
        gate_table(second_near, router_w, near(picked)), first_expert, local_experts, 2
    )

    def gather_rows(table, onehot):
        rows = jnp.einsum("best,btd->ebsd", onehot, table, preferred_element_type=F32)
        return rows.reshape(local_experts, -1, width)

    def slot_gates(gates, onehot):
        found = jnp.sum(onehot.astype(F32) * jnp.swapaxes(gates, 1, 2)[:, :, None, :], axis=-1)
        return found.swapaxes(0, 1).reshape(local_experts, -1, 1)

    near_rows = gather_rows(second_near, hot_near).astype(BF)
    near_gates = slot_gates(gates_near, hot_near)
    near_grads = gather_rows(grads_near, hot_near)
    near_d_out = (near_gates * near_grads).astype(BF)
    expert_out, d_rows = expert_pass(near_rows, near_d_out, w_experts)
    d_gates = jnp.sum(near_grads * expert_out.astype(F32), axis=-1)
    gated = (near_gates * expert_out.astype(F32)).astype(BF)

    def scatter_rows(rows):
        rows = rows.reshape(local_experts, shards, CAP, width)
        return jnp.einsum("best,ebsd->btd", hot_near, rows, preferred_element_type=F32).astype(BF)

    d_gates = d_gates.reshape(local_experts, shards, CAP).swapaxes(0, 1)
    d_gates = jnp.sum(hot_near.astype(F32) * d_gates[..., None], axis=2).swapaxes(1, 2)
    d_gates = jnp.pad(d_gates, ((0, 0), (0, 0), (0, EXPERTS - local_experts)))
    d_gates = jnp.roll(d_gates, first_expert, axis=2)
    coarse = d_gates.astype(BF)
    fine = (d_gates - coarse.astype(F32)).astype(BF)
    fill = jnp.zeros((shards, tok_count, 128 - 2 * EXPERTS), BF)
    back = jnp.concatenate([scatter_rows(d_rows), coarse, fine, fill], axis=2)
    back = to_all(back.reshape(shards * tok_count, -1), "fsdp").reshape(shards, tok_count, -1)
    back = jnp.sum(back.astype(F32), axis=0)
    branch = reduced(scatter_rows(gated).reshape(shards * tok_count, width), "fsdp")
    output = (middle + branch.astype(F32)).astype(BF)

    grad = cotangent[0].astype(F32)
    d_gates = back[:, width : width + EXPERTS] + back[:, width + EXPERTS : width + 2 * EXPERTS]
    own_picked = jnp.any(routes[0][:, :, None] == jnp.arange(EXPERTS, dtype=jnp.int32), axis=1)
    gates = gate_table(second[None], router_w, own_picked[None])[0]
    d_picked = gates * (d_gates - jnp.sum(gates * d_gates, axis=-1, keepdims=True))
    d_logits = jnp.where(own_picked, d_picked, 0.0).astype(BF)
    d_router = t_dot(second, d_logits)
    d_second = dot_t(d_logits, router_w) + back[:, :width]
    d_gain_moe = jnp.sum(d_second * middle * second_factor, axis=0)
    d_middle = grad + rms_input_grad(middle, second_factor, moe_g, d_second)
    d_proj = d_middle.astype(BF)
    d_attended = dot_t(d_proj, out_w).astype(BF)

    chunk = width // spans
    d_attended = d_attended.reshape(tok_count, HK, 1, GROUP * HD)
    d_attended = jnp.broadcast_to(d_attended, (tok_count, HK, copies, GROUP * HD))
    d_attended = d_attended.reshape(tok_count, spans, GROUP * HD)
    sent = jnp.concatenate([d_attended, d_proj.reshape(tok_count, spans, chunk)], axis=2)
    sent = to_all(sent.swapaxes(0, 1).reshape(length, -1), "ctx")
    d_mixed = attention_backward(
        q, k, v, allowed, log_norm, attended, sent[:, : GROUP * HD]
    )
    d_head_w = t_dot(normed, d_mixed)
    d_out_w = jnp.einsum(
        "hte,td->hed", attended_all, sent[:, GROUP * HD :], preferred_element_type=F32
    ).reshape(Q_COLS, chunk)
    small = jnp.concatenate(
        [d_router, d_gain_moe[:, None], jnp.zeros((width, SMALL - EXPERTS - 1), F32)], axis=1
    )
    weight_grads = jnp.concatenate([d_head_w, d_out_w, small], axis=1).astype(BF)
    weight_grads = reduced(weight_grads, "fsdp")
    weight_grads = gathered(weight_grads, "ctx").reshape(spans, shard_rows, -1).astype(F32)
    by_head = weight_grads[:, :, :HEAD_COLS].reshape(HK, copies, shard_rows, HEAD_COLS)
    by_head = jnp.sum(by_head, axis=1).swapaxes(0, 1)

    def columns(part):
        return part.reshape(shard_rows, -1)

    d_qkv_w = jnp.concatenate(
        [
            columns(by_head[:, :, : GROUP * HD]),
            columns(by_head[:, :, GROUP * HD : GROUP * HD + HD]),
            columns(by_head[:, :, GROUP * HD + HD :]),
        ],
        axis=1,
    )
    d_out_w = columns(weight_grads[:, :, HEAD_COLS : HEAD_COLS + chunk].swapaxes(0, 1))
    small = jnp.sum(weight_grads[:, :, HEAD_COLS + chunk :], axis=0)
    d_router_w = small[:, :EXPERTS]
    d_gain_moe = small[:, EXPERTS]
    d_gain_attn = jnp.sum(
        d_qkv_w * query_key_value_weight.astype(F32), axis=1
    ) / gain_attn.astype(F32)

    d_home = to_all(d_mixed, "ctx").reshape(HK, copies, tok_count, HEAD_COLS)
    d_home = jnp.sum(d_home.astype(F32), axis=1).astype(BF) if copies > 1 else d_home[:, 0]
    d_home = d_home.swapaxes(0, 1)
    d_home = jnp.concatenate(
        [
            d_home[:, :, : GROUP * HD].reshape(tok_count, -1),
            d_home[:, :, GROUP * HD : GROUP * HD + HD].reshape(tok_count, -1),
            d_home[:, :, GROUP * HD + HD :].reshape(tok_count, -1),
        ],
        axis=1,
    )
    d_normed = dot_t(d_home, qkv_w)
    d_tokens = (d_middle + rms_input_grad(x, rms_factor(x), attn_g, d_normed)).astype(BF)

    second_all = gathered(second, everyone).reshape(blocks, tok_count, width)
    gates_all = lax.dynamic_slice_in_dim(
        gate_table(second_all, router_w, picked), first_expert, local_experts, 2
    )
    all_rows = gather_rows(second_all, hot).astype(BF)
    all_d_out = (slot_gates(gates_all, hot) * gather_rows(grads_all, hot)).astype(BF)
    d_w_experts = expert_weight_grad(all_rows, all_d_out, w_experts)
    return (
        output[None],
        d_tokens[None],
        d_qkv_w,
        d_out_w,
        d_router_w,
        d_gain_attn,
        d_gain_moe,
        d_w_experts,
    )


def solution(mesh):
    placed = (
        P("fsdp", "ctx", None),
        P("fsdp", None),
        P("fsdp", None),
        P("fsdp", None),
        P("fsdp"),
        P("fsdp"),
        P("fsdp", None, None),
        P("fsdp", None),
        P("fsdp", "ctx", None),
        P("fsdp", "ctx", None),
    )
    return jax.shard_map(
        per_device,
        mesh=mesh,
        in_specs=placed,
        out_specs=(
            P("fsdp", "ctx", None),
            P("fsdp", "ctx", None),
            P("fsdp", None),
            P("fsdp", None),
            P("fsdp", None),
            P("fsdp"),
            P("fsdp"),
            P("fsdp", None, None),
        ),
        check_vma=False,
    )
```

time: 2290 us -> 733 us (0.32)
  waiting for transfers between devices: 1760 us -> 232 us
  matrix products: 169 us -> 254 us
  other arithmetic: 153 us -> 76 us
  starting transfers between devices: 92.8 us -> 23.6 us
  local copies, waits for them, and re-layouts: 45.7 us -> 93.8 us
    psum x1 -> x0, waiting for transfers between devices: 637 us -> none  [per_device(): lax.psum(qkv_part.astype(jnp.bfloat16), 'ctx').astype(jnp.float32)]
    reduce_scatter x3 -> x1, waiting for transfers between devices: 504 us -> 0.01 us  [reduced(): return lax.psum_scatter(value, axis, scatter_dimension=0, tiled=True)]
    all_gather x4 -> x8, waiting for transfers between devices: 521 us -> 209 us  [gathered(): return lax.all_gather(value, axis, axis=0, tiled=True)]
    ppermute x40 -> x0, starting transfers between devices: 92.1 us -> none  [the longest x24 71.5 us: passed_along(): return lax.ppermute(value, axis, pairs)]
    ppermute x40 -> x0, waiting for transfers between devices: 86.7 us -> none  [the longest x24 86.7 us: passed_along(): return lax.ppermute(value, axis, pairs)]
    dot_general x59 -> x31, matrix products: 169 us -> 254 us  [the longest x1 42.4 us: expert_weight_grad(): jnp.einsum('erd,erf->edf', rows, d_both, preferred_element_type=F32)]
    convert_element_type x53 -> x11, other arithmetic: 70.2 us -> 25.1 us  [the longest x1 13.3 us: per_device(): (slot_gates(gates_all, hot) * gather_rows(grads_all, hot)).astype(BF)]
    concatenate x1 -> x3, other arithmetic: 49.6 us -> 30.4 us  [the longest x1 27.7 us: expert_weight_grad(): return jnp.concatenate([inward, down], axis=-1)]
  transfers between devices with their start and end apart: 49 -> 13, of which waited for: 15 -> 6; matrix products, arithmetic and copies ran while one was open for 10% -> 51% of each run, Pallas kernels for 0% -> 0%
where the time goes in v1:
time: 733 us; the launch traced here: 723 us
  matrix products  254 us (35%)
  waiting for transfers between devices  232 us (32%)
  local copies, waits for them, and re-layouts  93.8 us (13%)
  other arithmetic  76 us (10%)
  blocking collectives  27.3 us (4%)
  starting transfers between devices  23.6 us (3%)
  between operations  15.8 us (2%)
    all_gather x8, waiting for transfers between devices, gathered(): return lax.all_gather(value, axis, axis=0, tiled=True)  209 us
    dot_general x1, matrix products, expert_weight_grad(): jnp.einsum('erd,erf->edf', rows, d_both, preferred_element_type=F32)  42.4 us
    dot_general x1, matrix products, expert_weight_grad(): jnp.einsum('erd,edf->erf', rows, w_experts[:, :, :2 * FF], preferred_elem...  35.7 us
    dot_general x1, matrix products, expert_weight_grad(): down = jnp.einsum('erd,erf->edf', d_out, hidden, preferred_element_type=F32)  29.3 us
    dot_general x1, matrix products, expert_weight_grad(): jnp.einsum('erd,edf->erf', d_out, w_experts[:, :, 2 * FF:], preferred_ele...  29 us
    concatenate x1, other arithmetic, expert_weight_grad(): return jnp.concatenate([inward, down], axis=-1)  27.7 us
    unnamed x126, local copies, waits for them, and re-layouts  26.6 us
    dot_general x4, matrix products, gather_rows(): jnp.einsum('best,btd->ebsd', onehot, table, preferred_element_type=F32)  25.8 us
  transfers between devices with their start and end apart: 13, of which 6 were waited for; matrix products, arithmetic and copies ran while one was open for 51% of the time, Pallas kernels for 0%

profile of v1, /device:TPU:0, one launch (start us, length us, event | category | flops | bytes accessed | tf_op | source)
XLA Modules:
  0.0 723.2 jit_solution(7575554259806219213)
XLA Ops:
  9.5 1.8 fusion.88
  12.8 2.8 copy.303
  16.0 11.4 %all_gather.28 = bf16[1536,330]{0,1:T(8,128)(2,1)S(1)} all-gather(bf16[384,330]{0,1:T(8,128)(2,1)S(1)} %concatenate.51), channel_id=1, replica_groups=mesh['ctx'=8,'fsdp'=4] {'fsdp'}, dimensions={0}, use_global_device_ids=true | all-gather | bytes 1267200 | tf_op jit(solution)/shard_map/all_gather | solution.py:56
  29.0 44.4 %all-gather.24.cloned.1.call-done = bf16[1,1024,1536]{2,1,0:T(8,128)(2,1)} async-done(((bf16[1,128,1536]{2,1,0:T(8,128)(2,1)}), bf16[1,1024,1536]{2,1,0:T(8,128)(2,1)}) %all-gather.24.cloned.1.call-update) | async-done | bytes 3145744 | tf_op jit(solution)/shard_map/all_gather | solution.py:56
  73.4 2.6 fusion.22
  76.0 3.3 convolution_convert_fusion.6
  79.4 2.5 fusion.7
  81.9 4.4 fusion.14
  86.9 5.8 fusion.138
  93.6 15.9 %all_to_all.27 = bf16[8,128,192]{1,2,0:T(8,128)(2,1)S(1)} all-to-all(bf16[8,128,192]{1,2,0:T(8,128)(2,1)S(1)} %copy.307), channel_id=1, replica_groups=mesh['ctx'=8,'fsdp'=4] {'ctx'}, dimensions={0} | all-to-all | bytes 786432 | tf_op jit(solution)/shard_map/all_to_all | solution.py:52
  109.5 1.6 all-gather.10.cloned.1.call-done
  111.1 3.2 multiply_reduce_fusion.5
  116.6 98.7 %all-gather.12.cloned.1.call-done = bf16[4096,1664]{1,0:T(8,128)(2,1)} async-done(((bf16[128,1664]{1,0:T(8,128)(2,1)}), bf16[4096,1664]{1,0:T(8,128)(2,1)}) %all-gather.12.cloned.1.call-update) | async-done | bytes 13631504 | tf_op jit(solution)/shard_map/all_gather | solution.py:56
  218.3 1.9 copy.311
  221.7 2.7 copy.312
  224.5 6.2 slice.138
  230.7 2.1 fusion.130
  235.8 2.0 fusion.47
  237.9 6.6 fusion.19
  244.6 7.5 %fusion.37 = (f32[2,256]{1,0:T(2,128)S(1)}, bf16[2,256,1536]{2,1,0:T(8,128)(2,1)}) fusion(f32[2,4,64,1536]{3,2,1,0:T(8,128)S(1)} %copy.321, bf16[2,1536,3072]{2,1,0:T(8,128)(2,1)} %param.16, f32[2,256,2048]{2,1,0:T(8,128)S(1)} %fusion.19), kind=kOutput, calls=%fused_computation.61 | convolution fusion | flops 1616903680 | bytes 15206400 | tf_op jit(solution)/shard_map/erf,edf->erd/dot_general | solution.py:121
  252.1 1.9 fusion.140
  255.3 3.6 fusion.38
  259.0 2.6 fusion.42
  262.2 10.4 %all-gather.22.cloned.1.call-start = ((), (), s32[]{:S(2)}) async-start(), calls=%async_computation.12 | async-start | bytes 12976128 | tf_op jit(solution)/shard_map/all_gather | solution.py:56
  273.0 6.8 multiply_convert_fusion.5
  279.8 8.3 %fusion.39 = bf16[2,256,1536]{2,1,0:T(8,128)(2,1)S(1)} fusion(bf16[2,1536,3072]{2,1,0:T(8,128)(2,1)} %param.16, bf16[2,256,1024]{2,1,0:T(8,128)(2,1)S(1)} %get-tuple-element.85, bf16[2,256,1024]{2,1,0:T(8,128)(2,1)S(1)} %get-tuple-element.84), kind=kOutput, calls=%fused_computation.64 | convolution fusion | flops 3226206208 | bytes 16252928 | tf_op jit(solution)/shard_map/erf,edf->erd/dot_general | solution.py:130
  290.4 3.3 concatenate.55
  293.7 3.6 all-to-all-start.1
  298.4 20.4 %all-to-all-done.1 = bf16[4,128,1664]{2,1,0:T(8,128)(2,1)S(1)} async-done(((bf16[4,128,1664]{2,1,0:T(8,128)(2,1)}), bf16[4,128,1664]{2,1,0:T(8,128)(2,1)S(1)}, u32[]{:S(2)}, u32[]{:S(2)}) %all-to-all-start.1) | async-done | bytes 1703968 | tf_op jit(solution)/shard_map/all_to_all | solution.py:52
  320.2 2.3 multiply_reduce_fusion.2
  322.4 2.4 fusion.132
  325.0 4.0 convolution_convert_fusion.4
  330.2 4.8 all-to-all-start.2
  335.1 31.7 %all-gather.18.cloned.1.call-done = bf16[8192,192]{0,1:T(8,128)(2,1)} async-done(((bf16[1024,192]{0,1:T(8,128)(2,1)}), bf16[8192,192]{0,1:T(8,128)(2,1)}) %all-gather.18.cloned.1.call-update) | async-done | bytes 3145744 | tf_op jit(solution)/shard_map/all_gather | solution.py:56
  366.8 4.1 copy.379
  370.9 1.7 copy.338
  374.0 2.3 copy.330
  376.3 1.9 slice.142
  380.7 3.1 convolution_convert_fusion.3
  383.8 9.4 %fusion.6 = bf16[3,1024,1024]{1,2,0:T(8,128)(2,1)S(1)} fusion(f32[1024,1024,3]{1,0,2:T(8,128)} %copy-done.3, f32[3,1024]{1,0:T(4,128)S(1)} %bitcast.296, f32[3,1024]{1,0:T(4,128)} %get-tuple-element.99, pred[1024,1024]{0,1:T(8,128)(4,1)} %fusion.35, bf16[1024,3,64]{0,2,1:T(8,128)(2,1)S(1)} %bitcast.278, bf16[1024,320]{0,1:T(8,128)(2,1)} %copy-done.29), kind=kOutput, calls=%fused_computation.15 | convolution fusion | flops 421527552 | bytes 20475904 | tf_op jit(solution)/shard_map/tgd,sd->gts/dot_general | solution.py:108
  393.3 2.3 fusion.57
  395.6 2.0 fusion.62
  397.7 3.0 fusion.63
  402.8 2.3 copy.371
  405.8 13.5 %convolution_bitcast_fusion = f32[2,32,64,1536]{3,2,0,1:T(8,128)} fusion(bf16[32,128,1536,1]{2,1,3,0:T(8,128)(2,1)} %bitcast.250, s32[32,2,128]{2,1,0:T(2,128)S(1)} %copy-done.22, pred[32,2,128]{2,1,0:T(4,128)(4,1)S(1)} %copy.310), kind=kOutput, calls=%fused_computation.3 | convolution fusion | flops 1611661312 | bytes 37789696 | tf_op jit(solution)/shard_map/best,btd->ebsd/dot_general | solution.py:242
  419.3 18.6 %copy.346 = f32[2,32,64,1536]{3,2,1,0:T(8,128)} copy(f32[2,32,64,1536]{3,2,0,1:T(8,128)} %convolution_bitcast_fusion) | data formatting | bytes 50331648 | tf_op jit(solution)/shard_map/best,btd->ebsd/transpose | solution.py:242
  439.0 4.2 all-to-all-start.3
  443.3 33.0 %all-gather.22.cloned.1.call-done = bf16[4096,1536]{1,0:T(8,128)(2,1)} async-done(((bf16[128,1536]{1,0:T(8,128)(2,1)}), bf16[4096,1536]{1,0:T(8,128)(2,1)}) %all-gather.22.cloned.1.call-update) | async-done | bytes 12582928 | tf_op jit(solution)/shard_map/all_gather | solution.py:56
  476.3 6.8 fusion.141
  484.0 9.8 %fusion.12 = bf16[2,32,64,1536]{3,2,0,1:T(8,128)(2,1)} fusion(bf16[32,128,1536,1]{2,1,3,0:T(8,128)(2,1)} %bitcast.248, s32[32,2,128]{2,1,0:T(2,128)S(1)} %copy-done.22, pred[32,2,128]{2,1,0:T(4,128)(4,1)S(1)} %copy.310), kind=kOutput, calls=%fused_computation.25 | convolution fusion | flops 1617952768 | bytes 25206784 | tf_op jit(solution)/shard_map/best,btd->ebsd/dot_general | solution.py:242
  493.8 11.0 %copy.344 = bf16[2,32,64,1536]{3,2,1,0:T(8,128)(2,1)} copy(bf16[2,32,64,1536]{3,2,0,1:T(8,128)(2,1)} %fusion.12) | data formatting | bytes 25165824 | tf_op jit(solution)/shard_map/convert_element_type | solution.py:346
  504.8 35.7 %fusion.15 = f32[2,2048,2048]{1,2,0:T(8,128)} fusion(bf16[2,2048,1536]{2,1,0:T(8,128)(2,1)} %bitcast.255, bf16[2,1536,3072]{2,1,0:T(8,128)(2,1)} %param.16), kind=kOutput, calls=%fused_computation.28 | convolution fusion | flops 25769803776 | bytes 58720256 | tf_op jit(solution)/shard_map/erd,edf->erf/dot_general | solution.py:137
  540.5 13.3 %fusion = bf16[2,2048,1536]{2,1,0:T(8,128)(2,1)} fusion(f32[2,32,64,1536]{3,2,1,0:T(8,128)} %copy.346, f32[2,2048]{1,0:T(2,128)S(1)} %mul.370), kind=kLoop, calls=%fused_computation.2 | loop fusion | flops 12582912 | bytes 37765120 | tf_op jit(solution)/shard_map/convert_element_type | solution.py:347
  553.9 29.0 %multiply_convert_fusion.2 = (bf16[2,2048,1024]{1,2,0:T(8,128)(2,1)}, bf16[2,2048,1024]{1,2,0:T(8,128)(2,1)}) fusion(f32[2,2048,2048]{1,2,0:T(8,128)} %fusion.15, bf16[2,2048,1536]{2,1,0:T(8,128)(2,1)} %fusion, bf16[2,1536,3072]{2,1,0:T(8,128)(2,1)} %param.16), kind=kOutput, calls=%fused_computation.10 | convolution fusion | flops 12939427840 | bytes 69206016 | tf_op jit(solution)/shard_map/erd,edf->erf/dot_general | solution.py:141
  582.8 29.3 %fusion.21 = f32[2,1536,1024]{2,1,0:T(8,128)} fusion(bf16[2,2048,1536]{2,1,0:T(8,128)(2,1)} %fusion, f32[2,2048,2048]{1,2,0:T(8,128)} %fusion.15), kind=kOutput, calls=%fused_computation.34 | convolution fusion | flops 12910067712 | bytes 58720256 | tf_op jit(solution)/shard_map/erd,erf->edf/dot_general | solution.py:148
  612.1 2.0 copy.372
  614.1 42.4 %fusion.1 = f32[2,1536,2048]{2,1,0:T(8,128)} fusion(bf16[2,2048,1536]{2,1,0:T(8,128)(2,1)} %bitcast.256, bf16[2,2048,1024]{1,2,0:T(8,128)(2,1)} %get-tuple-element.83, bf16[2,2048,1024]{1,2,0:T(8,128)(2,1)} %get-tuple-element.82), kind=kOutput, calls=%fused_computation.4 | convolution fusion | flops 25803358208 | bytes 54525952 | tf_op jit(solution)/shard_map/erd,erf->edf/dot_general | solution.py:147
  656.5 27.7 %pad_maximum_fusion = f32[2,1536,3072]{2,1,0:T(8,128)} fusion(f32[2,1536,1024]{2,1,0:T(8,128)} %fusion.21, f32[2,1536,2048]{2,1,0:T(8,128)} %fusion.1), kind=kLoop, calls=%fused_computation | loop fusion | flops 9437184 | bytes 75497472 | tf_op jit(solution)/shard_map/concatenate | solution.py:149
  686.4 6.0 fusion.71
  693.5 2.7 convert_element_type.239
  700.6 1.8 copy.342
  702.4 3.0 copy.353
  707.5 2.4 multiply_reduce_fusion
  710.4 5.4 copy.352
  (233 shorter events, 44.3 us)
Async XLA Ops:
  7.2 8.5 %copy-start.45 = (bf16[384,8]{0,1:T(8,128)(2,1)S(1)}, bf16[384,8]{0,1:T(8,128)(2,1)}, u32[]{:S(2)}) copy-start(bf16[384,8]{0,1:T(8,128)(2,1)} %param.13) | copy-start | bytes 18436
  7.2 8.7 %copy-start.52 = (s32[1,8]{1,0:T(1,128)S(1)}, s32[1,8]{1,0:T(1,128)}, u32[]{:S(2)}) copy-start(s32[1,8]{1,0:T(1,128)} %param.17) | copy-start | bytes 100
  7.2 66.2 %all-gather.24.cloned.1.call-start = ((), (), s32[]{:S(2)}) async-start(), calls=%async_computation.13 | async-start | bytes 3538944 | tf_op jit(solution)/shard_map/all_gather | solution.py:56
  7.9 103.1 %all-gather.10.cloned.1.call-start = ((), (), s32[]{:S(2)}) async-start(), calls=%async_computation.6 | async-start | bytes 5898240 | tf_op jit(solution)/shard_map/all_gather | solution.py:56
  8.7 206.6 %all-gather.12.cloned.1.call-start = ((), (), s32[]{:S(2)}) async-start(), calls=%async_computation.7 | async-start | bytes 14057472 | tf_op jit(solution)/shard_map/all_gather | solution.py:56
  9.5 2.6 copy-start.25
  11.4 224.4 %all-gather.14.cloned.1.call-start = ((), (), s32[]{:S(2)}) async-start(), calls=%async_computation.8 | async-start | bytes 1966080 | tf_op jit(solution)/shard_map/all_gather | solution.py:56
  15.6 63.6 %copy-start.5 = (bf16[384,2560]{0,1:T(8,128)(2,1)}, bf16[384,2560]{0,1:T(8,128)(2,1)S(1)}, u32[]{:S(2)}) copy-start(bf16[384,2560]{0,1:T(8,128)(2,1)S(1)} %copy.303) | copy-start | bytes 5898244
  27.4 51.9 %copy-start.23 = (bf16[1536,330]{0,1:T(8,128)(2,1)}, bf16[1536,330]{0,1:T(8,128)(2,1)S(1)}, u32[]{:S(2)}) copy-start(bf16[1536,330]{0,1:T(8,128)(2,1)S(1)} %all_gather.28) | copy-start | bytes 3041284
  27.4 51.9 %copy-start.42 = (f32[1536]{0:T(1024)}, f32[1536]{0:T(1024)S(1)}, u32[]{:S(2)}) copy-start(f32[1536]{0:T(1024)S(1)} %get-tuple-element.69) | copy-start | bytes 18436
  27.4 87.4 %copy-start.32 = (f32[1536]{0:T(1024)}, f32[1536]{0:T(1024)S(1)}, u32[]{:S(2)}) copy-start(f32[1536]{0:T(1024)S(1)} %get-tuple-element.68) | copy-start | bytes 18436
  76.0 3.3 copy-start.49
  76.0 3.4 copy-start.7
  79.3 2.5 copy-start.29
  79.3 2.5 copy-start.17
  81.9 5.0 copy-start.3
  86.9 24.2 %copy-start.10 = (bf16[1,128,1536]{2,1,0:T(8,128)(2,1)S(1)}, bf16[1,128,1536]{2,1,0:T(8,128)(2,1)}, u32[]{:S(2)}) copy-start(bf16[1,128,1536]{2,1,0:T(8,128)(2,1)} %param.10) | copy-start | bytes 1179652
  116.3 206.1 %reduce-scatter.7.cloned.1.call-start = ((), (), s32[]{:S(2)}) async-start(), calls=%async_computation.14 | async-start | bytes 1966080 | tf_op jit(solution)/shard_map/reduce_scatter | solution.py:60
  224.5 6.2 copy-start.21
  230.7 5.1 copy-start
  235.8 16.3 %copy-start.30 = (pred[32,128,8]{1,2,0:T(8,128)(4,1)}, pred[32,128,8]{1,2,0:T(8,128)(4,1)S(1)}, u32[]{:S(2)}) copy-start(pred[32,128,8]{1,2,0:T(8,128)(4,1)S(1)} %fusion.93) | copy-start | bytes 98308
  244.6 7.5 %copy-start.53 = (f32[2,256,2048]{2,1,0:T(8,128)}, f32[2,256,2048]{2,1,0:T(8,128)S(1)}, u32[]{:S(2)}) copy-start(f32[2,256,2048]{2,1,0:T(8,128)S(1)} %fusion.19) | copy-start | bytes 12582916
  261.6 105.2 %all-gather.18.cloned.1.call-start = ((), (), s32[]{:S(2)}) async-start(), calls=%async_computation.10 | async-start | bytes 3538944 | tf_op jit(solution)/shard_map/all_gather | solution.py:56
  262.2 214.1 %all-gather.22.cloned.1.call-start = ((), (), s32[]{:S(2)}) async-start(), calls=%async_computation.12 | async-start | bytes 12976128 | tf_op jit(solution)/shard_map/all_gather | solution.py:56
  288.1 9.2 %copy-start.26 = (s32[1,128,2]{2,1,0:T(8,128)S(1)}, s32[1,128,2]{2,1,0:T(8,128)}, u32[]{:S(2)}) copy-start(s32[1,128,2]{2,1,0:T(8,128)} %copy-done.25) | copy-start | bytes 3076
  288.1 9.3 %copy-start.4 = (bf16[128,1536]{1,0:T(8,128)(2,1)S(1)}, bf16[128,1536]{1,0:T(8,128)(2,1)}, u32[]{:S(2)}) copy-start(bf16[128,1536]{1,0:T(8,128)(2,1)} %multiply_convert_fusion.8) | copy-start | bytes 1179652
  288.1 32.0 %copy-start.2 = (f32[128,1536]{1,0:T(8,128)S(1)}, f32[128,1536]{1,0:T(8,128)}, u32[]{:S(2)}) copy-start(f32[128,1536]{1,0:T(8,128)} %copy-done.1) | copy-start | bytes 2359300
  288.1 32.0 %copy-start.33 = (f32[1536]{0:T(1024)S(1)}, f32[1536]{0:T(1024)}, u32[]{:S(2)}) copy-start(f32[1536]{0:T(1024)} %copy-done.32) | copy-start | bytes 18436
  288.1 32.0 %copy-start.47 = (f32[128]{0:T(128)S(1)}, f32[128]{0:T(128)}, u32[]{:S(2)}) copy-start(f32[128]{0:T(128)} %copy-done.46) | copy-start | bytes 1540
  290.4 32.1 %copy-start.15 = (bf16[1,128,1536]{2,1,0:T(8,128)(2,1)S(1)}, bf16[1,128,1536]{2,1,0:T(8,128)(2,1)}, u32[]{:S(2)}) copy-start(bf16[1,128,1536]{2,1,0:T(8,128)(2,1)} %param.19) | copy-start | bytes 1179652
  290.4 32.1 %copy-start.51 = (f32[128]{0:T(128)S(1)}, f32[128]{0:T(128)}, u32[]{:S(2)}) copy-start(f32[128]{0:T(128)} %get-tuple-element.105) | copy-start | bytes 1540
  293.7 25.0 %all-to-all-start.1 = ((bf16[4,128,1664]{2,1,0:T(8,128)(2,1)}), bf16[4,128,1664]{2,1,0:T(8,128)(2,1)S(1)}, u32[]{:S(2)}, u32[]{:S(2)}) async-start(bf16[4,128,1664]{2,1,0:T(8,128)(2,1)} %concatenate.55), calls=%async_computation.1 | async-start | bytes 3407872 | tf_op jit(solution)/shard_map/all_to_all | solution.py:52
  320.2 8.9 %copy-start.38 = (bf16[128,8]{0,1:T(8,128)(2,1)}, bf16[128,8]{0,1:T(8,128)(2,1)S(1)}, u32[]{:S(2)}) copy-start(bf16[128,8]{0,1:T(8,128)(2,1)S(1)} %select_convert_fusion) | copy-start | bytes 6148
  330.2 43.8 %all-to-all-start.2 = ((bf16[8,128,384]{1,2,0:T(8,128)(2,1)}), bf16[8,128,384]{1,2,0:T(8,128)(2,1)}, u32[]{:S(2)}, u32[]{:S(2)}) async-start(bf16[8,128,384]{1,2,0:T(8,128)(2,1)} %maximum_bitcast_fusion), calls=%async_computation.2 | async-start | bytes 1572864 | tf_op jit(solution)/shard_map/all_to_all | solution.py:52
  335.0 277.1 %reduce-scatter.9.cloned.1.call-start = ((), (), s32[]{:S(2)}) async-start(), calls=%async_computation.15 | async-start | bytes 2457600
  366.8 5.8 copy-start.40
  366.8 6.4 copy-start.39
  383.8 13.8 %slice-start = ((s8[12582912]{0:T(1024)(128)(4,1)}), s8[4194304]{0:T(1024)(128)(4,1)S(1)}, s32[]{:S(2)}) async-start(s8[12582912]{0:T(1024)(128)(4,1)} %bitcast.259), calls=%async_computation.16 | async-start | bytes 8388608
  383.8 13.8 %slice-start.1 = ((s8[12582912]{0:T(1024)(128)(4,1)}), s8[4194304]{0:T(1024)(128)(4,1)S(1)}, s32[]{:S(2)}) async-start(s8[12582912]{0:T(1024)(128)(4,1)} %bitcast.259), calls=%async_computation.17 | async-start | bytes 8388608
  393.2 2.3 copy-start.18
  393.2 4.4 slice-start.2
  393.2 4.4 copy-start.8
  393.3 4.4 copy-start.41
  395.5 5.2 copy-start.19
  397.6 3.1 copy-start.27
  397.7 3.1 copy-start.12
  397.7 3.1 copy-start.43
  397.7 3.1 copy-start.50
  400.7 1.5 copy-start.14
  400.7 1.5 copy-start.36
  400.7 1.5 copy-start.37
  402.1 3.7 copy-start.22
  405.1 281.3 %all-gather.16.cloned.1.call-start = ((), (), s32[]{:S(2)}) async-start(), calls=%async_computation.9 | async-start | bytes 9830400 | tf_op jit(solution)/shard_map/all_gather | solution.py:56
  419.3 18.6 %copy-start.28 = (bf16[1024,64]{0,1:T(8,128)(2,1)S(1)}, bf16[1024,64]{0,1:T(8,128)(2,1)}, u32[]{:S(2)}) copy-start(bf16[1024,64]{0,1:T(8,128)(2,1)} %copy-done.27) | copy-start | bytes 393220
  419.3 18.6 %copy-start.35 = (bf16[1024,64]{0,1:T(8,128)(2,1)S(1)}, bf16[1024,64]{0,1:T(8,128)(2,1)}, u32[]{:S(2)}) copy-start(bf16[1024,64]{0,1:T(8,128)(2,1)} %copy-done.34) | copy-start | bytes 393220
  419.3 18.6 %copy-start.20 = (bf16[64,3,1024]{2,0,1:T(8,128)(2,1)S(1)}, bf16[64,3,1024]{2,0,1:T(8,128)(2,1)}, u32[]{:S(2)}) copy-start(bf16[64,3,1024]{2,0,1:T(8,128)(2,1)} %copy-done.19) | copy-start | bytes 1179652
  419.3 56.9 %copy-start.31 = (pred[32,128,8]{1,2,0:T(8,128)(4,1)S(1)}, pred[32,128,8]{1,2,0:T(8,128)(4,1)}, u32[]{:S(2)}) copy-start(pred[32,128,8]{1,2,0:T(8,128)(4,1)} %copy-done.30) | copy-start | bytes 98308
  439.0 245.3 %all-to-all-start.3 = ((bf16[8,128,320]{1,2,0:T(8,128)(2,1)}), bf16[8,128,320]{1,2,0:T(8,128)(2,1)}, u32[]{:S(2)}, u32[]{:S(2)}) async-start(bf16[8,128,320]{1,2,0:T(8,128)(2,1)} %pad_maximum_fusion.2), calls=%async_computation.3 | async-start | bytes 1310720 | tf_op jit(solution)/shard_map/all_to_all | solution.py:52
  443.2 250.3 %all-gather.20.cloned.1.call-start = ((), (), s32[]{:S(2)}) async-start(), calls=%async_computation.11 | async-start | bytes 3649536 | tf_op jit(solution)/shard_map/all_gather | solution.py:56
  656.5 29.9 %copy-start.11 = (bf16[1,128,1536]{2,1,0:T(8,128)(2,1)S(1)}, bf16[1,128,1536]{2,1,0:T(8,128)(2,1)}, u32[]{:S(2)}) copy-start(bf16[1,128,1536]{2,1,0:T(8,128)(2,1)} %param.10) | copy-start | bytes 1179652
  656.5 29.9 %copy-start.44 = (f32[1536]{0:T(1024)S(1)}, f32[1536]{0:T(1024)}, u32[]{:S(2)}) copy-start(f32[1536]{0:T(1024)} %copy-done.42) | copy-start | bytes 18436
  684.3 8.2 %copy-start.13 = (f32[128,1536]{1,0:T(8,128)S(1)}, f32[128,1536]{1,0:T(8,128)}, u32[]{:S(2)}) copy-start(f32[128,1536]{1,0:T(8,128)} %get-tuple-element.75) | copy-start | bytes 2359300
  705.4 2.1 copy-start.6
  705.9 4.0 copy-start.48
  (6 other events, 6.0 us)
Sparse Core Ops, SparseCore 0:
  10.2 63.1 all-gather.23
  74.9 36.0 all-gather.9
  114.5 100.7 all-gather.11
  217.3 17.8 all-gather.13
  261.7 27.4 reduce-scatter.6
  291.5 75.1 all-gather.17
  370.6 105.5 all-gather.21
  479.6 29.6 reduce-scatter.8
  510.8 55.3 all-gather.15
  614.2 62.3 all-gather.19

commit v2 on v1

v2 whole, which is shorter than its diff:
```python
import functools

import jax
import jax.numpy as jnp
from jax import lax
from jax.experimental import pallas as pl
from jax.experimental.pallas import tpu as pltpu
from jax.sharding import PartitionSpec as P

HQ = 24
HK = 8
HD = 64
GROUP = HQ // HK
FF = 1024
EXPERTS = 8
CAP = 64
Q_COLS = HQ * HD
K_COLS = HK * HD
HEAD_COLS = GROUP * HD + 2 * HD
SMALL = 16
LANES = 128
TILE = 256
CHUNK = 512
WINDOW = 2 * CAP + 16
SEGMENT = 32

NORM_EPS = 1e-05
MASK_NEG = -1e30
BF = jnp.bfloat16
F32 = jnp.float32


def dot(a, b):
    return jnp.dot(a, b, preferred_element_type=F32)


def dot_t(a, b):
    return lax.dot_general(a, b, (((1,), (1,)), ((), ())), preferred_element_type=F32)


def t_dot(a, b):
    return lax.dot_general(a, b, (((0,), (0,)), ((), ())), preferred_element_type=F32)


def iota(shape, axis):
    return lax.broadcasted_iota(jnp.int32, shape, axis)


def rms_factor(values):
    return lax.rsqrt(jnp.mean(values * values, axis=-1, keepdims=True) + NORM_EPS)


def rms_input_grad(values, factor, gain_vec, incoming):
    inner = incoming * gain_vec
    cubed = factor * factor * factor
    return factor * inner - values * cubed * jnp.mean(inner * values, axis=-1, keepdims=True)


def doc_index(doc_bounds, positions):
    hits = (positions[:, None] >= doc_bounds[None, :]).astype(jnp.int32)
    return jnp.sum(hits, axis=1)


def to_all(value, axis):
    return lax.all_to_all(value, axis, 0, 0, tiled=True)


def gathered(value, axis):
    return lax.all_gather(value, axis, axis=0, tiled=True)


def exchanged(value, axis, distance):
    count = lax.axis_size(axis)
    return lax.ppermute(value, axis, [(i, i ^ distance) for i in range(count)])


def near_blocks(own):
    blocks = {0: own}
    distance = lax.axis_size("fsdp") // 2
    while distance:
        blocks.update({r ^ distance: exchanged(b, "fsdp", distance) for r, b in blocks.items()})
        distance //= 2
    return [blocks[r] for r in range(len(blocks))]


def near_sum(blocks):
    distance = 1
    while distance < lax.axis_size("fsdp"):
        blocks = {
            r: blocks[r].astype(F32)
            + exchanged(blocks[r ^ distance].astype(BF), "fsdp", distance).astype(F32)
            for r in range(0, lax.axis_size("fsdp"), 2 * distance)
        }
        distance *= 2
    return blocks[0]


def in_order(blocks, own):
    stacked = jnp.stack(blocks)
    return jnp.take(stacked, jnp.arange(len(blocks), dtype=jnp.int32) ^ own, axis=0)


def span_blocks(own):
    spans = lax.axis_size("ctx")
    half = own.shape[0] // 2
    first, last = own[:half], own[half:]
    pair = jnp.stack([first, exchanged(first, "ctx", 1)])
    firsts = [pair] + [exchanged(pair, "ctx", d) for d in range(2, spans, 2)]
    lasts = jnp.stack([last] + [exchanged(last, "ctx", d) for d in range(2, spans, 2)])
    other = exchanged(lasts, "ctx", 1)
    return [
        jnp.concatenate([firsts[r // 2][r % 2], (other if r % 2 else lasts)[r // 2]])
        for r in range(spans)
    ]


def picked_gates(second, router_t, chosen):
    logits = dot_t(router_t, second)
    ids = iota(logits.shape, 0)
    picked = (ids == chosen[0:1, :]) | (ids == chosen[1:2, :])
    logits = jnp.where(picked, logits, MASK_NEG)
    parts = jnp.where(picked, jnp.exp(logits - jnp.max(logits, axis=0, keepdims=True)), 0.0)
    return picked, parts / jnp.sum(parts, axis=0, keepdims=True)


def swiglu_grads(gate, up, d_hidden):
    sigma = 1.0 / (1.0 + jnp.exp(-gate))
    passed = gate * sigma
    d_gate = d_hidden * up * sigma * (1.0 + gate * (1.0 - sigma))
    return (passed * up).astype(BF), d_gate.astype(BF), (d_hidden * passed).astype(BF)


def near_kernel(shards, shard_ref, *refs):
    second, grads = refs[:shards], refs[shards : 2 * shards]
    chosen, router_t, w_gate, w_up, w_down = refs[2 * shards : 2 * shards + 5]
    branch_out = refs[2 * shards + 5 : 3 * shards + 5]
    back_out = refs[3 * shards + 5 : 4 * shards + 5]
    hot, rows, cots, d_outs, slot_gate, out_acc, row_acc, branch_acc, back_acc = refs[
        4 * shards + 5 :
    ]
    expert, tile = pl.program_id(0), pl.program_id(1)
    tokens = second[0].shape[0]
    width = second[0].shape[1]
    wanted = shard_ref[0] * pl.num_programs(0) + expert

    @pl.when(tile == 0)
    def _():
        before = (iota((tokens, tokens), 0) < iota((tokens, tokens), 1)).astype(BF)
        for f in range(shards):
            picked, gates = picked_gates(second[f][...], router_t[...], chosen[f])
            ranks = dot(picked.astype(BF), before)
            found = (iota(ranks.shape, 0) == wanted) & picked
            rank = jnp.sum(jnp.where(found, ranks + 1.0, 0.0), axis=0, keepdims=True)
            gate = jnp.sum(jnp.where(found, gates, 0.0), axis=0, keepdims=True)
            match = iota((CAP, tokens), 0).astype(F32) + 1.0 == rank
            one_hot = match.astype(BF)
            place = pl.ds(f * CAP, CAP)
            hot[f] = one_hot
            found_gate = jnp.sum(jnp.where(match, gate, 0.0), axis=1, keepdims=True)
            slot_gate[place, :] = jnp.broadcast_to(found_gate, (CAP, LANES))
            rows[place, :] = dot(one_hot, second[f][...]).astype(BF)
            cot = dot(one_hot, grads[f][:, :width])
            cots[place, :] = cot.astype(BF)
            d_outs[place, :] = (found_gate * cot).astype(BF)
        out_acc[...] = jnp.zeros_like(out_acc)
        row_acc[...] = jnp.zeros_like(row_acc)

    hidden, d_gate, d_up = swiglu_grads(
        dot(rows[...], w_gate[0]), dot(rows[...], w_up[0]), dot(d_outs[...], w_down[0])
    )
    out_acc[...] += dot_t(hidden, w_down[0])
    row_acc[...] += dot_t(d_gate, w_gate[0]) + dot_t(d_up, w_up[0])

    @pl.when(tile == pl.num_programs(1) - 1)
    def _():
        last = expert == pl.num_programs(0) - 1
        for f in range(shards):
            place = pl.ds(f * CAP, CAP)
            out = out_acc[place, :].astype(BF).astype(F32)
            d_gates = jnp.sum(cots[place, :].astype(F32) * out, axis=1, keepdims=True)
            gated = (slot_gate[place, 0:1] * out).astype(BF)
            lane = iota((CAP, LANES), 1)
            coarse = d_gates.astype(BF).astype(F32)
            extra = jnp.where(lane == wanted, coarse, 0.0)
            extra = extra + jnp.where(lane == EXPERTS + wanted, d_gates - coarse, 0.0)

            def add(acc, part, columns):
                @pl.when(expert == 0)
                def _():
                    acc[f, :, columns] = part

                @pl.when(expert > 0)
                def _():
                    acc[f, :, columns] += part

            add(branch_acc, t_dot(hot[f], gated), slice(0, width))
            add(back_acc, t_dot(hot[f], row_acc[place, :].astype(BF)), slice(0, width))
            add(back_acc, t_dot(hot[f], extra.astype(BF)), slice(width, width + LANES))

            @pl.when(last)
            def _():
                branch_out[f][...] = branch_acc[f].astype(BF)
                back_out[f][...] = back_acc[f].astype(BF)


def near_experts(second, grads, chosen, router_t, w_experts, shard):
    shards = len(second)
    tokens, width = second[0].shape
    experts = w_experts.shape[0]
    slots = shards * CAP
    tiles = FF // TILE

    def whole(shape):
        return pl.BlockSpec(shape, lambda e, j, s: (0,) * len(shape))

    def weight(part):
        return pl.BlockSpec((1, width, TILE), lambda e, j, s: (e, 0, part * tiles + j))

    outs = pl.pallas_call(
        functools.partial(near_kernel, shards),
        grid_spec=pltpu.PrefetchScalarGridSpec(
            num_scalar_prefetch=1,
            grid=(experts, tiles),
            in_specs=[whole((tokens, width))] * shards
            + [whole((tokens, width + LANES))] * shards
            + [whole(chosen.shape), whole(router_t.shape), weight(0), weight(1), weight(2)],
            out_specs=[whole((tokens, width))] * shards
            + [whole((tokens, width + LANES))] * shards,
            scratch_shapes=[
                pltpu.VMEM((shards, CAP, tokens), BF),
                pltpu.VMEM((slots, width), BF),
                pltpu.VMEM((slots, width), BF),
                pltpu.VMEM((slots, width), BF),
                pltpu.VMEM((slots, LANES), F32),
                pltpu.VMEM((slots, width), F32),
                pltpu.VMEM((slots, width), F32),
                pltpu.VMEM((shards, tokens, width), F32),
                pltpu.VMEM((shards, tokens, width + LANES), F32),
            ],
        ),
        out_shape=[jax.ShapeDtypeStruct((tokens, width), BF)] * shards
        + [jax.ShapeDtypeStruct((tokens, width + LANES), BF)] * shards,
        compiler_params=pltpu.CompilerParams(vmem_limit_bytes=56 * 1024 * 1024),
        cost_estimate=pl.CostEstimate(
            flops=12 * experts * slots * width * FF,
            bytes_accessed=w_experts.size * 2,
            transcendentals=experts * slots * FF,
        ),
        name="near_experts",
    )(shard.reshape(1), *second, *grads, chosen, router_t, w_experts, w_experts, w_experts)
    return outs[:shards], outs[shards:]


def far_kernel(
    meta,
    chosen,
    places,
    router_t,
    second_ref,
    grads_ref,
    w_gate,
    w_up,
    w_down,
    out_ref,
    rows,
    d_outs,
    act,
    fetched,
    tile_out,
    fetch_sem,
    store_sem,
):
    expert, tile = pl.program_id(0), pl.program_id(1)
    tiles = pl.num_programs(1)
    step = expert * tiles + tile
    slot = lax.rem(step, 2)
    groups = chosen.shape[0]
    size = chosen.shape[2]
    width = w_gate.shape[1]
    wanted = meta[pl.num_programs(0), 0] + expert
    count = meta[expert, groups]
    chunks = jnp.maximum((count + CHUNK - 1) // CHUNK, 1)

    def stores(which, e, j):
        return [
            pltpu.make_async_copy(
                tile_out.at[which, i],
                out_ref.at[e, :, pl.ds(pl.multiple_of(i * FF + j * TILE, TILE), TILE)],
                store_sem.at[which, i],
            )
            for i in range(3)
        ]

    def fetches(which, g):
        at = pl.ds(pl.multiple_of(g * size, size), size)
        return [
            pltpu.make_async_copy(
                ref.at[at, pl.ds(0, width)], fetched.at[which, i], fetch_sem.at[which, i]
            )
            for i, ref in enumerate((second_ref, grads_ref))
        ]

    @pl.when(tile == 0)
    def _():
        for copy in fetches(0, 0):
            copy.start()
        tail = pl.ds(pl.multiple_of((chunks - 1) * CHUNK, CHUNK), CHUNK)
        rows[tail, :] = jnp.zeros((CHUNK, width), BF)
        d_outs[tail, :] = jnp.zeros((CHUNK, width), BF)

        @pl.loop(0, groups)
        def _(g):
            which = lax.rem(g, 2)
            for copy in fetches(which, g):
                copy.wait()

            @pl.when(g + 1 < groups)
            def _():
                for copy in fetches(1 - which, g + 1):
                    copy.start()

            second, grads = fetched[which, 0], fetched[which, 1]
            picked, gates = picked_gates(second, router_t[...], chosen[g])
            found = (iota(gates.shape, 0) == wanted) & picked
            gate = jnp.sum(jnp.where(found, gates, 0.0), axis=0, keepdims=True)
            start = meta[expert, g]
            base = start // 16 * 16
            match = iota((WINDOW, size), 0) == places[expert, pl.ds(g, 1), :] - base
            one_hot = match.astype(BF)
            found_gate = jnp.sum(jnp.where(match, gate, 0.0), axis=1, keepdims=True)
            at = pl.ds(pl.multiple_of(base, 16), 16)
            rest = pl.ds(pl.multiple_of(base + 16, 16), WINDOW - 16)
            held = iota((16, width), 0) < start - base
            for ref, new in (
                (rows, dot(one_hot, second).astype(BF)),
                (d_outs, (found_gate * dot(one_hot, grads)).astype(BF)),
            ):
                ref[at, :] = jnp.where(held, ref[at, :], new[:16])
                ref[rest, :] = new[16:]

    @pl.loop(0, chunks)
    def _(i):
        at = pl.ds(pl.multiple_of(i * CHUNK, CHUNK), CHUNK)
        hidden, d_gate, d_up = swiglu_grads(
            dot(rows[at, :], w_gate[0]), dot(rows[at, :], w_up[0]), dot(d_outs[at, :], w_down[0])
        )
        act[0, at, :] = d_gate
        act[1, at, :] = d_up
        act[2, at, :] = hidden

    @pl.when(step >= 2)
    def _():
        for copy in stores(slot, (step - 2) // tiles, lax.rem(step - 2, tiles)):
            copy.wait()

    for k in range(1, act.shape[1] // CHUNK + 1):

        @pl.when(chunks == k)
        def _():
            upto = k * CHUNK
            tile_out[slot, 0] = t_dot(rows[:upto, :], act[0, :upto, :])
            tile_out[slot, 1] = t_dot(rows[:upto, :], act[1, :upto, :])
            tile_out[slot, 2] = t_dot(d_outs[:upto, :], act[2, :upto, :])

    for copy in stores(slot, expert, tile):
        copy.start()

    @pl.when(step == pl.num_programs(0) * tiles - 1)
    def _():
        for copy in stores(1 - slot, (step - 1) // tiles, lax.rem(step - 1, tiles)):
            copy.wait()
        for copy in stores(slot, expert, tile):
            copy.wait()


def far_weight_grads(meta, chosen, places, router_t, second, grads, w_experts):
    experts, width = w_experts.shape[:2]
    groups, _, size = chosen.shape
    tiles = FF // TILE
    most = groups * size // 2

    def whole(shape):
        return pl.BlockSpec(shape, lambda e, j, s: (0,) * len(shape))

    def weight(part):
        return pl.BlockSpec((1, width, TILE), lambda e, j, s: (e, 0, part * tiles + j))

    return pl.pallas_call(
        far_kernel,
        grid_spec=pltpu.PrefetchScalarGridSpec(
            num_scalar_prefetch=1,
            grid=(experts, tiles),
            in_specs=[
                whole(chosen.shape),
                whole(places.shape),
                whole(router_t.shape),
                pl.BlockSpec(memory_space=pl.ANY),
                pl.BlockSpec(memory_space=pl.ANY),
                weight(0),
                weight(1),
                weight(2),
            ],
            out_specs=pl.BlockSpec(memory_space=pl.ANY),
            scratch_shapes=[
                pltpu.VMEM((most + WINDOW, width), BF),
                pltpu.VMEM((most + WINDOW, width), BF),
                pltpu.VMEM((3, most, TILE), BF),
                pltpu.VMEM((2, 2, size, width), BF),
                pltpu.VMEM((2, 3, width, TILE), F32),
                pltpu.SemaphoreType.DMA((2, 2)),
                pltpu.SemaphoreType.DMA((2, 3)),
            ],
        ),
        out_shape=jax.ShapeDtypeStruct((experts, width, 3 * FF), F32),
        compiler_params=pltpu.CompilerParams(vmem_limit_bytes=56 * 1024 * 1024),
        cost_estimate=pl.CostEstimate(
            flops=12 * experts * most * width * FF,
            bytes_accessed=w_experts.size * 6 + 4 * experts * groups * size * width,
            transcendentals=experts * most * FF,
        ),
        name="far_weight_grads",
    )(meta, chosen, places, router_t, second, grads, w_experts, w_experts, w_experts)


def attention_forward(q, k, v, allowed):
    length = q.shape[0]
    scores = jnp.einsum(
        "tgd,sd->gts", q.reshape(length, GROUP, HD), k, preferred_element_type=F32
    ) * HD ** (-0.5)
    highest = jnp.max(jnp.where(allowed, scores, MASK_NEG), axis=-1, keepdims=True)
    weights = jnp.where(allowed, jnp.exp(scores - highest), 0.0)
    total = jnp.sum(weights, axis=-1, keepdims=True)
    total = jnp.where(total == 0.0, 1.0, total)
    log_norm = highest + jnp.log(total)
    probs = (weights / total).astype(BF)
    attended = jnp.einsum("gts,sd->tgd", probs, v, preferred_element_type=F32)
    return attended.reshape(length, GROUP * HD), log_norm


def attention_backward(q, k, v, allowed, log_norm, attended, grads):
    length = q.shape[0]
    scale = HD ** (-0.5)
    q3 = q.reshape(length, GROUP, HD)
    g3 = grads.reshape(length, GROUP, HD)
    delta = jnp.sum(g3.astype(F32) * attended.reshape(length, GROUP, HD), axis=-1).T
    scores = jnp.einsum("tgd,sd->gts", q3, k, preferred_element_type=F32) * scale
    probs = jnp.where(allowed, jnp.exp(scores - log_norm), 0.0)
    d_probs = jnp.einsum("tgd,sd->gts", g3, v, preferred_element_type=F32)
    d_scores = (probs * (d_probs - delta[..., None])).astype(BF)
    d_q = jnp.einsum("gts,sd->tgd", d_scores, k, preferred_element_type=F32) * scale
    d_k = jnp.einsum("gts,tgd->sd", d_scores, q3, preferred_element_type=F32) * scale
    d_v = jnp.einsum("gts,tgd->sd", probs.astype(BF), g3, preferred_element_type=F32)
    return jnp.concatenate([d_q.reshape(length, GROUP * HD), d_k, d_v], axis=1).astype(BF)


def per_device(
    tokens,
    query_key_value_weight,
    output_weight,
    routing_weight,
    gain_attn,
    gain_moe,
    w_experts,
    doc_starts,
    routes,
    cotangent,
):
    spans = lax.axis_size("ctx")
    shards = lax.axis_size("fsdp")
    here = lax.axis_index("ctx")
    shard = lax.axis_index("fsdp")
    tok_count, width = tokens.shape[1:]
    local_experts = w_experts.shape[0]
    copies = spans // HK
    head = here // copies
    length = spans * tok_count
    blocks = spans * shards
    everyone = ("ctx", "fsdp")
    first_expert = shard * local_experts

    route_cols = jnp.pad(routes[0].astype(BF), ((0, 0), (0, LANES - 2)))
    sent = jnp.concatenate([cotangent[0], route_cols], axis=1)
    grads_all = gathered(sent, everyone)

    shard_rows = query_key_value_weight.shape[0]
    head_w = jnp.concatenate(
        [
            lax.dynamic_slice_in_dim(query_key_value_weight, head * GROUP * HD, GROUP * HD, 1),
            lax.dynamic_slice_in_dim(query_key_value_weight, Q_COLS + head * HD, HD, 1),
            lax.dynamic_slice_in_dim(query_key_value_weight, Q_COLS + K_COLS + head * HD, HD, 1),
            routing_weight,
            gain_attn[:, None],
            gain_moe[:, None],
        ],
        axis=1,
    )
    head_w = in_order(near_blocks(head_w), shard).reshape(width, -1)
    router_w = head_w[:, HEAD_COLS : HEAD_COLS + EXPERTS]
    router_t = jnp.pad(router_w.T, ((0, 16 - EXPERTS), (0, 0)))
    attn_g = head_w[:, HEAD_COLS + EXPERTS].astype(F32)
    moe_g = head_w[:, HEAD_COLS + EXPERTS + 1].astype(F32)
    head_w = head_w[:, :HEAD_COLS]

    stream = in_order(span_blocks(tokens[0]), here).reshape(length, width)
    out_w = near_blocks(output_weight)
    qkv_w = near_blocks(query_key_value_weight)
    stream_f = stream.astype(F32)
    normed = (stream_f * rms_factor(stream_f) * attn_g).astype(BF)
    mixed = dot(normed, head_w).astype(BF)
    q = mixed[:, : GROUP * HD]
    k = mixed[:, GROUP * HD : GROUP * HD + HD]
    v = mixed[:, GROUP * HD + HD :]
    pos = jnp.arange(length, dtype=jnp.int32)
    docs = doc_index(doc_starts[0], pos)
    active = (pos // tok_count) % copies == here % copies
    allowed = (pos[None, :] <= pos[:, None]) & (docs[None, :] == docs[:, None]) & active[:, None]
    attended, log_norm = attention_forward(q, k, v, allowed)
    attended_low = attended.astype(BF)

    own = to_all(attended_low, "ctx").reshape(HK, copies, tok_count, GROUP * HD)
    own = jnp.sum(own, axis=1) if copies > 1 else own[:, 0]
    by_shard = jnp.arange(shards, dtype=jnp.int32) ^ shard
    own = own.reshape(shards, HK // shards, tok_count, GROUP * HD).swapaxes(1, 2)
    own = jnp.take(own, by_shard, axis=0).reshape(shards, tok_count, -1)
    x = tokens[0].astype(F32)
    middle = x
    for r in range(shards):
        middle = middle + dot(own[r], out_w[r])
    second_factor = rms_factor(middle)
    second = (middle * second_factor * moe_g).astype(BF)
    second_near = near_blocks(second)
    second_all = gathered(second, everyone)

    grads_all, second_near = lax.optimization_barrier((grads_all, second_near))
    chosen = grads_all[:, width : width + 2].astype(jnp.int32).reshape(blocks, tok_count, 2)
    chosen = chosen.swapaxes(1, 2)
    chosen_near = jnp.take(chosen, here * shards + by_shard, axis=0)
    grads_near = [
        lax.dynamic_slice_in_dim(grads_all, (here * shards + (shard ^ r)) * tok_count, tok_count, 0)
        for r in range(shards)
    ]
    branch, back = near_experts(
        second_near, grads_near, chosen_near, router_t, w_experts, shard
    )
    back = near_sum(back)
    output = (middle + near_sum(branch)).astype(BF)

    grad = cotangent[0].astype(F32)
    d_gates = back[:, width : width + EXPERTS] + back[:, width + EXPERTS : width + 2 * EXPERTS]
    own_picked = jnp.any(routes[0][:, :, None] == jnp.arange(EXPERTS, dtype=jnp.int32), axis=1)
    gates = jax.nn.softmax(jnp.where(own_picked, dot(second, router_w), MASK_NEG), axis=-1)
    d_picked = gates * (d_gates - jnp.sum(gates * d_gates, axis=-1, keepdims=True))
    d_logits = jnp.where(own_picked, d_picked, 0.0).astype(BF)
    d_router = t_dot(second, d_logits)
    d_second = dot_t(d_logits, router_w) + back[:, :width]
    d_gain_moe = jnp.sum(d_second * middle * second_factor, axis=0)
    d_middle = grad + rms_input_grad(middle, second_factor, moe_g, d_second)
    d_proj = d_middle.astype(BF)
    d_attended = in_order([dot_t(d_proj, out_w[r]).astype(BF) for r in range(shards)], shard)

    chunk = width // spans
    d_attended = d_attended.reshape(shards, tok_count, HK // shards, 1, GROUP * HD)
    d_attended = d_attended.transpose(0, 2, 3, 1, 4)
    d_attended = jnp.broadcast_to(
        d_attended, (shards, HK // shards, copies, tok_count, GROUP * HD)
    ).reshape(spans, tok_count, GROUP * HD)
    sent = jnp.concatenate(
        [d_attended, d_proj.reshape(tok_count, spans, chunk).swapaxes(0, 1)], axis=2
    )
    sent = to_all(sent.reshape(length, -1), "ctx")
    d_mixed = attention_backward(
        q, k, v, allowed, log_norm, attended, sent[:, : GROUP * HD]
    )
    attended_all = gathered(attended_low, "ctx").reshape(HK, copies, length, GROUP * HD)
    attended_all = jnp.sum(attended_all, axis=1) if copies > 1 else attended_all[:, 0]
    d_out_w = jnp.einsum(
        "hte,td->hed", attended_all, sent[:, GROUP * HD :], preferred_element_type=F32
    ).reshape(Q_COLS, chunk)
    small = jnp.concatenate(
        [d_router, d_gain_moe[:, None], jnp.zeros((width, SMALL - EXPERTS - 1), F32)], axis=1
    )
    d_head_w = t_dot(normed, d_mixed)

    def whole_columns(part):
        part = part.astype(BF)
        terms = [
            lax.dynamic_slice_in_dim(part, (shard ^ r) * shard_rows, shard_rows, 0)
            for r in range(shards)
        ]
        part = gathered(near_sum(terms).astype(BF), "ctx")
        return part.reshape(spans, shard_rows, -1).astype(F32)

    late = whole_columns(jnp.concatenate([d_head_w, d_out_w, small], axis=1))
    by_head = late[:, :, :HEAD_COLS].reshape(HK, copies, shard_rows, HEAD_COLS)
    by_head = jnp.sum(by_head, axis=1).swapaxes(0, 1)

    def columns(part):
        return part.reshape(shard_rows, -1)

    d_qkv_w = jnp.concatenate(
        [
            columns(by_head[:, :, : GROUP * HD]),
            columns(by_head[:, :, GROUP * HD : GROUP * HD + HD]),
            columns(by_head[:, :, GROUP * HD + HD :]),
        ],
        axis=1,
    )
    d_out_w = columns(late[:, :, HEAD_COLS : HEAD_COLS + chunk].swapaxes(0, 1))
    small = jnp.sum(late[:, :, HEAD_COLS + chunk :], axis=0)
    d_router_w = small[:, :EXPERTS]
    d_gain_moe = small[:, EXPERTS]
    d_gain_attn = jnp.sum(
        d_qkv_w * query_key_value_weight.astype(F32), axis=1
    ) / gain_attn.astype(F32)

    d_home = to_all(d_mixed, "ctx").reshape(HK, copies, tok_count, HEAD_COLS)
    d_home = jnp.sum(d_home.astype(F32), axis=1).astype(BF) if copies > 1 else d_home[:, 0]
    d_home = d_home.swapaxes(0, 1)
    d_home = jnp.concatenate(
        [
            d_home[:, :, : GROUP * HD].reshape(tok_count, -1),
            d_home[:, :, GROUP * HD : GROUP * HD + HD].reshape(tok_count, -1),
            d_home[:, :, GROUP * HD + HD :].reshape(tok_count, -1),
        ],
        axis=1,
    )
    d_normed = in_order([dot_t(d_home, qkv_w[r]) for r in range(shards)], shard)
    d_normed = d_normed.swapaxes(0, 1).reshape(tok_count, width)
    d_tokens = (d_middle + rms_input_grad(x, rms_factor(x), attn_g, d_normed)).astype(BF)

    segment = min(blocks, SEGMENT)
    parts = blocks // segment
    local_ids = (first_expert + jnp.arange(local_experts, dtype=jnp.int32))[:, None, None]
    mine = (chosen[None, :, 0] == local_ids) | (chosen[None, :, 1] == local_ids)
    before = jnp.arange(tok_count)[:, None] < jnp.arange(tok_count)[None, :]
    rank = jnp.einsum(
        "ebt,tu->ebu", mine.astype(BF), before.astype(BF), preferred_element_type=F32
    ).astype(jnp.int32)
    held = jnp.sum(mine.astype(jnp.int32), axis=2).reshape(local_experts, parts, segment)
    start = jnp.cumsum(held, axis=2) - held
    rank = rank.reshape(local_experts, parts, segment, tok_count)
    mine = mine.reshape(local_experts, parts, segment, tok_count)
    places = jnp.where(mine, rank + start[..., None], -WINDOW * segment)
    places = places.reshape(local_experts, parts, segment // 2, 2 * tok_count)
    meta = jnp.concatenate(
        [start[:, :, ::2], jnp.sum(held, axis=2, keepdims=True)], axis=2
    ).swapaxes(0, 1)
    meta = jnp.pad(meta, ((0, 0), (0, 1), (0, 0)))
    meta = meta.at[:, local_experts, 0].set(first_expert)
    pairs = chosen.reshape(parts, segment // 2, 2, 2, tok_count).swapaxes(2, 3)
    pairs = pairs.reshape(parts, segment // 2, 2, 2 * tok_count)
    rows = segment * tok_count
    d_w_experts = [
        far_weight_grads(
            meta[i],
            pairs[i],
            places[:, i],
            router_t,
            second_all[i * rows : (i + 1) * rows],
            grads_all[i * rows : (i + 1) * rows],
            w_experts,
        )
        for i in range(parts)
    ]
    d_w_experts = sum(d_w_experts[1:], d_w_experts[0])
    return (
        output[None],
        d_tokens[None],
        d_qkv_w,
        d_out_w,
        d_router_w,
        d_gain_attn,
        d_gain_moe,
        d_w_experts,
    )


def solution(mesh):
    placed = (
        P("fsdp", "ctx", None),
        P("fsdp", None),
        P("fsdp", None),
        P("fsdp", None),
        P("fsdp"),
        P("fsdp"),
        P("fsdp", None, None),
        P("fsdp", None),
        P("fsdp", "ctx", None),
        P("fsdp", "ctx", None),
    )
    return jax.shard_map(
        per_device,
        mesh=mesh,
        in_specs=placed,
        out_specs=(
            P("fsdp", "ctx", None),
            P("fsdp", "ctx", None),
            P("fsdp", None),
            P("fsdp", None),
            P("fsdp", None),
            P("fsdp"),
            P("fsdp"),
            P("fsdp", None, None),
        ),
        check_vma=False,
    )
```

time: 733 us -> 551 us (0.75)
  matrix products: 254 us -> 55.7 us
  Pallas kernels: 0 us -> 146 us
  waiting for transfers between devices: 232 us -> 166 us
  blocking collectives: 27.3 us -> 0 us
  local copies, waits for them, and re-layouts: 93.8 us -> 67.4 us
  other arithmetic: 76 us -> 50.5 us
  starting transfers between devices: 23.6 us -> 42.8 us
    all_gather x8 -> x4, waiting for transfers between devices: 209 us -> 0.04 us  [gathered(): return lax.all_gather(value, axis, axis=0, tiled=True)]
    dot_general x17 -> x1, matrix products: 205 us -> 1 us  [per_device(): jnp.einsum('ebt,tu->ebu', mine.astype(BF), before.astype(BF), preferred_e...]
    ppermute x0 -> x29, waiting for transfers between devices: none -> 147 us  [exchanged(): return lax.ppermute(value, axis, [(i, i ^ distance) for i in range(count)])]
    pallas_call x0 -> x2, Pallas kernels: none -> 146 us  [the longest x1 119 us: far_weight_grads(): pl.pallas_call(far_kernel, grid_spec=pltpu.PrefetchScalarGridSpec(num_sca...]
    concatenate x2 -> x3, other arithmetic: 29.5 us -> 2.81 us  [the longest x1 1.8 us: per_device(): sent = jnp.concatenate([cotangent[0], route_cols], axis=1)]
    ppermute x0 -> x29, starting transfers between devices: none -> 26.4 us  [exchanged(): return lax.ppermute(value, axis, [(i, i ^ distance) for i in range(count)])]
    transpose x9 -> x2, local copies, waits for them, and re-layouts: 21 us -> 1.36 us  [the longest x1 0.74 us: per_device(): router_t = jnp.pad(router_w.T, ((0, 16 - EXPERTS), (0, 0)))]
    all_to_all x1 -> x0, blocking collectives: 15.9 us -> none  [to_all(): return lax.all_to_all(value, axis, 0, 0, tiled=True)]
  transfers between devices with their start and end apart: 13 -> 36, of which waited for: 6 -> 11; matrix products, arithmetic and copies ran while one was open for 51% -> 27% of each run, Pallas kernels for 0% -> 27%
where the time goes in v2:
time: 551 us; the launch traced here: 544 us
  waiting for transfers between devices  166 us (30%)
  Pallas kernels  146 us (26%)
  local copies, waits for them, and re-layouts  67.4 us (12%)
  matrix products  55.7 us (10%)
  other arithmetic  50.5 us (9%)
  starting transfers between devices  42.8 us (8%)
  between operations  15.3 us (3%)
    ppermute x29, waiting for transfers between devices, exchanged(): return lax.ppermute(value, axis, [(i, i ^ distance) for i in range(count)])  147 us
    pallas_call x1, Pallas kernels, far_weight_grads(): pl.pallas_call(far_kernel, grid_spec=pltpu.PrefetchScalarGridSpec(num_sca...  119 us
    pallas_call x1, Pallas kernels, near_experts(): pl.pallas_call(functools.partial(near_kernel, shards), grid_spec=pltpu.Pr...  27.8 us
    ppermute x29, starting transfers between devices, exchanged(): return lax.ppermute(value, axis, [(i, i ^ distance) for i in range(count)])  26.4 us
    unnamed x121, local copies, waits for them, and re-layouts  22.5 us
    all_to_all x3, waiting for transfers between devices, to_all(): return lax.all_to_all(value, axis, 0, 0, tiled=True)  19.1 us
    dot_general x9, matrix products, dot_t(): lax.dot_general(a, b, (((1,), (1,)), ((), ())), preferred_element_type=F32)  16.8 us
    all_to_all x3, starting transfers between devices, to_all(): return lax.all_to_all(value, axis, 0, 0, tiled=True)  15.7 us
  transfers between devices with their start and end apart: 36, of which 11 were waited for; matrix products, arithmetic and copies ran while one was open for 27% of the time, Pallas kernels for 27%

profile of v2, /device:TPU:0, one launch (start us, length us, event | category | flops | bytes accessed | tf_op | source)
XLA Modules:
  0.0 544.4 jit_solution(14029197507977679298)
XLA Ops:
  8.1 1.8 fusion.46
  14.9 3.0 collective-permute-start.9
  18.0 3.7 collective-permute-start.3
  21.6 1.5 collective-permute-start
  24.6 1.6 fusion.13
  27.0 4.7 collective-permute-done
  33.1 3.5 collective-permute-start.7
  36.6 20.3 %collective-permute-done.2 = bf16[64,1536]{1,0:T(8,128)(2,1)S(1)} collective-permute-done((bf16[64,1536]{1,0:T(8,128)(2,1)S(1)}, bf16[64,1536]{1,0:T(8,128)(2,1)S(1)}, u32[]{:S(2)}, u32[]{:S(2)}) %collective-permute-start.2) | collective-permute-done | bytes 196640 | tf_op jit(solution)/shard_map/ppermute | solution.py:74
  56.9 3.0 collective-permute-start.5
  60.9 1.5 collective-permute-start.4
  64.7 1.5 slice_bitcast_fusion.1
  66.1 34.1 %collective-permute-done.6 = bf16[2,64,1536]{2,1,0:T(8,128)(2,1)} collective-permute-done((bf16[2,64,1536]{2,1,0:T(8,128)(2,1)}, bf16[2,64,1536]{2,1,0:T(8,128)(2,1)}, u32[]{:S(2)}, u32[]{:S(2)}) %collective-permute-start.6) | collective-permute-done | bytes 393248 | tf_op jit(solution)/shard_map/ppermute | solution.py:74
  107.9 2.8 gather_fusion
  110.6 1.6 multiply_reduce_fusion
  112.3 1.6 multiply_convert_fusion
  115.9 2.5 fusion.2
  118.4 4.4 fusion.8
  123.4 5.8 %fusion.88 = (bf16[1024,3,64]{0,2,1:T(8,128)(2,1)}, f32[1024,3,64]{0,2,1:T(8,128)}) fusion(f32[1024,1024,3]{1,0,2:T(8,128)S(1)} %get-tuple-element.140, f32[3,1024]{1,0:T(4,128)S(1)} %get-tuple-element.134, f32[3,1024]{1,0:T(4,128)S(1)} %get-tuple-element.139, pred[1024,1024]{0,1:T(8,128)(4,1)} %fusion.13, bf16[1024,320]{0,1:T(8,128)(2,1)} %copy-done.29), kind=kOutput, calls=%fused_computation.227 | convolution fusion | flops 418578432 | bytes 14966784 | tf_op jit(solution)/shard_map/gts,sd->tgd/dot_general | solution.py:436
  132.4 5.0 all-to-all-start
  138.1 19.7 %collective-permute-done.12 = bf16[384,1536]{1,0:T(8,128)(2,1)} collective-permute-done((bf16[384,1536]{1,0:T(8,128)(2,1)}, bf16[384,1536]{1,0:T(8,128)(2,1)}, u32[]{:S(2)}, u32[]{:S(2)}) %collective-permute-start.12) | collective-permute-done | bytes 1179680 | tf_op jit(solution)/shard_map/ppermute | solution.py:74
  159.2 1.7 fusion.90
  162.3 1.7 multiply_reduce_fusion.5
  167.5 51.5 %collective-permute-done.15.refs_2_ = bf16[128,1536]{1,0:T(8,128)(2,1)S(1)} collective-permute-done((bf16[128,1536]{1,0:T(8,128)(2,1)}, bf16[128,1536]{1,0:T(8,128)(2,1)S(1)}, u32[]{:S(2)}, u32[]{:S(2)}) %collective-permute-start.15) | collective-permute-done | bytes 393248 | tf_op jit(solution)/shard_map/ppermute | solution.py:74
  225.1 2.6 constant_dynamic-slice_fusion.2
  227.8 27.8 %near_experts.1 = (bf16[128,1536]{1,0:T(8,128)(2,1)}, bf16[128,1536]{1,0:T(8,128)(2,1)}, bf16[128,1536]{1,0:T(8,128)(2,1)}, bf16[128,1536]{1,0:T(8,128)(2,1)}, b...) custom-call(s32[1]{0:T(128)} %bitcast.47.shard_ref, ...), custom_call_target="tpu_custom_call" | custom-call | flops 9663676416 | bytes 18874368 | tf_op jit(solution)/shard_map/near_experts/pallas_call | solution.py:219
  260.7 1.5 collective-permute-start.19
  262.1 9.4 %collective-permute-done.22 = bf16[128,1664]{1,0:T(8,128)(2,1)S(1)} collective-permute-done((bf16[128,1664]{1,0:T(8,128)(2,1)S(1)}, bf16[128,1664]{1,0:T(8,128)(2,1)S(1)}, u32[]{:S(2)}, u32[]{:S(2)}) %collective-permute-start.22) | collective-permute-done | bytes 426016 | tf_op jit(solution)/shard_map/ppermute | solution.py:74
  273.1 1.8 multiply_reduce_fusion.2
  274.9 4.7 collective-permute-done.19
  279.6 2.5 fusion.81
  282.3 1.9 fusion.25
  284.2 1.8 fusion.28
  286.0 1.8 fusion.27
  290.4 5.6 %all-to-all-start.1 = ((bf16[8,128,384]{1,2,0:T(8,128)(2,1)}), bf16[8,128,384]{1,2,0:T(8,128)(2,1)}, u32[]{:S(2)}, u32[]{:S(2)}) async-start(bf16[8,128,384]{1,2,0:T(8,128)(2,1)} %pad_maximum_fusion.3), calls=%async_computation.1 | async-start | bytes 1572864 | tf_op jit(solution)/shard_map/all_to_all | solution.py:65
  297.3 4.2 copy.199
  303.4 4.1 copy.219
  307.5 1.7 copy.196
  311.3 19.1 %all-to-all-done.1 = bf16[8,128,384]{1,2,0:T(8,128)(2,1)} async-done(((bf16[8,128,384]{1,2,0:T(8,128)(2,1)}), bf16[8,128,384]{1,2,0:T(8,128)(2,1)}, u32[]{:S(2)}, u32[]{:S(2)}) %all-to-all-start.1) | async-done | bytes 786464 | tf_op jit(solution)/shard_map/all_to_all | solution.py:65
  330.4 2.3 copy.186
  332.7 2.0 slice.242
  334.7 2.0 copy.187
  336.7 1.4 multiply_reduce_fusion.3
  338.2 3.1 convolution_convert_fusion.1
  341.3 9.1 %fusion.1 = bf16[3,1024,1024]{1,2,0:T(8,128)(2,1)S(1)} fusion(f32[1024,1024,3]{1,0,2:T(8,128)} %copy-done, f32[3,1024]{1,0:T(4,128)S(1)} %bitcast.388, f32[3,1024]{1,0:T(4,128)S(1)} %copy-done.41, pred[1024,1024]{0,1:T(8,128)(4,1)S(1)} %copy-done.7, bf16[1024,3,64]{0,2,1:T(8,128)(2,1)} %bitcast.343, bf16[1024,320]{0,1:T(8,128)(2,1)} %copy-done.29), kind=kOutput, calls=%fused_computation.8 | convolution fusion | flops 421527552 | bytes 20471808 | tf_op jit(solution)/shard_map/tgd,sd->gts/dot_general | solution.py:448
  350.5 2.3 fusion.16
  352.8 2.4 fusion.21
  355.3 3.0 fusion.22
  358.3 2.1 convolution_convert_fusion
  360.5 4.1 concatenate.85
  367.9 1.9 add_convert_fusion.2
  369.8 1.5 collective-permute-start.28
  374.5 5.1 all-to-all-start.2
  379.6 1.9 collective-permute-done.28
  381.4 2.0 add_convert_fusion.1
  383.5 118.7 %far_weight_grads.1 = f32[2,1536,3072]{2,1,0:T(8,128)} custom-call(s32[3,17]{1,0:T(4,128)} %copy-done.46, s32[16,2,256]{2,1,0:T(2,128)} %squeeze_reshape.11.chosen, s32[2,16,256]{2,1,0:T(8,128)} %squeeze_reshape.12.places, bf16[16,1536]{1,0:T(8,128)(2,1)} %pad.16.refs_9_.router_t, bf16[4096,1536]{1,0:T(8,128)(2,1)} %all-gather.11.cloned.1.call-done.second_ref, ...), custom_call_target="tpu_custom_call" | custom-call | flops 77309411328 | bytes 106954752 | tf_op jit(solution)/shard_map/far_weight_grads/pallas_call | solution.py:388
  502.3 2.3 convolution_bitcast_fusion.4
  504.5 2.3 convolution_bitcast_fusion.2
  506.8 2.3 convolution_bitcast_fusion.3
  509.1 2.3 convolution_bitcast_fusion.1
  515.1 2.7 convert_element_type.256
  522.8 1.6 slice.248
  524.8 2.0 copy.205
  526.8 4.9 multiply_reduce_fusion.1
  532.2 5.4 %copy.204 = f32[384,2560]{1,0:T(8,128)} copy(f32[384,2560]{0,1:T(8,128)} %get-tuple-element.103) | data formatting | bytes 7864320
  (296 shorter events, 69.8 us)
Async XLA Ops:
  7.2 10.7 %copy-start.1 = (bf16[1,128,1536]{2,1,0:T(8,128)(2,1)S(1)}, bf16[1,128,1536]{2,1,0:T(8,128)(2,1)}, u32[]{:S(2)}) copy-start(bf16[1,128,1536]{2,1,0:T(8,128)(2,1)} %param.12) | copy-start | bytes 1179652
  7.2 16.6 %copy-start.50 = (s32[1,8]{1,0:T(1,128)S(1)}, s32[1,8]{1,0:T(1,128)}, u32[]{:S(2)}) copy-start(s32[1,8]{1,0:T(1,128)} %param.19) | copy-start | bytes 100
  7.2 214.5 %all-gather.5.cloned.1.call-start = ((), (), s32[]{:S(2)}) async-start(), calls=%async_computation.3 | async-start | bytes 14057472 | tf_op jit(solution)/shard_map/all_gather | solution.py:69
  9.9 293.5 %all-gather.7.cloned.1.call-start = ((), (), s32[]{:S(2)}) async-start(), calls=%async_computation.4 | async-start | bytes 3538944 | tf_op jit(solution)/shard_map/all_gather | solution.py:69
  14.9 17.5 %collective-permute-start.9 = (bf16[384,330]{1,0:T(8,128)(2,1)S(1)}, bf16[384,330]{1,0:T(8,128)(2,1)S(1)}, u32[]{:S(2)}, u32[]{:S(2)}) collective-permute-start(bf16[384,330]{1,0:T(8,128)(2,1)S(1)} %concatenate.75), channel_id=1, source_target_pairs={{0,2},{1,3},{2,0},{3,1},{4,6},{5,7},{6,4},{7,5},{8,10},{9,11},{10,... | collective-permute-start | bytes 760328 | tf_op jit(solution)/shard_map/ppermute | solution.py:74
  17.9 43.0 %collective-permute-start.8 = (bf16[384,330]{1,0:T(8,128)(2,1)S(1)}, bf16[384,330]{1,0:T(8,128)(2,1)S(1)}, u32[]{:S(2)}, u32[]{:S(2)}) collective-permute-start(bf16[384,330]{1,0:T(8,128)(2,1)S(1)} %concatenate.75), channel_id=1, source_target_pairs={{0,1},{1,0},{2,3},{3,2},{4,5},{5,4},{6,7},{7,6},{8,9},{9,8},{10,11... | collective-permute-start | bytes 760328 | tf_op jit(solution)/shard_map/ppermute | solution.py:74
  18.0 15.2 %collective-permute-start.3 = (bf16[64,1536]{1,0:T(8,128)(2,1)S(1)}, bf16[64,1536]{1,0:T(8,128)(2,1)S(1)}, u32[]{:S(2)}, u32[]{:S(2)}) collective-permute-start(bf16[64,1536]{1,0:T(8,128)(2,1)S(1)} %get-tuple-element.129), channel_id=1, source_target_pairs={{0,24},{4,28},{8,16},{12,20},{16,8},{20,12},{24,0},{28,4},{1,25},{... | collective-permute-start | bytes 589832 | tf_op jit(solution)/shard_map/ppermute | solution.py:74
  21.6 35.3 %collective-permute-start.2 = (bf16[64,1536]{1,0:T(8,128)(2,1)S(1)}, bf16[64,1536]{1,0:T(8,128)(2,1)S(1)}, u32[]{:S(2)}, u32[]{:S(2)}) collective-permute-start(bf16[64,1536]{1,0:T(8,128)(2,1)S(1)} %get-tuple-element.129), channel_id=1, source_target_pairs={{0,16},{4,20},{8,24},{12,28},{16,0},{20,4},{24,8},{28,12},{1,17},{... | collective-permute-start | bytes 589832 | tf_op jit(solution)/shard_map/ppermute | solution.py:74
  21.6 10.1 %collective-permute-start = (bf16[64,1536]{1,0:T(8,128)(2,1)S(1)}, bf16[64,1536]{1,0:T(8,128)(2,1)S(1)}, u32[]{:S(2)}, u32[]{:S(2)}) collective-permute-start(bf16[64,1536]{1,0:T(8,128)(2,1)S(1)} %get-tuple-element.128), channel_id=1, source_target_pairs={{0,4},{4,0},{8,12},{12,8},{16,20},{20,16},{24,28},{28,24},{1,5},{5... | collective-permute-start | bytes 589832 | tf_op jit(solution)/shard_map/ppermute | solution.py:74
  23.2 39.6 %copy-start.44 = (s32[1024]{0:T(1024)}, s32[1024]{0:T(1024)S(1)}, u32[]{:S(2)}) copy-start(s32[1024]{0:T(1024)S(1)} %pad_clamp_fusion.1) | copy-start | bytes 12292
  26.2 36.2 %copy-start.51 = (pred[8]{0:T(512)(128)(4,1)}, pred[8]{0:T(512)(128)(4,1)S(1)}, u32[]{:S(2)}) copy-start(pred[8]{0:T(512)(128)(4,1)S(1)} %compare_and_fusion.1) | copy-start | bytes 28
  31.7 30.7 %copy-start.25 = (bf16[64,1536]{1,0:T(8,128)(2,1)}, bf16[64,1536]{1,0:T(8,128)(2,1)S(1)}, u32[]{:S(2)}) copy-start(bf16[64,1536]{1,0:T(8,128)(2,1)S(1)} %collective-permute-done) | copy-start | bytes 589828
  31.7 25.2 %collective-permute-start.1 = (bf16[64,1536]{1,0:T(8,128)(2,1)S(1)}, bf16[64,1536]{1,0:T(8,128)(2,1)S(1)}, u32[]{:S(2)}, u32[]{:S(2)}) collective-permute-start(bf16[64,1536]{1,0:T(8,128)(2,1)S(1)} %get-tuple-element.129), channel_id=1, source_target_pairs={{0,8},{4,12},{8,0},{12,4},{16,24},{20,28},{24,16},{28,20},{1,9},{5... | collective-permute-start | bytes 589832 | tf_op jit(solution)/shard_map/ppermute | solution.py:74
  32.4 30.1 %collective-permute-start.10 = (bf16[384,330]{1,0:T(8,128)(2,1)S(1)}, bf16[384,330]{1,0:T(8,128)(2,1)S(1)}, u32[]{:S(2)}, u32[]{:S(2)}) collective-permute-start(bf16[384,330]{1,0:T(8,128)(2,1)S(1)} %collective-permute-done.9), channel_id=1, source_target_pairs={{0,1},{1,0},{2,3},{3,2},{4,5},{5,4},{6,7},{7,6},{8,9},{9,8},{10,11... | collective-permute-start | bytes 760328 | tf_op jit(solution)/shard_map/ppermute | solution.py:74
  33.1 29.3 %copy-start.19 = (bf16[64,1536]{1,0:T(8,128)(2,1)}, bf16[64,1536]{1,0:T(8,128)(2,1)S(1)}, u32[]{:S(2)}) copy-start(bf16[64,1536]{1,0:T(8,128)(2,1)S(1)} %collective-permute-done.3) | copy-start | bytes 589828
  33.1 31.5 %collective-permute-start.7 = (bf16[2,64,1536]{2,1,0:T(8,128)(2,1)}, bf16[2,64,1536]{2,1,0:T(8,128)(2,1)}, u32[]{:S(2)}, u32[]{:S(2)}) collective-permute-start(bf16[2,64,1536]{2,1,0:T(8,128)(2,1)} %pad_maximum_fusion.7), channel_id=1, source_target_pairs={{0,24},{4,28},{8,16},{12,20},{16,8},{20,12},{24,0},{28,4},{1,25},{... | collective-permute-start | bytes 1179656 | tf_op jit(solution)/shard_map/ppermute | solution.py:74
  56.9 5.5 %copy-start.21 = (bf16[64,1536]{1,0:T(8,128)(2,1)}, bf16[64,1536]{1,0:T(8,128)(2,1)S(1)}, u32[]{:S(2)}) copy-start(bf16[64,1536]{1,0:T(8,128)(2,1)S(1)} %collective-permute-done.2) | copy-start | bytes 589828
  56.9 43.3 %collective-permute-start.6 = (bf16[2,64,1536]{2,1,0:T(8,128)(2,1)}, bf16[2,64,1536]{2,1,0:T(8,128)(2,1)}, u32[]{:S(2)}, u32[]{:S(2)}) collective-permute-start(bf16[2,64,1536]{2,1,0:T(8,128)(2,1)} %pad_maximum_fusion.7), channel_id=1, source_target_pairs={{0,16},{4,20},{8,24},{12,28},{16,0},{20,4},{24,8},{28,12},{1,17},{... | collective-permute-start | bytes 1179656 | tf_op jit(solution)/shard_map/ppermute | solution.py:74
  56.9 5.5 %copy-start.23 = (bf16[64,1536]{1,0:T(8,128)(2,1)}, bf16[64,1536]{1,0:T(8,128)(2,1)S(1)}, u32[]{:S(2)}) copy-start(bf16[64,1536]{1,0:T(8,128)(2,1)S(1)} %collective-permute-done.1) | copy-start | bytes 589828
  56.9 44.3 %collective-permute-start.5 = (bf16[2,64,1536]{2,1,0:T(8,128)(2,1)}, bf16[2,64,1536]{2,1,0:T(8,128)(2,1)}, u32[]{:S(2)}, u32[]{:S(2)}) collective-permute-start(bf16[2,64,1536]{2,1,0:T(8,128)(2,1)} %pad_maximum_fusion.7), channel_id=1, source_target_pairs={{0,8},{4,12},{8,0},{12,4},{16,24},{20,28},{24,16},{28,20},{1,9},{5... | collective-permute-start | bytes 1179656 | tf_op jit(solution)/shard_map/ppermute | solution.py:74
  60.9 41.5 %collective-permute-start.4 = (bf16[4,64,1536]{2,1,0:T(8,128)(2,1)}, bf16[4,64,1536]{2,1,0:T(8,128)(2,1)S(1)}, u32[]{:S(2)}, u32[]{:S(2)}) collective-permute-start(bf16[4,64,1536]{2,1,0:T(8,128)(2,1)} %pad_maximum_fusion.2), channel_id=1, source_target_pairs={{0,4},{4,0},{8,12},{12,8},{16,20},{20,16},{24,28},{28,24},{1,5},{5... | collective-permute-start | bytes 2359304 | tf_op jit(solution)/shard_map/ppermute | solution.py:74
  64.5 38.0 %copy-start.26 = (bf16[64,1536]{1,0:T(8,128)(2,1)S(1)}, bf16[64,1536]{1,0:T(8,128)(2,1)}, u32[]{:S(2)}) copy-start(bf16[64,1536]{1,0:T(8,128)(2,1)} %copy-done.25) | copy-start | bytes 589828
  64.5 38.7 %copy-start.24 = (bf16[64,1536]{1,0:T(8,128)(2,1)S(1)}, bf16[64,1536]{1,0:T(8,128)(2,1)}, u32[]{:S(2)}) copy-start(bf16[64,1536]{1,0:T(8,128)(2,1)} %copy-done.23) | copy-start | bytes 589828
  64.6 40.2 %copy-start.17 = (bf16[1536,330]{0,1:T(8,128)(2,1)}, bf16[1536,330]{0,1:T(8,128)(2,1)S(1)}, u32[]{:S(2)}) copy-start(bf16[1536,330]{0,1:T(8,128)(2,1)S(1)} %broadcast_select_fusion) | copy-start | bytes 3041284
  64.6 40.1 %copy-start.22 = (bf16[64,1536]{1,0:T(8,128)(2,1)S(1)}, bf16[64,1536]{1,0:T(8,128)(2,1)}, u32[]{:S(2)}) copy-start(bf16[64,1536]{1,0:T(8,128)(2,1)} %copy-done.21) | copy-start | bytes 589828
  101.3 5.1 copy-start.20
  118.4 5.0 copy-start
  129.3 28.4 %collective-permute-start.12 = (bf16[384,1536]{1,0:T(8,128)(2,1)}, bf16[384,1536]{1,0:T(8,128)(2,1)}, u32[]{:S(2)}, u32[]{:S(2)}) collective-permute-start(bf16[384,1536]{1,0:T(8,128)(2,1)} %param.14), channel_id=1, source_target_pairs={{0,2},{1,3},{2,0},{3,1},{4,6},{5,7},{6,4},{7,5},{8,10},{9,11},{10,... | collective-permute-start | bytes 3538952 | tf_op jit(solution)/shard_map/ppermute | solution.py:74
  131.6 29.3 %copy-start.5 = (bf16[384,1536]{1,0:T(8,128)(2,1)S(1)}, bf16[384,1536]{1,0:T(8,128)(2,1)}, u32[]{:S(2)}) copy-start(bf16[384,1536]{1,0:T(8,128)(2,1)} %param.14) | copy-start | bytes 3538948
  132.4 25.3 %all-to-all-start = ((bf16[8,128,192]{1,2,0:T(8,128)(2,1)}), bf16[8,128,192]{1,2,0:T(8,128)(2,1)S(1)}, u32[]{:S(2)}, u32[]{:S(2)}) async-start(bf16[8,128,192]{1,2,0:T(8,128)(2,1)} %copy.173), calls=%async_computation | async-start | bytes 786432 | tf_op jit(solution)/shard_map/all_to_all | solution.py:65
  137.4 246.1 %all-gather.11.cloned.1.call-start = ((), (), s32[]{:S(2)}) async-start(), calls=%async_computation.6 | async-start | bytes 12976128 | tf_op jit(solution)/shard_map/all_gather | solution.py:69
  138.0 23.3 %collective-permute-start.11 = (bf16[384,1536]{1,0:T(8,128)(2,1)}, bf16[384,1536]{1,0:T(8,128)(2,1)S(1)}, u32[]{:S(2)}, u32[]{:S(2)}) collective-permute-start(bf16[384,1536]{1,0:T(8,128)(2,1)} %param.14), channel_id=1, source_target_pairs={{0,1},{1,0},{2,3},{3,2},{4,5},{5,4},{6,7},{7,6},{8,9},{9,8},{10,11... | collective-permute-start | bytes 3538952 | tf_op jit(solution)/shard_map/ppermute | solution.py:74
  157.7 4.2 collective-permute-start.13
  161.7 4.4 copy-start.28
  165.0 137.8 %collective-permute-start.24 = (bf16[384,2560]{1,0:T(8,128)(2,1)}, bf16[384,2560]{1,0:T(8,128)(2,1)}, u32[]{:S(2)}, u32[]{:S(2)}) collective-permute-start(bf16[384,2560]{1,0:T(8,128)(2,1)} %param.13), channel_id=1, source_target_pairs={{0,2},{1,3},{2,0},{3,1},{4,6},{5,7},{6,4},{7,5},{8,10},{9,11},{10,... | collective-permute-start | bytes 5898248 | tf_op jit(solution)/shard_map/ppermute | solution.py:74
  166.2 52.7 %collective-permute-start.15 = (bf16[128,1536]{1,0:T(8,128)(2,1)}, bf16[128,1536]{1,0:T(8,128)(2,1)S(1)}, u32[]{:S(2)}, u32[]{:S(2)}) collective-permute-start(bf16[128,1536]{1,0:T(8,128)(2,1)} %multiply_convert_fusion.1.refs_0_), channel_id=1, source_target_pairs={{0,2},{1,3},{2,0},{3,1},{4,6},{5,7},{6,4},{7,5},{8,10},{9,11},{10,... | collective-permute-start | bytes 1179656 | tf_op jit(solution)/shard_map/ppermute | solution.py:74
  167.4 54.2 %collective-permute-start.14 = (bf16[128,1536]{1,0:T(8,128)(2,1)}, bf16[128,1536]{1,0:T(8,128)(2,1)}, u32[]{:S(2)}, u32[]{:S(2)}) collective-permute-start(bf16[128,1536]{1,0:T(8,128)(2,1)} %multiply_convert_fusion.1.refs_0_), channel_id=1, source_target_pairs={{0,1},{1,0},{2,3},{3,2},{4,5},{5,4},{6,7},{7,6},{8,9},{9,8},{10,11... | collective-permute-start | bytes 1179656 | tf_op jit(solution)/shard_map/ppermute | solution.py:74
  218.9 2.7 collective-permute-start.16
  223.9 31.7 %copy-start.32 = (s32[32,128,2]{1,2,0:T(2,128)}, s32[32,128,2]{1,2,0:T(2,128)S(1)}, u32[]{:S(2)}) copy-start(s32[32,128,2]{1,2,0:T(2,128)S(1)} %copy.175) | copy-start | bytes 98308
  255.5 2.2 collective-permute-start.21
  256.5 18.4 %collective-permute-start.17 = (bf16[128,1536]{1,0:T(8,128)(2,1)}, bf16[128,1536]{1,0:T(8,128)(2,1)}, u32[]{:S(2)}, u32[]{:S(2)}) collective-permute-start(bf16[128,1536]{1,0:T(8,128)(2,1)} %get-tuple-element.39), channel_id=1, source_target_pairs={{0,1},{1,0},{2,3},{3,2},{4,5},{5,4},{6,7},{7,6},{8,9},{9,8},{10,11... | collective-permute-start | bytes 1179656 | tf_op jit(solution)/shard_map/ppermute | solution.py:74
  256.6 3.0 collective-permute-start.18
  257.1 5.1 collective-permute-start.20
  258.9 20.7 %copy-start.16 = (bf16[1,128,1536]{2,1,0:T(8,128)(2,1)S(1)}, bf16[1,128,1536]{2,1,0:T(8,128)(2,1)}, u32[]{:S(2)}) copy-start(bf16[1,128,1536]{2,1,0:T(8,128)(2,1)} %param.21) | copy-start | bytes 1179652
  258.9 20.7 %copy-start.31 = (bf16[128,1536]{1,0:T(8,128)(2,1)S(1)}, bf16[128,1536]{1,0:T(8,128)(2,1)}, u32[]{:S(2)}) copy-start(bf16[128,1536]{1,0:T(8,128)(2,1)} %get-tuple-element.38) | copy-start | bytes 1179652
  258.9 12.7 %collective-permute-start.22 = (bf16[128,1664]{1,0:T(8,128)(2,1)S(1)}, bf16[128,1664]{1,0:T(8,128)(2,1)S(1)}, u32[]{:S(2)}, u32[]{:S(2)}) collective-permute-start(bf16[128,1664]{1,0:T(8,128)(2,1)S(1)} %add_convert_fusion), channel_id=1, source_target_pairs={{0,2},{1,3},{2,0},{3,1},{4,6},{5,7},{6,4},{7,5},{8,10},{9,11},{10,... | collective-permute-start | bytes 1277960 | tf_op jit(solution)/shard_map/ppermute | solution.py:74
  260.7 18.9 %collective-permute-start.19 = (bf16[128,1536]{1,0:T(8,128)(2,1)S(1)}, bf16[128,1536]{1,0:T(8,128)(2,1)}, u32[]{:S(2)}, u32[]{:S(2)}) collective-permute-start(bf16[128,1536]{1,0:T(8,128)(2,1)S(1)} %add_convert_fusion.4), channel_id=1, source_target_pairs={{0,2},{1,3},{2,0},{3,1},{4,6},{5,7},{6,4},{7,5},{8,10},{9,11},{10,... | collective-permute-start | bytes 1179656 | tf_op jit(solution)/shard_map/ppermute | solution.py:74
  273.1 9.0 %copy-start.34 = (bf16[128,8]{1,0:T(8,128)(2,1)}, bf16[128,8]{1,0:T(8,128)(2,1)S(1)}, u32[]{:S(2)}) copy-start(bf16[128,8]{1,0:T(8,128)(2,1)S(1)} %copy.183) | copy-start | bytes 6148
  282.1 5.7 %copy-start.4 = (bf16[384,1536]{1,0:T(8,128)(2,1)S(1)}, bf16[384,1536]{1,0:T(8,128)(2,1)}, u32[]{:S(2)}) copy-start(bf16[384,1536]{1,0:T(8,128)(2,1)} %copy-done.3) | copy-start | bytes 3538948
  290.4 39.9 %all-to-all-start.1 = ((bf16[8,128,384]{1,2,0:T(8,128)(2,1)}), bf16[8,128,384]{1,2,0:T(8,128)(2,1)}, u32[]{:S(2)}, u32[]{:S(2)}) async-start(bf16[8,128,384]{1,2,0:T(8,128)(2,1)} %pad_maximum_fusion.3), calls=%async_computation.1 | async-start | bytes 1572864 | tf_op jit(solution)/shard_map/all_to_all | solution.py:65
  296.1 210.7 %collective-permute-start.23 = (bf16[384,2560]{1,0:T(8,128)(2,1)}, bf16[384,2560]{1,0:T(8,128)(2,1)}, u32[]{:S(2)}, u32[]{:S(2)}) collective-permute-start(bf16[384,2560]{1,0:T(8,128)(2,1)} %param.13), channel_id=1, source_target_pairs={{0,1},{1,0},{2,3},{3,2},{4,5},{5,4},{6,7},{7,6},{8,9},{9,8},{10,11... | collective-permute-start | bytes 5898248 | tf_op jit(solution)/shard_map/ppermute | solution.py:74
  302.8 206.3 %collective-permute-start.25 = (bf16[384,2560]{1,0:T(8,128)(2,1)}, bf16[384,2560]{1,0:T(8,128)(2,1)}, u32[]{:S(2)}, u32[]{:S(2)}) collective-permute-start(bf16[384,2560]{1,0:T(8,128)(2,1)} %collective-permute-done.24), channel_id=1, source_target_pairs={{0,1},{1,0},{2,3},{3,2},{4,5},{5,4},{6,7},{7,6},{8,9},{9,8},{10,11... | collective-permute-start | bytes 5898248 | tf_op jit(solution)/shard_map/ppermute | solution.py:74
  336.7 4.6 copy-start.7
  336.7 4.6 copy-start.41
  341.3 13.9 %slice-start = ((s8[12582912]{0:T(1024)(128)(4,1)}), s8[4194304]{0:T(1024)(128)(4,1)S(1)}, s32[]{:S(2)}) async-start(s8[12582912]{0:T(1024)(128)(4,1)} %bitcast.325), calls=%async_computation.7 | async-start | bytes 8388608
  341.3 13.9 %slice-start.1 = ((s8[12582912]{0:T(1024)(128)(4,1)}), s8[4194304]{0:T(1024)(128)(4,1)S(1)}, s32[]{:S(2)}) async-start(s8[12582912]{0:T(1024)(128)(4,1)} %bitcast.325), calls=%async_computation.8 | async-start | bytes 8388608
  350.5 4.8 slice-start.2
  364.5 9.0 %copy-start.37 = (bf16[1024,64]{0,1:T(8,128)(2,1)S(1)}, bf16[1024,64]{0,1:T(8,128)(2,1)}, u32[]{:S(2)}) copy-start(bf16[1024,64]{0,1:T(8,128)(2,1)} %copy-done.36) | copy-start | bytes 393220
  364.6 3.3 collective-permute-start.27
  367.4 12.2 %collective-permute-start.26 = (bf16[384,528]{0,1:T(8,128)(2,1)S(1)}, bf16[384,528]{0,1:T(8,128)(2,1)}, u32[]{:S(2)}, u32[]{:S(2)}) collective-permute-start(bf16[384,528]{0,1:T(8,128)(2,1)S(1)} %get-tuple-element.108), channel_id=1, source_target_pairs={{0,1},{1,0},{2,3},{3,2},{4,5},{5,4},{6,7},{7,6},{8,9},{9,8},{10,11... | collective-permute-start | bytes 1216520 | tf_op jit(solution)/shard_map/ppermute | solution.py:74
  369.8 11.6 %collective-permute-start.28 = (bf16[384,528]{0,1:T(8,128)(2,1)}, bf16[384,528]{0,1:T(8,128)(2,1)}, u32[]{:S(2)}, u32[]{:S(2)}) collective-permute-start(bf16[384,528]{0,1:T(8,128)(2,1)} %add_convert_fusion.2), channel_id=1, source_target_pairs={{0,2},{1,3},{2,0},{3,1},{4,6},{5,7},{6,4},{7,5},{8,10},{9,11},{10,... | collective-permute-start | bytes 1216520 | tf_op jit(solution)/shard_map/ppermute | solution.py:74
  374.5 127.7 %all-to-all-start.2 = ((bf16[8,128,320]{1,2,0:T(8,128)(2,1)}), bf16[8,128,320]{1,2,0:T(8,128)(2,1)S(1)}, u32[]{:S(2)}, u32[]{:S(2)}) async-start(bf16[8,128,320]{1,2,0:T(8,128)(2,1)} %pad_maximum_fusion.5), calls=%async_computation.2 | async-start | bytes 1310720 | tf_op jit(solution)/shard_map/all_to_all | solution.py:65
  379.5 135.6 %all-gather.9.cloned.1.call-start = ((), (), s32[]{:S(2)}) async-start(), calls=%async_computation.5 | async-start | bytes 3649536 | tf_op jit(solution)/shard_map/all_gather | solution.py:69
  526.8 4.9 copy-start.45
  (27 other events, 63.8 us)
Sparse Core Ops, SparseCore 0:
  10.9 150.6 all-gather.4
  164.4 57.9 all-gather.6
  225.3 109.1 all-gather.10
  383.6 64.8 all-gather.8

commit v3 on v2

--- a/solution.py
+++ b/solution.py
@@ -20,9 +20,10 @@
 SMALL = 16
 LANES = 128
 TILE = 256
-CHUNK = 512
-WINDOW = 2 * CAP + 16
+CHUNK = 256
 SEGMENT = 32
+JOINED = 2
+DEPTHS = (1, 2, 3, 4, 6, 8)
 
 NORM_EPS = 1e-05
 MASK_NEG = -1e30
@@ -100,18 +101,29 @@
     return jnp.take(stacked, jnp.arange(len(blocks), dtype=jnp.int32) ^ own, axis=0)
 
 
+def line_blocks(own):
+    spans = lax.axis_size("ctx")
+    return jnp.stack([own] + [exchanged(own, "ctx", d) for d in range(2, spans, 2)])
+
+
 def span_blocks(own):
-    spans = lax.axis_size("ctx")
     half = own.shape[0] // 2
-    first, last = own[:half], own[half:]
-    pair = jnp.stack([first, exchanged(first, "ctx", 1)])
-    firsts = [pair] + [exchanged(pair, "ctx", d) for d in range(2, spans, 2)]
-    lasts = jnp.stack([last] + [exchanged(last, "ctx", d) for d in range(2, spans, 2)])
-    other = exchanged(lasts, "ctx", 1)
+    same = [line_blocks(part) for part in (own[:half], own[half:])]
+    other = [exchanged(part, "ctx", 1) for part in same]
     return [
-        jnp.concatenate([firsts[r // 2][r % 2], (other if r % 2 else lasts)[r // 2]])
-        for r in range(spans)
+        jnp.concatenate([part[r // 2] for part in (other if r % 2 else same)])
+        for r in range(lax.axis_size("ctx"))
     ]
+
+
+def all_blocks(line):
+    spans, shards = lax.axis_size("ctx"), lax.axis_size("fsdp")
+    sets = [
+        [(2 * pair + side) * shards + f for side in range(2) for f in range(shards)]
+        for pair in range(spans // 2)
+    ]
+    merged = lax.all_gather(line, ("ctx", "fsdp"), axis=0, tiled=True, axis_index_groups=sets)
+    return merged.reshape(-1, line.shape[-1])
 
 
 def picked_gates(second, router_t, chosen):
@@ -270,6 +282,7 @@
     fetch_sem,
     store_sem,
 ):
+    experts = rows.shape[0]
     expert, tile = pl.program_id(0), pl.program_id(1)
     tiles = pl.num_programs(1)
     step = expert * tiles + tile
@@ -277,9 +290,12 @@
     groups = chosen.shape[0]
     size = chosen.shape[2]
     width = w_gate.shape[1]
-    wanted = meta[pl.num_programs(0), 0] + expert
-    count = meta[expert, groups]
-    chunks = jnp.maximum((count + CHUNK - 1) // CHUNK, 1)
+    window = JOINED * CAP + 16
+
+    def count_chunks(e):
+        return jnp.maximum((meta[e, groups] + CHUNK - 1) // CHUNK, 1)
+
+    chunks = count_chunks(expert)
 
     def stores(which, e, j):
         return [
@@ -300,13 +316,14 @@
             for i, ref in enumerate((second_ref, grads_ref))
         ]
 
-    @pl.when(tile == 0)
+    @pl.when(step == 0)
     def _():
         for copy in fetches(0, 0):
             copy.start()
-        tail = pl.ds(pl.multiple_of((chunks - 1) * CHUNK, CHUNK), CHUNK)
-        rows[tail, :] = jnp.zeros((CHUNK, width), BF)
-        d_outs[tail, :] = jnp.zeros((CHUNK, width), BF)
+        for e in range(experts):
+            tail = pl.ds(pl.multiple_of((count_chunks(e) - 1) * CHUNK, CHUNK), CHUNK)
+            rows[e, tail, :] = jnp.zeros((CHUNK, width), BF)
+            d_outs[e, tail, :] = jnp.zeros((CHUNK, width), BF)
 
         @pl.loop(0, groups)
         def _(g):
@@ -321,28 +338,35 @@
 
             second, grads = fetched[which, 0], fetched[which, 1]
             picked, gates = picked_gates(second, router_t[...], chosen[g])
-            found = (iota(gates.shape, 0) == wanted) & picked
-            gate = jnp.sum(jnp.where(found, gates, 0.0), axis=0, keepdims=True)
-            start = meta[expert, g]
-            base = start // 16 * 16
-            match = iota((WINDOW, size), 0) == places[expert, pl.ds(g, 1), :] - base
-            one_hot = match.astype(BF)
-            found_gate = jnp.sum(jnp.where(match, gate, 0.0), axis=1, keepdims=True)
-            at = pl.ds(pl.multiple_of(base, 16), 16)
-            rest = pl.ds(pl.multiple_of(base + 16, 16), WINDOW - 16)
-            held = iota((16, width), 0) < start - base
-            for ref, new in (
-                (rows, dot(one_hot, second).astype(BF)),
-                (d_outs, (found_gate * dot(one_hot, grads)).astype(BF)),
-            ):
-                ref[at, :] = jnp.where(held, ref[at, :], new[:16])
-                ref[rest, :] = new[16:]
+            starts = [meta[e, g] for e in range(experts)]
+            bases = [start // 16 * 16 for start in starts]
+            matches, found_gates = [], []
+            for e in range(experts):
+                found = (iota(gates.shape, 0) == meta[experts, 0] + e) & picked
+                gate = jnp.sum(jnp.where(found, gates, 0.0), axis=0, keepdims=True)
+                match = iota((window, size), 0) == places[e, pl.ds(g, 1), :] - bases[e]
+                matches.append(match.astype(BF))
+                found_gates.append(
+                    jnp.sum(jnp.where(match, gate, 0.0), axis=1, keepdims=True)
+                )
+            one_hot = jnp.concatenate(matches, axis=0)
+            new_rows = dot(one_hot, second).astype(BF)
+            new_grads = (jnp.concatenate(found_gates, axis=0) * dot(one_hot, grads)).astype(BF)
+            for e in range(experts):
+                at = pl.ds(pl.multiple_of(bases[e], 16), 16)
+                rest = pl.ds(pl.multiple_of(bases[e] + 16, 16), window - 16)
+                held = iota((16, width), 0) < starts[e] - bases[e]
+                for ref, new in ((rows, new_rows), (d_outs, new_grads)):
+                    new = new[e * window : (e + 1) * window]
+                    ref[e, at, :] = jnp.where(held, ref[e, at, :], new[:16])
+                    ref[e, rest, :] = new[16:]
 
     @pl.loop(0, chunks)
     def _(i):
         at = pl.ds(pl.multiple_of(i * CHUNK, CHUNK), CHUNK)
+        row, d_out = rows[expert, at, :], d_outs[expert, at, :]
         hidden, d_gate, d_up = swiglu_grads(
-            dot(rows[at, :], w_gate[0]), dot(rows[at, :], w_up[0]), dot(d_outs[at, :], w_down[0])
+            dot(row, w_gate[0]), dot(row, w_up[0]), dot(d_out, w_down[0])
         )
         act[0, at, :] = d_gate
         act[1, at, :] = d_up
@@ -353,14 +377,26 @@
         for copy in stores(slot, (step - 2) // tiles, lax.rem(step - 2, tiles)):
             copy.wait()
 
-    for k in range(1, act.shape[1] // CHUNK + 1):
-
-        @pl.when(chunks == k)
+    most = act.shape[1] // CHUNK
+    depths = [k for k in DEPTHS if k < most] + [most]
+    for low, k in zip([0] + depths[:-1], depths):
+
+        @pl.when((chunks > low) & (chunks <= k))
         def _():
+            for extra in range(low + 1, k):
+
+                @pl.when(chunks == extra)
+                def _():
+                    spare = slice(extra * CHUNK, k * CHUNK)
+                    empty = jnp.zeros(((k - extra) * CHUNK, width), BF)
+                    rows[expert, spare, :] = empty
+                    d_outs[expert, spare, :] = empty
+                    for i in range(3):
+                        act[i, spare, :] = empty[:, :TILE]
+
             upto = k * CHUNK
-            tile_out[slot, 0] = t_dot(rows[:upto, :], act[0, :upto, :])
-            tile_out[slot, 1] = t_dot(rows[:upto, :], act[1, :upto, :])
-            tile_out[slot, 2] = t_dot(d_outs[:upto, :], act[2, :upto, :])
+            for i, left in enumerate((rows, rows, d_outs)):
+                tile_out[slot, i] = t_dot(left[expert, :upto, :], act[i, :upto, :])
 
     for copy in stores(slot, expert, tile):
         copy.start()
@@ -377,7 +413,8 @@
     experts, width = w_experts.shape[:2]
     groups, _, size = chosen.shape
     tiles = FF // TILE
-    most = groups * size // 2
+    most = groups * JOINED * CAP
+    held = most + JOINED * CAP + 16
 
     def whole(shape):
         return pl.BlockSpec(shape, lambda e, j, s: (0,) * len(shape))
@@ -385,6 +422,7 @@
     def weight(part):
         return pl.BlockSpec((1, width, TILE), lambda e, j, s: (e, 0, part * tiles + j))
 
+    anywhere = pl.BlockSpec(memory_space=pl.ANY)
     return pl.pallas_call(
         far_kernel,
         grid_spec=pltpu.PrefetchScalarGridSpec(
@@ -394,16 +432,16 @@
                 whole(chosen.shape),
                 whole(places.shape),
                 whole(router_t.shape),
-                pl.BlockSpec(memory_space=pl.ANY),
-                pl.BlockSpec(memory_space=pl.ANY),
+                anywhere,
+                anywhere,
                 weight(0),
                 weight(1),
                 weight(2),
             ],
-            out_specs=pl.BlockSpec(memory_space=pl.ANY),
+            out_specs=anywhere,
             scratch_shapes=[
-                pltpu.VMEM((most + WINDOW, width), BF),
-                pltpu.VMEM((most + WINDOW, width), BF),
+                pltpu.VMEM((experts, held, width), BF),
+                pltpu.VMEM((experts, held, width), BF),
                 pltpu.VMEM((3, most, TILE), BF),
                 pltpu.VMEM((2, 2, size, width), BF),
                 pltpu.VMEM((2, 3, width, TILE), F32),
@@ -412,10 +450,10 @@
             ],
         ),
         out_shape=jax.ShapeDtypeStruct((experts, width, 3 * FF), F32),
-        compiler_params=pltpu.CompilerParams(vmem_limit_bytes=56 * 1024 * 1024),
+        compiler_params=pltpu.CompilerParams(vmem_limit_bytes=58 * 1024 * 1024),
         cost_estimate=pl.CostEstimate(
-            flops=12 * experts * most * width * FF,
-            bytes_accessed=w_experts.size * 6 + 4 * experts * groups * size * width,
+            flops=8 * experts * most * width * FF,
+            bytes_accessed=w_experts.size * 6 + 4 * groups * size * width,
             transcendentals=experts * most * FF,
         ),
         name="far_weight_grads",
@@ -475,12 +513,10 @@
     head = here // copies
     length = spans * tok_count
     blocks = spans * shards
-    everyone = ("ctx", "fsdp")
     first_expert = shard * local_experts
 
     route_cols = jnp.pad(routes[0].astype(BF), ((0, 0), (0, LANES - 2)))
     sent = jnp.concatenate([cotangent[0], route_cols], axis=1)
-    grads_all = gathered(sent, everyone)
 
     shard_rows = query_key_value_weight.shape[0]
     head_w = jnp.concatenate(
@@ -502,8 +538,10 @@
     head_w = head_w[:, :HEAD_COLS]
 
     stream = in_order(span_blocks(tokens[0]), here).reshape(length, width)
+    sent, output_weight, stream = lax.optimization_barrier((sent, output_weight, stream))
     out_w = near_blocks(output_weight)
-    qkv_w = near_blocks(query_key_value_weight)
+    grads_near = near_blocks(sent)
+    grads_all = all_blocks(line_blocks(sent))
     stream_f = stream.astype(F32)
     normed = (stream_f * rms_factor(stream_f) * attn_g).astype(BF)
     mixed = dot(normed, head_w).astype(BF)
@@ -529,16 +567,18 @@
     second_factor = rms_factor(middle)
     second = (middle * second_factor * moe_g).astype(BF)
     second_near = near_blocks(second)
-    second_all = gathered(second, everyone)
-
-    grads_all, second_near = lax.optimization_barrier((grads_all, second_near))
-    chosen = grads_all[:, width : width + 2].astype(jnp.int32).reshape(blocks, tok_count, 2)
-    chosen = chosen.swapaxes(1, 2)
-    chosen_near = jnp.take(chosen, here * shards + by_shard, axis=0)
-    grads_near = [
-        lax.dynamic_slice_in_dim(grads_all, (here * shards + (shard ^ r)) * tok_count, tok_count, 0)
-        for r in range(shards)
-    ]
+    second_line = line_blocks(second)
+    second_all = all_blocks(second_line)
+    attended_low, later_qkv, second_near, second_line = lax.optimization_barrier(
+        (attended_low, query_key_value_weight, second_near, second_line)
+    )
+    qkv_w = near_blocks(later_qkv)
+    attended_all = span_blocks(attended_low)
+
+    def routes_of(payload):
+        return payload[:, width : width + 2].astype(jnp.int32).reshape(-1, tok_count, 2).swapaxes(1, 2)
+
+    chosen_near = jnp.concatenate([routes_of(block) for block in grads_near])
     branch, back = near_experts(
         second_near, grads_near, chosen_near, router_t, w_experts, shard
     )
@@ -571,11 +611,9 @@
     d_mixed = attention_backward(
         q, k, v, allowed, log_norm, attended, sent[:, : GROUP * HD]
     )
-    attended_all = gathered(attended_low, "ctx").reshape(HK, copies, length, GROUP * HD)
-    attended_all = jnp.sum(attended_all, axis=1) if copies > 1 else attended_all[:, 0]
-    d_out_w = jnp.einsum(
-        "hte,td->hed", attended_all, sent[:, GROUP * HD :], preferred_element_type=F32
-    ).reshape(Q_COLS, chunk)
+    d_out_w = in_order([t_dot(block, sent[:, GROUP * HD :]) for block in attended_all], here)
+    d_out_w = jnp.sum(d_out_w.reshape(HK, copies, GROUP * HD, chunk), axis=1)
+    d_out_w = d_out_w.reshape(Q_COLS, chunk)
     small = jnp.concatenate(
         [d_router, d_gain_moe[:, None], jnp.zeros((width, SMALL - EXPERTS - 1), F32)], axis=1
     )
@@ -628,41 +666,38 @@
     d_normed = d_normed.swapaxes(0, 1).reshape(tok_count, width)
     d_tokens = (d_middle + rms_input_grad(x, rms_factor(x), attn_g, d_normed)).astype(BF)
 
+    chosen = routes_of(grads_all)
     segment = min(blocks, SEGMENT)
-    parts = blocks // segment
+    groups = segment // JOINED
     local_ids = (first_expert + jnp.arange(local_experts, dtype=jnp.int32))[:, None, None]
-    mine = (chosen[None, :, 0] == local_ids) | (chosen[None, :, 1] == local_ids)
     before = jnp.arange(tok_count)[:, None] < jnp.arange(tok_count)[None, :]
-    rank = jnp.einsum(
-        "ebt,tu->ebu", mine.astype(BF), before.astype(BF), preferred_element_type=F32
-    ).astype(jnp.int32)
-    held = jnp.sum(mine.astype(jnp.int32), axis=2).reshape(local_experts, parts, segment)
-    start = jnp.cumsum(held, axis=2) - held
-    rank = rank.reshape(local_experts, parts, segment, tok_count)
-    mine = mine.reshape(local_experts, parts, segment, tok_count)
-    places = jnp.where(mine, rank + start[..., None], -WINDOW * segment)
-    places = places.reshape(local_experts, parts, segment // 2, 2 * tok_count)
-    meta = jnp.concatenate(
-        [start[:, :, ::2], jnp.sum(held, axis=2, keepdims=True)], axis=2
-    ).swapaxes(0, 1)
-    meta = jnp.pad(meta, ((0, 0), (0, 1), (0, 0)))
-    meta = meta.at[:, local_experts, 0].set(first_expert)
-    pairs = chosen.reshape(parts, segment // 2, 2, 2, tok_count).swapaxes(2, 3)
-    pairs = pairs.reshape(parts, segment // 2, 2, 2 * tok_count)
-    rows = segment * tok_count
-    d_w_experts = [
-        far_weight_grads(
-            meta[i],
-            pairs[i],
-            places[:, i],
-            router_t,
-            second_all[i * rows : (i + 1) * rows],
-            grads_all[i * rows : (i + 1) * rows],
-            w_experts,
+    parts = []
+    for j in range(blocks // segment):
+        inside = slice(j * segment, (j + 1) * segment)
+        part = chosen[inside]
+        mine = (part[None, :, 0] == local_ids) | (part[None, :, 1] == local_ids)
+        rank = jnp.einsum(
+            "ebt,tu->ebu", mine.astype(BF), before.astype(BF), preferred_element_type=F32
+        ).astype(jnp.int32)
+        held = jnp.sum(mine.astype(jnp.int32), axis=2)
+        start = jnp.cumsum(held, axis=1) - held
+        places = jnp.where(mine, rank + start[..., None], -(2**20))
+        meta = jnp.concatenate([start[:, ::JOINED], jnp.sum(held, axis=1, keepdims=True)], axis=1)
+        meta = jnp.pad(meta, ((0, 1), (0, 0))).at[local_experts, 0].set(first_expert)
+        part = part.reshape(groups, JOINED, 2, tok_count).swapaxes(1, 2)
+        tokens_in = slice(j * segment * tok_count, (j + 1) * segment * tok_count)
+        parts.append(
+            far_weight_grads(
+                meta,
+                part.reshape(groups, 2, JOINED * tok_count),
+                places.reshape(local_experts, groups, JOINED * tok_count),
+                router_t,
+                second_all[tokens_in],
+                grads_all[tokens_in],
+                w_experts,
+            )
         )
-        for i in range(parts)
-    ]
-    d_w_experts = sum(d_w_experts[1:], d_w_experts[0])
+    d_w_experts = sum(parts[1:], parts[0])
     return (
         output[None],
         d_tokens[None],

time: 551 us -> 767 us (1.39)
  waiting for transfers between devices: 166 us -> 287 us
  local copies, waits for them, and re-layouts: 67.4 us -> 125 us
  Pallas kernels: 146 us -> 118 us
  starting transfers between devices: 42.8 us -> 68.1 us
  matrix products: 55.7 us -> 77.5 us
  other arithmetic: 50.5 us -> 65.7 us
    ppermute x29 -> x46, waiting for transfers between devices: 147 us -> 222 us  [exchanged(): return lax.ppermute(value, axis, [(i, i ^ distance) for i in range(count)])]
    all_gather x0 -> x2, waiting for transfers between devices: none -> 61.7 us  [all_blocks(): lax.all_gather(line, ('ctx', 'fsdp'), axis=0, tiled=True, axis_index_grou...]
    pallas_call x1, Pallas kernels: 119 us -> 89.7 us  [far_weight_grads(): pl.pallas_call(far_kernel, grid_spec=pltpu.PrefetchScalarGridSpec(num_sca...]
    ppermute x29 -> x46, starting transfers between devices: 26.4 us -> 46 us  [exchanged(): return lax.ppermute(value, axis, [(i, i ^ distance) for i in range(count)])]
    dot_general x2 -> x10, matrix products: 2.95 us -> 22.5 us  [t_dot(): lax.dot_general(a, b, (((0,), (0,)), ((), ())), preferred_element_type=F32)]
    all_to_all x3, waiting for transfers between devices: 19.1 us -> 3.96 us  [to_all(): return lax.all_to_all(value, axis, 0, 0, tiled=True)]
    gather x6 -> x8, local copies, waits for them, and re-layouts: 6.31 us -> 18.9 us  [in_order(): jnp.take(stacked, jnp.arange(len(blocks), dtype=jnp.int32) ^ own, axis=0)]
    pallas_call x0 -> x8, local copies, waits for them, and re-layouts: none -> 10.7 us  [near_experts(): pl.pallas_call(functools.partial(near_kernel, shards), grid_spec=pltpu.Pr...]
  transfers between devices with their start and end apart: 36 -> 52, of which waited for: 11 -> 18; matrix products, arithmetic and copies ran while one was open for 27% -> 23% of each run, Pallas kernels for 27% -> 0%
where the time goes in v3:
time: 767 us; the launch traced here: 757 us
  waiting for transfers between devices  287 us (37%)
  local copies, waits for them, and re-layouts  125 us (16%)
  Pallas kernels  118 us (15%)
  matrix products  77.5 us (10%)
  starting transfers between devices  68.1 us (9%)
  other arithmetic  65.7 us (9%)
  between operations  15.2 us (2%)
    ppermute x46, waiting for transfers between devices, exchanged(): return lax.ppermute(value, axis, [(i, i ^ distance) for i in range(count)])  222 us
    pallas_call x1, Pallas kernels, far_weight_grads(): pl.pallas_call(far_kernel, grid_spec=pltpu.PrefetchScalarGridSpec(num_sca...  89.7 us
    all_gather x2, waiting for transfers between devices, all_blocks(): lax.all_gather(line, ('ctx', 'fsdp'), axis=0, tiled=True, axis_index_grou...  61.7 us
    ppermute x46, starting transfers between devices, exchanged(): return lax.ppermute(value, axis, [(i, i ^ distance) for i in range(count)])  46 us
    pallas_call x1, Pallas kernels, near_experts(): pl.pallas_call(functools.partial(near_kernel, shards), grid_spec=pltpu.Pr...  28.1 us
    unnamed x153, local copies, waits for them, and re-layouts  23.2 us
    dot_general x10, matrix products, t_dot(): lax.dot_general(a, b, (((0,), (0,)), ((), ())), preferred_element_type=F32)  22.5 us
    all_to_all x3, starting transfers between devices, to_all(): return lax.all_to_all(value, axis, 0, 0, tiled=True)  22 us
  transfers between devices with their start and end apart: 52, of which 18 were waited for; matrix products, arithmetic and copies ran while one was open for 23% of the time, Pallas kernels for 0%

profile of v3, /device:TPU:0, one launch (start us, length us, event | category | flops | bytes accessed | tf_op | source)
XLA Modules:
  0.0 756.8 jit_solution(12785140802479682548)
XLA Ops:
  12.2 3.0 collective-permute-start.9
  16.3 3.7 collective-permute-start.2
  26.0 3.6 collective-permute-start.6
  29.6 12.3 %collective-permute-done.1 = bf16[64,1536]{1,0:T(8,128)(2,1)S(1)} collective-permute-done((bf16[64,1536]{1,0:T(8,128)(2,1)S(1)}, bf16[64,1536]{1,0:T(8,128)(2,1)S(1)}, u32[]{:S(2)}, u32[]{:S(2)}) %collective-permute-start.1) | collective-permute-done | bytes 196640 | tf_op jit(solution)/shard_map/ppermute | solution.py:75
  42.0 3.0 collective-permute-start.4
  47.5 6.7 collective-permute-done.5
  62.4 4.3 collective-permute-done.3
  67.9 15.2 %collective-permute-done.7 = bf16[4,64,1536]{2,1,0:T(8,128)(2,1)} collective-permute-done((bf16[4,64,1536]{2,1,0:T(8,128)(2,1)}, bf16[4,64,1536]{2,1,0:T(8,128)(2,1)}, u32[]{:S(2)}, u32[]{:S(2)}) %collective-permute-start.7) | collective-permute-done | bytes 786464 | tf_op jit(solution)/shard_map/ppermute | solution.py:75
  89.8 4.4 gather_fusion
  94.2 2.2 bitcast_select_fusion.1
  100.8 6.0 fusion.2
  106.8 7.3 fusion.8
  114.8 7.7 %fusion.131 = (bf16[1024,3,64]{0,2,1:T(8,128)(2,1)S(1)}, f32[1024,3,64]{0,2,1:T(8,128)}) fusion(f32[1024,1024,3]{1,0,2:T(8,128)} %get-tuple-element.151, f32[3,1024]{1,0:T(4,128)S(1)} %get-tuple-element.145, f32[3,1024]{1,0:T(4,128)S(1)} %get-tuple-element.150, pred[1024,1024]{0,1:T(8,128)(4,1)S(1)} %copy-done.6, ...), kind=kOutput, calls=%fused_computation.283 | convolution fusion | flops 418578432 | bytes 14974976 | tf_op jit(solution)/shard_map/gts,sd->tgd/dot_general | solution.py:474
  123.4 7.2 all-to-all-start
  136.3 4.0 all-to-all-done
  162.2 8.7 %collective-permute-done.19 = bf16[128,1536]{0,1:T(8,128)(2,1)S(1)} collective-permute-done((bf16[128,1536]{0,1:T(8,128)(2,1)S(1)}, bf16[128,1536]{0,1:T(8,128)(2,1)S(1)}, u32[]{:S(2)}, u32[]{:S(2)}) %collective-permute-start.19) | collective-permute-done | bytes 393248 | tf_op jit(solution)/shard_map/ppermute | solution.py:75
  171.0 23.0 %collective-permute-done.18 = bf16[128,1536]{0,1:T(8,128)(2,1)S(1)} collective-permute-done((bf16[128,1536]{0,1:T(8,128)(2,1)S(1)}, bf16[128,1536]{0,1:T(8,128)(2,1)S(1)}, u32[]{:S(2)}, u32[]{:S(2)}) %collective-permute-start.18) | collective-permute-done | bytes 393248 | tf_op jit(solution)/shard_map/ppermute | solution.py:75
  202.5 28.1 %near_experts.1 = (bf16[128,1536]{1,0:T(8,128)(2,1)}, bf16[128,1536]{1,0:T(8,128)(2,1)}, bf16[128,1536]{1,0:T(8,128)(2,1)}, bf16[128,1536]{1,0:T(8,128)(2,1)}, b...) custom-call(s32[1]{0:T(128)} %bitcast.48.shard_ref, ...), custom_call_target="tpu_custom_call" | custom-call | flops 9663676416 | bytes 18874368 | tf_op jit(solution)/shard_map/near_experts/pallas_call | solution.py:231
  242.9 2.4 collective-permute-start.38
  246.6 3.8 collective-permute-done.28
  265.8 2.4 pad_maximum_fusion.6
  268.2 4.2 all-to-all-start.1
  272.4 3.7 collective-permute-start.34
  279.8 13.3 %collective-permute-done.34 = bf16[512,192]{0,1:T(8,128)(2,1)S(1)} collective-permute-done((bf16[512,192]{0,1:T(8,128)(2,1)}, bf16[512,192]{0,1:T(8,128)(2,1)S(1)}, u32[]{:S(2)}, u32[]{:S(2)}) %collective-permute-start.34) | collective-permute-done | bytes 196640 | tf_op jit(solution)/shard_map/ppermute | solution.py:75
  298.3 3.4 collective-permute-done.39
  303.7 13.6 %collective-permute-done.35 = bf16[4,512,192]{1,2,0:T(8,128)(2,1)} collective-permute-done((bf16[4,512,192]{1,2,0:T(8,128)(2,1)}, bf16[4,512,192]{1,2,0:T(8,128)(2,1)}, u32[]{:S(2)}, u32[]{:S(2)}) %collective-permute-start.35) | collective-permute-done | bytes 786464 | tf_op jit(solution)/shard_map/ppermute | solution.py:75
  317.4 2.1 slice_bitcast_fusion.1
  323.9 7.2 fusion.33
  331.1 7.2 fusion.1
  340.3 2.2 fusion.19
  342.5 2.1 fusion.32
  346.8 2.3 fusion.30
  349.1 2.1 fusion.29
  351.3 2.3 fusion.28
  355.6 2.2 fusion.26
  357.9 2.1 fusion.25
  360.0 2.7 gather_fusion.5
  362.7 2.2 copy.290
  366.9 4.2 convolution_convert_fusion
  371.1 9.9 %concatenate.120 = bf16[1536,528]{0,1:T(8,128)(2,1)} concatenate(bf16[1536,320]{0,1:T(8,128)(2,1)} %convolution_convert_fusion, bf16[1536,192]{0,1:T(8,128)(2,1)} %select_convert_fusion, bf16[1536,8]{0,1:T(8,128)(2,1)S(1)} %convolution_convert_fusion.1, bf16[1536,1]{0,1:T(2,128)(2,1)S(1)} %broadcast_in_dim.177, bf16[1536,7]{0,1:T(8,128)(2,1)S(1)} %broadcast_in_dim.178), dimensions={1} | concatenate | bytes 3244032 | tf_op jit(solution)/shard_map/concatenate | solution.py:631
  387.8 11.1 %collective-permute-done.42 = bf16[384,528]{0,1:T(8,128)(2,1)} collective-permute-done((bf16[384,528]{0,1:T(8,128)(2,1)}, bf16[384,528]{0,1:T(8,128)(2,1)}, u32[]{:S(2)}, u32[]{:S(2)}) %collective-permute-start.42) | collective-permute-done | bytes 405536 | tf_op jit(solution)/shard_map/ppermute | solution.py:75
  401.1 3.1 collective-permute-start.45
  404.2 2.8 collective-permute-start.44
  407.1 10.0 %collective-permute-done.45 = bf16[128,1664]{0,1:T(8,128)(2,1)S(1)} collective-permute-done((bf16[128,1664]{0,1:T(8,128)(2,1)}, bf16[128,1664]{0,1:T(8,128)(2,1)S(1)}, u32[]{:S(2)}, u32[]{:S(2)}) %collective-permute-start.45) | collective-permute-done | bytes 426016 | tf_op jit(solution)/shard_map/ppermute | solution.py:75
  417.1 42.9 %collective-permute-done.44 = bf16[128,1664]{0,1:T(8,128)(2,1)S(1)} collective-permute-done((bf16[128,1664]{0,1:T(8,128)(2,1)}, bf16[128,1664]{0,1:T(8,128)(2,1)S(1)}, u32[]{:S(2)}, u32[]{:S(2)}) %collective-permute-start.44) | collective-permute-done | bytes 426016 | tf_op jit(solution)/shard_map/ppermute | solution.py:75
  460.0 2.4 pad_maximum_fusion.1
  462.4 3.7 copy.271
  466.2 2.6 copy.275
  470.0 10.5 %all-to-all-start.2 = ((bf16[8,128,320]{1,2,0:T(8,128)(2,1)}), bf16[8,128,320]{1,2,0:T(8,128)(2,1)}, u32[]{:S(2)}, u32[]{:S(2)}) async-start(bf16[8,128,320]{1,2,0:T(8,128)(2,1)} %pad_maximum_fusion.10), calls=%async_computation.2 | async-start | bytes 1310720 | tf_op jit(solution)/shard_map/all_to_all | solution.py:66
  480.5 51.5 %collective-permute-done.30 = bf16[384,2560]{1,0:T(8,128)(2,1)} collective-permute-done((bf16[384,2560]{1,0:T(8,128)(2,1)}, bf16[384,2560]{1,0:T(8,128)(2,1)}, u32[]{:S(2)}, u32[]{:S(2)}) %collective-permute-start.30) | collective-permute-done | bytes 1966112 | tf_op jit(solution)/shard_map/ppermute | solution.py:75
  535.1 4.1 copy.270
  547.6 2.3 convolution_bitcast_fusion.12
  549.9 2.3 convolution_bitcast_fusion.10
  552.2 2.3 convolution_bitcast_fusion.11
  554.5 2.3 convolution_bitcast_fusion.9
  557.7 2.8 gather_fusion.4
  560.5 2.9 multiply_reduce_fusion.2
  563.4 2.3 copy.265
  571.0 2.8 convert_element_type.256
  576.3 2.6 copy.302
  584.8 2.4 multiply_reduce_fusion
  587.2 5.5 copy.278
  598.5 61.7 %all-gather.8.cloned.1.call-done = bf16[32,128,1536]{2,1,0:T(8,128)(2,1)} async-done(((bf16[4,128,1536]{2,1,0:T(8,128)(2,1)}), bf16[32,128,1536]{2,1,0:T(8,128)(2,1)}) %all-gather.8.cloned.1.call-update) | async-done | bytes 12582928 | tf_op jit(solution)/shard_map/all_gather | solution.py:125
  660.3 89.7 %far_weight_grads.1 = f32[2,1536,3072]{2,1,0:T(8,128)} custom-call(s32[3,17]{1,0:T(4,128)} %copy-done.61, s32[16,2,256]{2,1,0:T(2,128)} %reshape.364.chosen, s32[2,16,256]{2,1,0:T(8,128)} %reshape.365.places, bf16[16,1536]{1,0:T(8,128)(2,1)} %pad.17.refs_9_.router_t, bf16[4096,1536]{1,0:T(8,128)(2,1)} %bitcast.456, bf16[4096,1664]{1,0:T(8,128)(2,1)} %bitcast.451, ...), custom_call_target="tpu_custom_call" | custom-call | flops 51539607552 | bytes 81788928 | tf_op jit(solution)/shard_map/far_weight_grads/pallas_call | solution.py:426
  (382 shorter events, 166.6 us)
Async XLA Ops:
  12.2 32.8 %collective-permute-start.9 = (bf16[384,330]{1,0:T(8,128)(2,1)S(1)}, bf16[384,330]{1,0:T(8,128)(2,1)S(1)}, u32[]{:S(2)}, u32[]{:S(2)}) collective-permute-start(bf16[384,330]{1,0:T(8,128)(2,1)S(1)} %concatenate.102), channel_id=1, source_target_pairs={{0,2},{1,3},{2,0},{3,1},{4,6},{5,7},{6,4},{7,5},{8,10},{9,11},{10,... | collective-permute-start | bytes 760328 | tf_op jit(solution)/shard_map/ppermute | solution.py:75
  15.2 41.5 %collective-permute-start.8 = (bf16[384,330]{1,0:T(8,128)(2,1)S(1)}, bf16[384,330]{1,0:T(8,128)(2,1)S(1)}, u32[]{:S(2)}, u32[]{:S(2)}) collective-permute-start(bf16[384,330]{1,0:T(8,128)(2,1)S(1)} %concatenate.102), channel_id=1, source_target_pairs={{0,1},{1,0},{2,3},{3,2},{4,5},{5,4},{6,7},{7,6},{8,9},{9,8},{10,11... | collective-permute-start | bytes 760328 | tf_op jit(solution)/shard_map/ppermute | solution.py:75
  16.3 9.7 %collective-permute-start.2 = (bf16[64,1536]{1,0:T(8,128)(2,1)S(1)}, bf16[64,1536]{1,0:T(8,128)(2,1)S(1)}, u32[]{:S(2)}, u32[]{:S(2)}) collective-permute-start(bf16[64,1536]{1,0:T(8,128)(2,1)S(1)} %get-tuple-element.139), channel_id=1, source_target_pairs={{0,24},{4,28},{8,16},{12,20},{16,8},{20,12},{24,0},{28,4},{1,25},{... | collective-permute-start | bytes 589832 | tf_op jit(solution)/shard_map/ppermute | solution.py:75
  20.0 22.0 %collective-permute-start.1 = (bf16[64,1536]{1,0:T(8,128)(2,1)S(1)}, bf16[64,1536]{1,0:T(8,128)(2,1)S(1)}, u32[]{:S(2)}, u32[]{:S(2)}) collective-permute-start(bf16[64,1536]{1,0:T(8,128)(2,1)S(1)} %get-tuple-element.139), channel_id=1, source_target_pairs={{0,16},{4,20},{8,24},{12,28},{16,0},{20,4},{24,8},{28,12},{1,17},{... | collective-permute-start | bytes 589832 | tf_op jit(solution)/shard_map/ppermute | solution.py:75
  20.0 22.0 %collective-permute-start = (bf16[64,1536]{1,0:T(8,128)(2,1)S(1)}, bf16[64,1536]{1,0:T(8,128)(2,1)S(1)}, u32[]{:S(2)}, u32[]{:S(2)}) collective-permute-start(bf16[64,1536]{1,0:T(8,128)(2,1)S(1)} %get-tuple-element.139), channel_id=1, source_target_pairs={{0,8},{4,12},{8,0},{12,4},{16,24},{20,28},{24,16},{28,20},{1,9},{5... | collective-permute-start | bytes 589832 | tf_op jit(solution)/shard_map/ppermute | solution.py:75
  20.8 34.4 %copy-start.54 = (pred[4]{0:T(512)(128)(4,1)}, pred[4]{0:T(512)(128)(4,1)S(1)}, u32[]{:S(2)}) copy-start(pred[4]{0:T(512)(128)(4,1)S(1)} %compare_and_fusion.1) | copy-start | bytes 16
  20.9 37.9 %copy-start.50 = (s32[1024]{0:T(1024)}, s32[1024]{0:T(1024)S(1)}, u32[]{:S(2)}) copy-start(s32[1024]{0:T(1024)S(1)} %pad_clamp_fusion) | copy-start | bytes 12292
  25.0 33.8 %copy-start.68 = (pred[8]{0:T(512)(128)(4,1)}, pred[8]{0:T(512)(128)(4,1)S(1)}, u32[]{:S(2)}) copy-start(pred[8]{0:T(512)(128)(4,1)S(1)} %compare_and_fusion) | copy-start | bytes 28
  26.0 20.0 %collective-permute-start.6 = (bf16[64,1536]{1,0:T(8,128)(2,1)S(1)}, bf16[64,1536]{1,0:T(8,128)(2,1)S(1)}, u32[]{:S(2)}, u32[]{:S(2)}) collective-permute-start(bf16[64,1536]{1,0:T(8,128)(2,1)S(1)} %get-tuple-element.140), channel_id=1, source_target_pairs={{0,24},{4,28},{8,16},{12,20},{16,8},{20,12},{24,0},{28,4},{1,25},{... | collective-permute-start | bytes 589832 | tf_op jit(solution)/shard_map/ppermute | solution.py:75
  41.9 12.3 %collective-permute-start.5 = (bf16[64,1536]{1,0:T(8,128)(2,1)S(1)}, bf16[64,1536]{1,0:T(8,128)(2,1)S(1)}, u32[]{:S(2)}, u32[]{:S(2)}) collective-permute-start(bf16[64,1536]{1,0:T(8,128)(2,1)S(1)} %get-tuple-element.140), channel_id=1, source_target_pairs={{0,16},{4,20},{8,24},{12,28},{16,0},{20,4},{24,8},{28,12},{1,17},{... | collective-permute-start | bytes 589832 | tf_op jit(solution)/shard_map/ppermute | solution.py:75
  42.0 12.2 %collective-permute-start.4 = (bf16[64,1536]{1,0:T(8,128)(2,1)S(1)}, bf16[64,1536]{1,0:T(8,128)(2,1)S(1)}, u32[]{:S(2)}, u32[]{:S(2)}) collective-permute-start(bf16[64,1536]{1,0:T(8,128)(2,1)S(1)} %get-tuple-element.140), channel_id=1, source_target_pairs={{0,8},{4,12},{8,0},{12,4},{16,24},{20,28},{24,16},{28,20},{1,9},{5... | collective-permute-start | bytes 589832 | tf_op jit(solution)/shard_map/ppermute | solution.py:75
  45.0 11.7 %collective-permute-start.10 = (bf16[384,330]{1,0:T(8,128)(2,1)S(1)}, bf16[384,330]{1,0:T(8,128)(2,1)S(1)}, u32[]{:S(2)}, u32[]{:S(2)}) collective-permute-start(bf16[384,330]{1,0:T(8,128)(2,1)S(1)} %collective-permute-done.9), channel_id=1, source_target_pairs={{0,1},{1,0},{2,3},{3,2},{4,5},{5,4},{6,7},{7,6},{8,9},{9,8},{10,11... | collective-permute-start | bytes 760328 | tf_op jit(solution)/shard_map/ppermute | solution.py:75
  46.0 20.7 %collective-permute-start.3 = (bf16[4,64,1536]{2,1,0:T(8,128)(2,1)}, bf16[4,64,1536]{2,1,0:T(8,128)(2,1)}, u32[]{:S(2)}, u32[]{:S(2)}) collective-permute-start(bf16[4,64,1536]{2,1,0:T(8,128)(2,1)} %pad_maximum_fusion.4), channel_id=1, source_target_pairs={{0,4},{4,0},{8,12},{12,8},{16,20},{20,16},{24,28},{28,24},{1,5},{5... | collective-permute-start | bytes 2359304 | tf_op jit(solution)/shard_map/ppermute | solution.py:75
  55.2 27.9 %collective-permute-start.7 = (bf16[4,64,1536]{2,1,0:T(8,128)(2,1)}, bf16[4,64,1536]{2,1,0:T(8,128)(2,1)}, u32[]{:S(2)}, u32[]{:S(2)}) collective-permute-start(bf16[4,64,1536]{2,1,0:T(8,128)(2,1)} %pad_maximum_fusion.5), channel_id=1, source_target_pairs={{0,4},{4,0},{8,12},{12,8},{16,20},{20,16},{24,28},{28,24},{1,5},{5... | collective-permute-start | bytes 2359304 | tf_op jit(solution)/shard_map/ppermute | solution.py:75
  62.4 35.4 %copy-start.41 = (f32[1536]{0:T(1024)}, f32[1536]{0:T(1024)S(1)}, u32[]{:S(2)}) copy-start(f32[1536]{0:T(1024)S(1)} %get-tuple-element.97) | copy-start | bytes 18436
  97.2 37.9 %collective-permute-start.21 = (bf16[128,1664]{0,1:T(8,128)(2,1)}, bf16[128,1664]{0,1:T(8,128)(2,1)}, u32[]{:S(2)}, u32[]{:S(2)}) collective-permute-start(bf16[128,1664]{0,1:T(8,128)(2,1)} %fusion.57), channel_id=1, source_target_pairs={{0,2},{1,3},{2,0},{3,1},{4,6},{5,7},{6,4},{7,5},{8,10},{9,11},{10,... | collective-permute-start | bytes 1277960 | tf_op jit(solution)/shard_map/ppermute | solution.py:75
  99.9 41.1 %collective-permute-start.12 = (bf16[384,1536]{1,0:T(8,128)(2,1)}, bf16[384,1536]{1,0:T(8,128)(2,1)}, u32[]{:S(2)}, u32[]{:S(2)}) collective-permute-start(bf16[384,1536]{1,0:T(8,128)(2,1)} %param.14), channel_id=1, source_target_pairs={{0,2},{1,3},{2,0},{3,1},{4,6},{5,7},{6,4},{7,5},{8,10},{9,11},{10,... | collective-permute-start | bytes 3538952 | tf_op jit(solution)/shard_map/ppermute | solution.py:75
  122.5 117.4 %copy-start.9 = (bf16[1024,3,64]{0,2,1:T(8,128)(2,1)}, bf16[1024,3,64]{0,2,1:T(8,128)(2,1)S(1)}, u32[]{:S(2)}) copy-start(bf16[1024,3,64]{0,2,1:T(8,128)(2,1)S(1)} %get-tuple-element.152) | copy-start | bytes 1179652
  123.4 16.9 %all-to-all-start = ((bf16[8,128,192]{1,2,0:T(8,128)(2,1)}), bf16[8,128,192]{1,2,0:T(8,128)(2,1)S(1)}, u32[]{:S(2)}, u32[]{:S(2)}) async-start(bf16[8,128,192]{1,2,0:T(8,128)(2,1)} %copy.233), calls=%async_computation | async-start | bytes 786432 | tf_op jit(solution)/shard_map/all_to_all | solution.py:66
  133.9 14.6 %collective-permute-start.20 = (bf16[128,1664]{0,1:T(8,128)(2,1)}, bf16[128,1664]{0,1:T(8,128)(2,1)}, u32[]{:S(2)}, u32[]{:S(2)}) collective-permute-start(bf16[128,1664]{0,1:T(8,128)(2,1)} %fusion.57), channel_id=1, source_target_pairs={{0,1},{1,0},{2,3},{3,2},{4,5},{5,4},{6,7},{7,6},{8,9},{9,8},{10,11... | collective-permute-start | bytes 1277960 | tf_op jit(solution)/shard_map/ppermute | solution.py:75
  133.9 11.1 %collective-permute-start.11 = (bf16[384,1536]{1,0:T(8,128)(2,1)}, bf16[384,1536]{1,0:T(8,128)(2,1)S(1)}, u32[]{:S(2)}, u32[]{:S(2)}) collective-permute-start(bf16[384,1536]{1,0:T(8,128)(2,1)} %param.14), channel_id=1, source_target_pairs={{0,1},{1,0},{2,3},{3,2},{4,5},{5,4},{6,7},{7,6},{8,9},{9,8},{10,11... | collective-permute-start | bytes 3538952 | tf_op jit(solution)/shard_map/ppermute | solution.py:75
  135.1 18.1 %collective-permute-start.22 = (bf16[128,1664]{0,1:T(8,128)(2,1)}, bf16[128,1664]{0,1:T(8,128)(2,1)}, u32[]{:S(2)}, u32[]{:S(2)}) collective-permute-start(bf16[128,1664]{0,1:T(8,128)(2,1)} %collective-permute-done.21), channel_id=1, source_target_pairs={{0,1},{1,0},{2,3},{3,2},{4,5},{5,4},{6,7},{7,6},{8,9},{9,8},{10,11... | collective-permute-start | bytes 1277960 | tf_op jit(solution)/shard_map/ppermute | solution.py:75
  141.0 4.6 collective-permute-start.13
  146.8 48.5 %copy-start.48 = (f32[128]{0:T(128)}, f32[128]{0:T(128)S(1)}, u32[]{:S(2)}) copy-start(f32[128]{0:T(128)S(1)} %get-tuple-element.149) | copy-start | bytes 1540
  147.0 14.4 %collective-permute-start.15 = (bf16[128,1536]{0,1:T(8,128)(2,1)S(1)}, bf16[128,1536]{0,1:T(8,128)(2,1)S(1)}, u32[]{:S(2)}, u32[]{:S(2)}) collective-permute-start(bf16[128,1536]{0,1:T(8,128)(2,1)S(1)} %multiply_convert_fusion), channel_id=1, source_target_pairs={{0,2},{1,3},{2,0},{3,1},{4,6},{5,7},{6,4},{7,5},{8,10},{9,11},{10,... | collective-permute-start | bytes 1179656 | tf_op jit(solution)/shard_map/ppermute | solution.py:75
  157.1 13.9 %collective-permute-start.19 = (bf16[128,1536]{0,1:T(8,128)(2,1)S(1)}, bf16[128,1536]{0,1:T(8,128)(2,1)S(1)}, u32[]{:S(2)}, u32[]{:S(2)}) collective-permute-start(bf16[128,1536]{0,1:T(8,128)(2,1)S(1)} %multiply_convert_fusion), channel_id=1, source_target_pairs={{0,24},{4,28},{8,16},{12,20},{16,8},{20,12},{24,0},{28,4},{1,25},{... | collective-permute-start | bytes 1179656 | tf_op jit(solution)/shard_map/ppermute | solution.py:75
  158.2 35.7 %collective-permute-start.18 = (bf16[128,1536]{0,1:T(8,128)(2,1)S(1)}, bf16[128,1536]{0,1:T(8,128)(2,1)S(1)}, u32[]{:S(2)}, u32[]{:S(2)}) collective-permute-start(bf16[128,1536]{0,1:T(8,128)(2,1)S(1)} %multiply_convert_fusion), channel_id=1, source_target_pairs={{0,16},{4,20},{8,24},{12,28},{16,0},{20,4},{24,8},{28,12},{1,17},{... | collective-permute-start | bytes 1179656 | tf_op jit(solution)/shard_map/ppermute | solution.py:75
  159.5 34.5 %collective-permute-start.17 = (bf16[128,1536]{0,1:T(8,128)(2,1)S(1)}, bf16[128,1536]{0,1:T(8,128)(2,1)S(1)}, u32[]{:S(2)}, u32[]{:S(2)}) collective-permute-start(bf16[128,1536]{0,1:T(8,128)(2,1)S(1)} %multiply_convert_fusion), channel_id=1, source_target_pairs={{0,8},{4,12},{8,0},{12,4},{16,24},{20,28},{24,16},{28,20},{1,9},{5... | collective-permute-start | bytes 1179656 | tf_op jit(solution)/shard_map/ppermute | solution.py:75
  161.4 33.9 %collective-permute-start.14 = (bf16[128,1536]{0,1:T(8,128)(2,1)S(1)}, bf16[128,1536]{0,1:T(8,128)(2,1)S(1)}, u32[]{:S(2)}, u32[]{:S(2)}) collective-permute-start(bf16[128,1536]{0,1:T(8,128)(2,1)S(1)} %multiply_convert_fusion), channel_id=1, source_target_pairs={{0,1},{1,0},{2,3},{3,2},{4,5},{5,4},{6,7},{7,6},{8,9},{9,8},{10,11... | collective-permute-start | bytes 1179656 | tf_op jit(solution)/shard_map/ppermute | solution.py:75
  161.5 33.9 %collective-permute-start.16 = (bf16[128,1536]{0,1:T(8,128)(2,1)S(1)}, bf16[128,1536]{0,1:T(8,128)(2,1)S(1)}, u32[]{:S(2)}, u32[]{:S(2)}) collective-permute-start(bf16[128,1536]{0,1:T(8,128)(2,1)S(1)} %collective-permute-done.15), channel_id=1, source_target_pairs={{0,1},{1,0},{2,3},{3,2},{4,5},{5,4},{6,7},{7,6},{8,9},{9,8},{10,11... | collective-permute-start | bytes 1179656 | tf_op jit(solution)/shard_map/ppermute | solution.py:75
  232.6 3.8 collective-permute-start.27
  235.9 10.6 %collective-permute-start.26 = (bf16[128,1664]{0,1:T(8,128)(2,1)}, bf16[128,1664]{0,1:T(8,128)(2,1)}, u32[]{:S(2)}, u32[]{:S(2)}) collective-permute-start(bf16[128,1664]{0,1:T(8,128)(2,1)} %copy.251), channel_id=1, source_target_pairs={{0,1},{1,0},{2,3},{3,2},{4,5},{5,4},{6,7},{7,6},{8,9},{9,8},{10,11... | collective-permute-start | bytes 1277960 | tf_op jit(solution)/shard_map/ppermute | solution.py:75
  238.3 12.1 %collective-permute-start.28 = (bf16[128,1664]{0,1:T(8,128)(2,1)}, bf16[128,1664]{0,1:T(8,128)(2,1)}, u32[]{:S(2)}, u32[]{:S(2)}) collective-permute-start(bf16[128,1664]{0,1:T(8,128)(2,1)} %add_convert_fusion), channel_id=1, source_target_pairs={{0,2},{1,3},{2,0},{3,1},{4,6},{5,7},{6,4},{7,5},{8,10},{9,11},{10,... | collective-permute-start | bytes 1277960 | tf_op jit(solution)/shard_map/ppermute | solution.py:75
  240.9 31.6 %collective-permute-start.37 = (bf16[512,192]{0,1:T(8,128)(2,1)}, bf16[512,192]{0,1:T(8,128)(2,1)}, u32[]{:S(2)}, u32[]{:S(2)}) collective-permute-start(bf16[512,192]{0,1:T(8,128)(2,1)} %get-tuple-element.132), channel_id=1, source_target_pairs={{0,16},{4,20},{8,24},{12,28},{16,0},{20,4},{24,8},{28,12},{1,17},{... | collective-permute-start | bytes 589832 | tf_op jit(solution)/shard_map/ppermute | solution.py:75
  240.9 35.3 %collective-permute-start.36 = (bf16[512,192]{0,1:T(8,128)(2,1)}, bf16[512,192]{0,1:T(8,128)(2,1)}, u32[]{:S(2)}, u32[]{:S(2)}) collective-permute-start(bf16[512,192]{0,1:T(8,128)(2,1)} %get-tuple-element.132), channel_id=1, source_target_pairs={{0,8},{4,12},{8,0},{12,4},{16,24},{20,28},{24,16},{28,20},{1,9},{5... | collective-permute-start | bytes 589832 | tf_op jit(solution)/shard_map/ppermute | solution.py:75
  242.9 33.3 %collective-permute-start.38 = (bf16[512,192]{0,1:T(8,128)(2,1)}, bf16[512,192]{0,1:T(8,128)(2,1)}, u32[]{:S(2)}, u32[]{:S(2)}) collective-permute-start(bf16[512,192]{0,1:T(8,128)(2,1)} %get-tuple-element.132), channel_id=1, source_target_pairs={{0,24},{4,28},{8,16},{12,20},{16,8},{20,12},{24,0},{28,4},{1,25},{... | collective-permute-start | bytes 589832 | tf_op jit(solution)/shard_map/ppermute | solution.py:75
  246.5 33.3 %collective-permute-start.33 = (bf16[512,192]{0,1:T(8,128)(2,1)}, bf16[512,192]{0,1:T(8,128)(2,1)}, u32[]{:S(2)}, u32[]{:S(2)}) collective-permute-start(bf16[512,192]{0,1:T(8,128)(2,1)} %get-tuple-element.133), channel_id=1, source_target_pairs={{0,16},{4,20},{8,24},{12,28},{16,0},{20,4},{24,8},{28,12},{1,17},{... | collective-permute-start | bytes 589832 | tf_op jit(solution)/shard_map/ppermute | solution.py:75
  250.4 29.4 %collective-permute-start.32 = (bf16[512,192]{0,1:T(8,128)(2,1)}, bf16[512,192]{0,1:T(8,128)(2,1)}, u32[]{:S(2)}, u32[]{:S(2)}) collective-permute-start(bf16[512,192]{0,1:T(8,128)(2,1)} %get-tuple-element.133), channel_id=1, source_target_pairs={{0,8},{4,12},{8,0},{12,4},{16,24},{20,28},{24,16},{28,20},{1,9},{5... | collective-permute-start | bytes 589832 | tf_op jit(solution)/shard_map/ppermute | solution.py:75
  265.7 30.9 %copy-start.69 = (pred[8]{0:T(512)(128)(4,1)S(1)}, pred[8]{0:T(512)(128)(4,1)}, u32[]{:S(2)}) copy-start(pred[8]{0:T(512)(128)(4,1)} %copy-done.68) | copy-start | bytes 28
  265.7 31.6 %copy-start.45 = (pred[128,8]{0,1:T(8,128)(4,1)S(1)}, pred[128,8]{0,1:T(8,128)(4,1)}, u32[]{:S(2)}) copy-start(pred[128,8]{0,1:T(8,128)(4,1)} %copy-done.44) | copy-start | bytes 3076
  265.8 31.6 %copy-start.47 = (f32[128]{0:T(128)S(1)}, f32[128]{0:T(128)}, u32[]{:S(2)}) copy-start(f32[128]{0:T(128)} %copy-done.46) | copy-start | bytes 1540
  265.8 31.6 %copy-start.52 = (f32[128]{0:T(128)S(1)}, f32[128]{0:T(128)}, u32[]{:S(2)}) copy-start(f32[128]{0:T(128)} %copy-done.51) | copy-start | bytes 1540
  265.8 31.6 %copy-start.57 = (f32[128]{0:T(128)S(1)}, f32[128]{0:T(128)}, u32[]{:S(2)}) copy-start(f32[128]{0:T(128)} %copy-done.56) | copy-start | bytes 1540
  268.2 51.3 %all-to-all-start.1 = ((bf16[8,128,384]{2,1,0:T(8,128)(2,1)}), bf16[8,128,384]{2,1,0:T(8,128)(2,1)}, u32[]{:S(2)}, u32[]{:S(2)}) async-start(bf16[8,128,384]{2,1,0:T(8,128)(2,1)} %pad_maximum_fusion.6), calls=%async_computation.1 | async-start | bytes 1572864 | tf_op jit(solution)/shard_map/all_to_all | solution.py:66
  272.4 298.6 %all-gather.4.cloned.1.call-start = ((), (), s32[]{:S(2)}) async-start(), calls=%async_computation.3 | async-start | bytes 3649536 | tf_op jit(solution)/shard_map/all_gather | solution.py:70
  272.4 20.7 %collective-permute-start.34 = (bf16[512,192]{0,1:T(8,128)(2,1)}, bf16[512,192]{0,1:T(8,128)(2,1)S(1)}, u32[]{:S(2)}, u32[]{:S(2)}) collective-permute-start(bf16[512,192]{0,1:T(8,128)(2,1)} %get-tuple-element.133), channel_id=1, source_target_pairs={{0,24},{4,28},{8,16},{12,20},{16,8},{20,12},{24,0},{28,4},{1,25},{... | collective-permute-start | bytes 589832 | tf_op jit(solution)/shard_map/ppermute | solution.py:75
  278.3 23.4 %collective-permute-start.39 = (bf16[4,512,192]{1,2,0:T(8,128)(2,1)}, bf16[4,512,192]{1,2,0:T(8,128)(2,1)}, u32[]{:S(2)}, u32[]{:S(2)}) collective-permute-start(bf16[4,512,192]{1,2,0:T(8,128)(2,1)} %pad_maximum_fusion.9), channel_id=1, source_target_pairs={{0,4},{4,0},{8,12},{12,8},{16,20},{20,16},{24,28},{28,24},{1,5},{5... | collective-permute-start | bytes 2359304 | tf_op jit(solution)/shard_map/ppermute | solution.py:75
  295.2 22.2 %collective-permute-start.35 = (bf16[4,512,192]{1,2,0:T(8,128)(2,1)}, bf16[4,512,192]{1,2,0:T(8,128)(2,1)}, u32[]{:S(2)}, u32[]{:S(2)}) collective-permute-start(bf16[4,512,192]{1,2,0:T(8,128)(2,1)} %pad_maximum_fusion.8), channel_id=1, source_target_pairs={{0,4},{4,0},{8,12},{12,8},{16,20},{20,16},{24,28},{28,24},{1,5},{5... | collective-permute-start | bytes 2359304 | tf_op jit(solution)/shard_map/ppermute | solution.py:75
  383.1 2.1 collective-permute-start.41
  383.1 4.7 collective-permute-start.40
  387.2 11.7 %collective-permute-start.42 = (bf16[384,528]{0,1:T(8,128)(2,1)}, bf16[384,528]{0,1:T(8,128)(2,1)}, u32[]{:S(2)}, u32[]{:S(2)}) collective-permute-start(bf16[384,528]{0,1:T(8,128)(2,1)} %add_convert_fusion.2), channel_id=1, source_target_pairs={{0,2},{1,3},{2,0},{3,1},{4,6},{5,7},{6,4},{7,5},{8,10},{9,11},{10,... | collective-permute-start | bytes 1216520 | tf_op jit(solution)/shard_map/ppermute | solution.py:75
  401.1 192.8 %all-gather.6.cloned.1.call-start = ((), (), s32[]{:S(2)}) async-start(), calls=%async_computation.4 | async-start | bytes 15335424 | tf_op jit(solution)/shard_map/all_gather | solution.py:125
  401.1 16.0 %collective-permute-start.45 = (bf16[128,1664]{0,1:T(8,128)(2,1)}, bf16[128,1664]{0,1:T(8,128)(2,1)S(1)}, u32[]{:S(2)}, u32[]{:S(2)}) collective-permute-start(bf16[128,1664]{0,1:T(8,128)(2,1)} %fusion.57), channel_id=1, source_target_pairs={{0,24},{4,28},{8,16},{12,20},{16,8},{20,12},{24,0},{28,4},{1,25},{... | collective-permute-start | bytes 1277960 | tf_op jit(solution)/shard_map/ppermute | solution.py:75
  404.2 55.8 %collective-permute-start.44 = (bf16[128,1664]{0,1:T(8,128)(2,1)}, bf16[128,1664]{0,1:T(8,128)(2,1)S(1)}, u32[]{:S(2)}, u32[]{:S(2)}) collective-permute-start(bf16[128,1664]{0,1:T(8,128)(2,1)} %fusion.57), channel_id=1, source_target_pairs={{0,16},{4,20},{8,24},{12,28},{16,0},{20,4},{24,8},{28,12},{1,17},{... | collective-permute-start | bytes 1277960 | tf_op jit(solution)/shard_map/ppermute | solution.py:75
  407.0 53.0 %collective-permute-start.43 = (bf16[128,1664]{0,1:T(8,128)(2,1)}, bf16[128,1664]{0,1:T(8,128)(2,1)S(1)}, u32[]{:S(2)}, u32[]{:S(2)}) collective-permute-start(bf16[128,1664]{0,1:T(8,128)(2,1)} %fusion.57), channel_id=1, source_target_pairs={{0,8},{4,12},{8,0},{12,4},{16,24},{20,28},{24,16},{28,20},{1,9},{5... | collective-permute-start | bytes 1277960 | tf_op jit(solution)/shard_map/ppermute | solution.py:75
  466.1 194.2 %all-gather.8.cloned.1.call-start = ((), (), s32[]{:S(2)}) async-start(), calls=%async_computation.5 | async-start | bytes 14155776 | tf_op jit(solution)/shard_map/all_gather | solution.py:125
  468.8 63.3 %collective-permute-start.30 = (bf16[384,2560]{1,0:T(8,128)(2,1)}, bf16[384,2560]{1,0:T(8,128)(2,1)}, u32[]{:S(2)}, u32[]{:S(2)}) collective-permute-start(bf16[384,2560]{1,0:T(8,128)(2,1)} %param.13), channel_id=1, source_target_pairs={{0,2},{1,3},{2,0},{3,1},{4,6},{5,7},{6,4},{7,5},{8,10},{9,11},{10,... | collective-permute-start | bytes 5898248 | tf_op jit(solution)/shard_map/ppermute | solution.py:75
  468.9 83.3 %collective-permute-start.29 = (bf16[384,2560]{1,0:T(8,128)(2,1)}, bf16[384,2560]{1,0:T(8,128)(2,1)}, u32[]{:S(2)}, u32[]{:S(2)}) collective-permute-start(bf16[384,2560]{1,0:T(8,128)(2,1)} %param.13), channel_id=1, source_target_pairs={{0,1},{1,0},{2,3},{3,2},{4,5},{5,4},{6,7},{7,6},{8,9},{9,8},{10,11... | collective-permute-start | bytes 5898248 | tf_op jit(solution)/shard_map/ppermute | solution.py:75
  470.0 75.5 %all-to-all-start.2 = ((bf16[8,128,320]{1,2,0:T(8,128)(2,1)}), bf16[8,128,320]{1,2,0:T(8,128)(2,1)}, u32[]{:S(2)}, u32[]{:S(2)}) async-start(bf16[8,128,320]{1,2,0:T(8,128)(2,1)} %pad_maximum_fusion.10), calls=%async_computation.2 | async-start | bytes 1310720 | tf_op jit(solution)/shard_map/all_to_all | solution.py:66
  532.1 22.4 %collective-permute-start.31 = (bf16[384,2560]{1,0:T(8,128)(2,1)}, bf16[384,2560]{1,0:T(8,128)(2,1)}, u32[]{:S(2)}, u32[]{:S(2)}) collective-permute-start(bf16[384,2560]{1,0:T(8,128)(2,1)} %collective-permute-done.30), channel_id=1, source_target_pairs={{0,1},{1,0},{2,3},{3,2},{4,5},{5,4},{6,7},{7,6},{8,9},{9,8},{10,11... | collective-permute-start | bytes 5898248 | tf_op jit(solution)/shard_map/ppermute | solution.py:75
  534.0 10.1 %collective-permute-start.24 = (bf16[128,1536]{0,1:T(8,128)(2,1)}, bf16[128,1536]{0,1:T(8,128)(2,1)}, u32[]{:S(2)}, u32[]{:S(2)}) collective-permute-start(bf16[128,1536]{0,1:T(8,128)(2,1)} %copy.249), channel_id=1, source_target_pairs={{0,1},{1,0},{2,3},{3,2},{4,5},{5,4},{6,7},{7,6},{8,9},{9,8},{10,11... | collective-permute-start | bytes 1179656 | tf_op jit(solution)/shard_map/ppermute | solution.py:75
  544.1 22.3 %collective-permute-start.23 = (bf16[128,1536]{0,1:T(8,128)(2,1)}, bf16[128,1536]{0,1:T(8,128)(2,1)}, u32[]{:S(2)}, u32[]{:S(2)}) collective-permute-start(bf16[128,1536]{0,1:T(8,128)(2,1)} %copy.247), channel_id=1, source_target_pairs={{0,1},{1,0},{2,3},{3,2},{4,5},{5,4},{6,7},{7,6},{8,9},{9,8},{10,11... | collective-permute-start | bytes 1179656 | tf_op jit(solution)/shard_map/ppermute | solution.py:75
  545.3 21.1 %collective-permute-start.25 = (bf16[128,1536]{0,1:T(8,128)(2,1)S(1)}, bf16[128,1536]{0,1:T(8,128)(2,1)S(1)}, u32[]{:S(2)}, u32[]{:S(2)}) collective-permute-start(bf16[128,1536]{0,1:T(8,128)(2,1)S(1)} %add_convert_fusion.4), channel_id=1, source_target_pairs={{0,2},{1,3},{2,0},{3,1},{4,6},{5,7},{6,4},{7,5},{8,10},{9,11},{10,... | collective-permute-start | bytes 1179656 | tf_op jit(solution)/shard_map/ppermute | solution.py:75
  598.5 61.8 %copy-start.61 = (s32[3,17]{1,0:T(4,128)}, s32[3,17]{1,0:T(4,128)S(1)}, u32[]{:S(2)}) copy-start(s32[3,17]{1,0:T(4,128)S(1)} %scatter.4.meta) | copy-start | bytes 616
  (58 other events, 539.2 us)
Sparse Core Ops, SparseCore 0:
  401.2 84.7 all-gather.3
  487.8 98.3 all-gather.5
  588.1 72.1 all-gather.7

commit v4 on v3

v4 whole, which is shorter than its diff:
```python
import functools

import jax
import jax.numpy as jnp
from jax import lax
from jax.experimental import pallas as pl
from jax.experimental.pallas import tpu as pltpu
from jax.sharding import PartitionSpec as P

HQ = 24
HK = 8
HD = 64
GROUP = HQ // HK
FF = 1024
EXPERTS = 8
CAP = 64
Q_COLS = HQ * HD
K_COLS = HK * HD
HEAD = GROUP * HD
HEAD_COLS = HEAD + 2 * HD
SCALE = HD**-0.5
EXTRA = 16
LANES = 128
TILE = 256
CHUNK = 256
SEGMENT = 32
JOINED = 2
QUERIES = 256
DEPTHS = (1, 2, 3, 4, 6, 8)
VMEM = 58 * 1024 * 1024

NORM_EPS = 1e-05
MASK_NEG = -1e30
BF = jnp.bfloat16
F32 = jnp.float32


def dot(a, b):
    return jnp.dot(a, b, preferred_element_type=F32)


def dot_t(a, b):
    return lax.dot_general(a, b, (((1,), (1,)), ((), ())), preferred_element_type=F32)


def t_dot(a, b):
    return lax.dot_general(a, b, (((0,), (0,)), ((), ())), preferred_element_type=F32)


def iota(shape, axis):
    return lax.broadcasted_iota(jnp.int32, shape, axis)


def rms_factor(values):
    return lax.rsqrt(jnp.mean(values * values, axis=-1, keepdims=True) + NORM_EPS)


def rms_input_grad(values, factor, gain_vec, incoming):
    inner = incoming * gain_vec
    cubed = factor * factor * factor
    return factor * inner - values * cubed * jnp.mean(inner * values, axis=-1, keepdims=True)


def to_all(value, axis):
    return lax.all_to_all(value, axis, 0, 0, tiled=True)


def exchanged(value, axis, distance):
    count = lax.axis_size(axis)
    return lax.ppermute(value, axis, [(i, i ^ distance) for i in range(count)])


def near_blocks(own):
    blocks = {0: own}
    distance = lax.axis_size("fsdp") // 2
    while distance:
        blocks.update({r ^ distance: exchanged(b, "fsdp", distance) for r, b in blocks.items()})
        distance //= 2
    return [blocks[r] for r in range(len(blocks))]


def near_terms(blocks):
    shards = lax.axis_size("fsdp")
    terms = {r: [block] for r, block in enumerate(blocks)}
    distance = 1

    def total(parts):
        if len(parts) == 1:
            return parts[0]
        return sum((part.astype(F32) for part in parts[1:]), parts[0].astype(F32)).astype(BF)

    while distance < shards:
        terms = {
            r: terms[r] + [exchanged(total(terms[r ^ distance]), "fsdp", distance)]
            for r in range(0, shards, 2 * distance)
        }
        distance *= 2
    return terms[0]


def line_blocks(own):
    spans = lax.axis_size("ctx")
    return jnp.stack([own] + [exchanged(own, "ctx", d) for d in range(2, spans, 2)])


def span_pieces(own):
    half = own.shape[0] // 2
    same = [line_blocks(part) for part in (own[:half], own[half:])]
    return same + [exchanged(part, "ctx", 1) for part in same]


def all_blocks(line):
    spans, shards = lax.axis_size("ctx"), lax.axis_size("fsdp")
    sets = [
        [(2 * pair + side) * shards + f for side in range(2) for f in range(shards)]
        for pair in range(spans // 2)
    ]
    return lax.all_gather(line, ("ctx", "fsdp"), axis=0, tiled=True, axis_index_groups=sets)


def after(values, *others):
    return lax.optimization_barrier((values, others))[0]


def whole(array):
    shape = array.shape
    return pl.BlockSpec(shape, lambda *_: (0,) * len(shape))


def anywhere():
    return pl.BlockSpec(memory_space=pl.ANY)


def place_pieces(here, pieces, target, sems):
    copies = []
    for i, piece in enumerate(pieces):
        odd, last = divmod(i, 2)
        rows = piece.shape[1]
        for j in range(piece.shape[0]):
            copies.append(
                pltpu.make_async_copy(
                    piece.at[j],
                    target.at[here ^ (2 * j + odd), pl.ds(last * rows, rows)],
                    sems.at[i, j],
                )
            )
    for copy in copies:
        copy.start()
    return copies


def doc_of(starts, positions):
    found = jnp.zeros(positions.shape, jnp.int32)
    for i in range(starts.shape[0]):
        found = found + (positions >= starts[i]).astype(jnp.int32)
    return found


def visible(starts, here, copies, tokens, first, rows, keys):
    query = first + iota((rows, 1), 0)
    key = iota((1, keys), 1)
    allowed = (key <= query) & (doc_of(starts, key) == doc_of(starts, query))
    if copies > 1:
        allowed = allowed & (lax.rem(query // tokens, copies) == lax.rem(here, copies))
    return allowed


def stream_kernel(
    copies,
    place,
    starts,
    *refs,
):
    shards = len(refs) - 15
    pieces, weights, side = refs[:4], refs[4 : 4 + shards], refs[4 + shards]
    normed, mixed, attended_low, attended, log_norm, rows, weight, piece_sems, weight_sems = refs[
        5 + shards : 14 + shards
    ]
    here, shard = place[0], place[1]
    spans, tokens, width = rows.shape
    length = spans * tokens
    copying = place_pieces(here, pieces, rows, piece_sems)
    loading = [
        pltpu.make_async_copy(ref, weight.at[shard ^ r], weight_sems.at[r])
        for r, ref in enumerate(weights)
    ]
    for copy in loading:
        copy.start()
    for copy in loading + copying:
        copy.wait()
    head_weight = weight[...].reshape(width, HEAD_COLS)
    gain = side[EXPERTS : EXPERTS + 1, :].astype(F32)

    @pl.loop(0, spans)
    def _(span):
        x = rows[span].astype(F32)
        low = (x * rms_factor(x) * gain).astype(BF)
        at = pl.ds(pl.multiple_of(span * tokens, tokens), tokens)
        normed[at, :] = low
        mixed[at, :] = dot(low, head_weight).astype(BF)

    for first in range(0, length, QUERIES):
        keys = first + QUERIES
        at = slice(first, keys)
        allowed = visible(starts, here, copies, tokens, first, QUERIES, keys)
        for g in range(GROUP):
            columns = slice(g * HD, (g + 1) * HD)
            scores = dot_t(mixed[at, columns], mixed[:keys, HEAD : HEAD + HD]) * SCALE
            scores = jnp.where(allowed, scores, MASK_NEG)
            highest = jnp.max(scores, axis=1, keepdims=True)
            parts = jnp.where(allowed, jnp.exp(scores - highest), 0.0)
            total = jnp.sum(parts, axis=1, keepdims=True)
            total = jnp.where(total == 0.0, 1.0, total)
            log_norm[at, g : g + 1] = highest + jnp.log(total)
            result = dot((parts / total).astype(BF), mixed[:keys, HEAD + HD :])
            attended[at, columns] = result
            attended_low[at, columns] = result.astype(BF)


def stream_attention(place, starts, pieces, head_weights, side, copies):
    spans, tokens = 2 * pieces[0].shape[0], 2 * pieces[0].shape[1]
    width = pieces[0].shape[2]
    length = spans * tokens
    shards = len(head_weights)
    return pl.pallas_call(
        functools.partial(stream_kernel, copies),
        grid_spec=pltpu.PrefetchScalarGridSpec(
            num_scalar_prefetch=2,
            grid=(1,),
            in_specs=[anywhere()] * (4 + shards) + [whole(side)],
            out_specs=[
                pl.BlockSpec((length, columns), lambda *_: (0, 0))
                for columns in (width, HEAD_COLS, HEAD, HEAD, LANES)
            ],
            scratch_shapes=[
                pltpu.VMEM((spans, tokens, width), BF),
                pltpu.VMEM((shards, width // shards, HEAD_COLS), BF),
                pltpu.SemaphoreType.DMA((4, spans // 2)),
                pltpu.SemaphoreType.DMA((shards,)),
                pltpu.SMEM((1,), jnp.int32),
            ],
        ),
        out_shape=[
            jax.ShapeDtypeStruct((length, columns), kind)
            for columns, kind in (
                (width, BF),
                (HEAD_COLS, BF),
                (HEAD, BF),
                (HEAD, F32),
                (LANES, F32),
            )
        ],
        compiler_params=pltpu.CompilerParams(vmem_limit_bytes=VMEM),
        cost_estimate=pl.CostEstimate(
            flops=2 * length * width * HEAD_COLS + 4 * length * length * HEAD,
            bytes_accessed=8 * length * width,
            transcendentals=GROUP * length * length,
        ),
        name="stream_attention",
    )(place, starts, *pieces, *head_weights, side)


def home_kernel(copies, place, own, tokens, side, *refs):
    weights, (middle, second) = refs[:-2], refs[-2:]
    shards = len(weights)
    heads = HK // shards
    total = tokens[...].astype(F32)
    for r, weight in enumerate(weights):
        first = (place[1] ^ r) * heads
        for h in range(heads):
            part = own[(first + h) * copies]
            for i in range(1, copies):
                part = part + own[(first + h) * copies + i]
            total = total + dot(part, weight[h * HEAD : (h + 1) * HEAD, :])
    middle[...] = total
    gain = side[EXPERTS + 1 : EXPERTS + 2, :].astype(F32)
    second[...] = (total * rms_factor(total) * gain).astype(BF)


def home_forward(place, own, tokens, side, weights, copies):
    args = (own, tokens, side, *weights)
    return pl.pallas_call(
        functools.partial(home_kernel, copies),
        grid_spec=pltpu.PrefetchScalarGridSpec(
            num_scalar_prefetch=1,
            grid=(1,),
            in_specs=[whole(a) for a in args],
            out_specs=[whole(tokens)] * 2,
        ),
        out_shape=[
            jax.ShapeDtypeStruct(tokens.shape, F32),
            jax.ShapeDtypeStruct(tokens.shape, BF),
        ],
        compiler_params=pltpu.CompilerParams(vmem_limit_bytes=VMEM),
        cost_estimate=pl.CostEstimate(
            flops=2 * tokens.size * tokens.shape[1],
            bytes_accessed=8 * tokens.size + 2 * tokens.shape[1] ** 2,
            transcendentals=tokens.shape[0],
        ),
        name="home_forward",
    )(place, *args)


def turn_kernel(copies, term_count, place, *refs):
    terms, refs = refs[:term_count], refs[term_count:]
    middle_ref, second_ref, grad, routes, side, *weights = refs[:-3]
    d_middle_out, sent, small = refs[-3:]
    shards = len(weights)
    heads = HK // shards
    width = middle_ref.shape[1]
    back = terms[0][...].astype(F32)
    for term in terms[1:]:
        back = back + term[...].astype(F32)
    middle, second = middle_ref[...], second_ref[...]
    d_gates = back[:, width : width + EXTRA]
    ids = iota(d_gates.shape, 1)
    d_gates = d_gates + back[:, width + EXPERTS : width + EXPERTS + EXTRA]
    picked = (ids == routes[:, 0:1]) | (ids == routes[:, 1:2])
    logits = jnp.where(picked, dot_t(second, side[...]), MASK_NEG)
    gates = jnp.where(picked, jnp.exp(logits - jnp.max(logits, axis=1, keepdims=True)), 0.0)
    gates = gates / jnp.sum(gates, axis=1, keepdims=True)
    d_gates = jnp.where(picked, d_gates, 0.0)
    d_picked = gates * (d_gates - jnp.sum(gates * d_gates, axis=1, keepdims=True))
    d_logits = d_picked.astype(BF)
    d_second = dot(d_logits, side[...]) + back[:, :width]
    factor = rms_factor(middle)
    small[...] = t_dot(d_logits, second)
    small[EXPERTS : EXPERTS + 1, :] = jnp.sum(d_second * middle * factor, axis=0, keepdims=True)
    gain = side[EXPERTS + 1 : EXPERTS + 2, :].astype(F32)
    d_middle = grad[...].astype(F32) + rms_input_grad(middle, factor, gain, d_second)
    d_middle_out[...] = d_middle
    d_proj = d_middle.astype(BF)
    for r, weight in enumerate(weights):
        d_heads = dot_t(d_proj, weight[...]).astype(BF)
        for h in range(heads):
            for i in range(copies):
                spot = ((place[1] ^ r) * heads + h) * copies + i
                sent[spot, :, :HEAD] = d_heads[:, h * HEAD : (h + 1) * HEAD]
    chunk = sent.shape[2] - HEAD
    for span in range(sent.shape[0]):
        sent[span, :, HEAD:] = d_proj[:, span * chunk : (span + 1) * chunk]


def home_turn(place, terms, middle, second, grad, routes, side, weights, spans):
    args = (*terms, middle, second, grad, routes, side, *weights)
    tokens, width = middle.shape
    shapes = [
        jax.ShapeDtypeStruct((tokens, width), F32),
        jax.ShapeDtypeStruct((spans, tokens, HEAD + width // spans), BF),
        jax.ShapeDtypeStruct((EXTRA, width), F32),
    ]
    return pl.pallas_call(
        functools.partial(turn_kernel, spans // HK, len(terms)),
        grid_spec=pltpu.PrefetchScalarGridSpec(
            num_scalar_prefetch=1,
            grid=(1,),
            in_specs=[whole(a) for a in args],
            out_specs=[whole(shape) for shape in shapes],
        ),
        out_shape=shapes,
        compiler_params=pltpu.CompilerParams(vmem_limit_bytes=VMEM),
        cost_estimate=pl.CostEstimate(
            flops=2 * tokens * width * width,
            bytes_accessed=24 * tokens * width + 2 * width * width,
            transcendentals=tokens,
        ),
        name="home_turn",
    )(place, *args)


def stream_grad_kernel(
    copies, place, starts, pieces0, pieces1, pieces2, pieces3, sent, mixed, attended, log_norm,
    normed, small, d_mixed, out, everyones, d_kv, sems
):
    here, shard = place[0], place[1]
    length, width = normed.shape
    spans = everyones.shape[0]
    tokens = length // spans
    shards = out.shape[0]
    shard_rows = width // shards
    heads = HK // shards
    copying = place_pieces(here, (pieces0, pieces1, pieces2, pieces3), everyones, sems)
    d_kv[...] = jnp.zeros_like(d_kv)
    for first in range(0, length, QUERIES):
        keys = first + QUERIES
        at = slice(first, keys)
        allowed = visible(starts, here, copies, tokens, first, QUERIES, keys)
        k, v = mixed[:keys, HEAD : HEAD + HD], mixed[:keys, HEAD + HD :]
        for g in range(GROUP):
            columns = slice(g * HD, (g + 1) * HD)
            q, grad = mixed[at, columns], sent[at, columns]
            delta = jnp.sum(grad.astype(F32) * attended[at, columns], axis=1, keepdims=True)
            scores = dot_t(q, k) * SCALE
            probs = jnp.where(allowed, jnp.exp(scores - log_norm[at, g : g + 1]), 0.0)
            d_scores = (probs * (dot_t(grad, v) - delta)).astype(BF)
            d_mixed[at, columns] = (dot(d_scores, k) * SCALE).astype(BF)
            d_kv[0, :keys, :] += t_dot(d_scores, q)
            d_kv[1, :keys, :] += t_dot(probs.astype(BF), grad)
    d_mixed[:, HEAD : HEAD + HD] = (d_kv[0] * SCALE).astype(BF)
    d_mixed[:, HEAD + HD :] = d_kv[1].astype(BF)
    for copy in copying:
        copy.wait()
    d_proj = sent[:, HEAD:]
    low = small[...].astype(BF)
    for f in range(shards):
        spot = shard ^ f
        columns = slice(f * shard_rows, (f + 1) * shard_rows)
        out[spot, :shard_rows, :HEAD_COLS] = t_dot(normed[:, columns], d_mixed[...]).astype(BF)
        for h in range(heads):
            first = (f * heads + h) * copies
            part = everyones[first]
            for i in range(1, copies):
                part = part + everyones[first + i]
            out[spot, h * HEAD : (h + 1) * HEAD, HEAD_COLS:] = t_dot(part, d_proj).astype(BF)
        out[spot, shard_rows:, :] = jnp.zeros((EXTRA, out.shape[2]), BF)
        out[spot, shard_rows:, :shard_rows] = low[:, columns]


def stream_backward(place, starts, pieces, sent, mixed, attended, log_norm, normed, small, shards):
    args = (sent, mixed, attended, log_norm, normed, small)
    length, width = normed.shape
    spans = 2 * pieces[0].shape[0]
    shapes = [
        jax.ShapeDtypeStruct(mixed.shape, BF),
        jax.ShapeDtypeStruct(
            (shards, width // shards + EXTRA, HEAD_COLS + width // spans), BF
        ),
    ]
    return pl.pallas_call(
        functools.partial(stream_grad_kernel, spans // HK),
        grid_spec=pltpu.PrefetchScalarGridSpec(
            num_scalar_prefetch=2,
            grid=(1,),
            in_specs=[anywhere()] * 4 + [whole(a) for a in args],
            out_specs=[whole(shape) for shape in shapes],
            scratch_shapes=[
                pltpu.VMEM((spans, length, HEAD), BF),
                pltpu.VMEM((2, length, HD), F32),
                pltpu.SemaphoreType.DMA((4, spans // 2)),
            ],
        ),
        out_shape=shapes,
        compiler_params=pltpu.CompilerParams(vmem_limit_bytes=VMEM),
        cost_estimate=pl.CostEstimate(
            flops=2 * length * width * (HEAD_COLS + width // spans) + 10 * length * length * HEAD,
            bytes_accessed=8 * length * width,
            transcendentals=GROUP * length * length,
        ),
        name="stream_backward",
    )(place, starts, *pieces, *args)


def home_grad_kernel(copies, place, d_home, tokens, side, d_middle, *refs):
    weight_refs, (d_tokens, weight, mixed, d_normed, sems) = refs[:-5], refs[-5:]
    shards = len(weight_refs)
    loading = [
        pltpu.make_async_copy(ref, weight.at[place[1] ^ r], sems.at[r])
        for r, ref in enumerate(weight_refs)
    ]
    for copy in loading:
        copy.start()
    for head in range(HK):
        part = d_home[head * copies]
        if copies > 1:
            part = part.astype(F32)
            for i in range(1, copies):
                part = part + d_home[head * copies + i].astype(F32)
            part = part.astype(BF)
        mixed[:, head * HEAD : (head + 1) * HEAD] = part[:, :HEAD]
        key = Q_COLS + head * HD
        mixed[:, key : key + HD] = part[:, HEAD : HEAD + HD]
        value = key + K_COLS
        mixed[:, value : value + HD] = part[:, HEAD + HD :]
    for copy in loading:
        copy.wait()
    rows = weight.shape[1]
    for f in range(shards):
        d_normed[:, f * rows : (f + 1) * rows] = dot_t(mixed[...], weight[f])
    x = tokens[...].astype(F32)
    gain = side[EXPERTS : EXPERTS + 1, :].astype(F32)
    d_x = rms_input_grad(x, rms_factor(x), gain, d_normed[...])
    d_tokens[...] = (d_middle[...] + d_x).astype(BF)


def home_backward(place, d_home, tokens, side, d_middle, weights, copies):
    args = (d_home, tokens, side, d_middle)
    count, width = tokens.shape
    shards = len(weights)
    columns = Q_COLS + 2 * K_COLS
    return pl.pallas_call(
        functools.partial(home_grad_kernel, copies),
        grid_spec=pltpu.PrefetchScalarGridSpec(
            num_scalar_prefetch=1,
            grid=(1,),
            in_specs=[whole(a) for a in args] + [anywhere()] * shards,
            out_specs=whole(tokens),
            scratch_shapes=[
                pltpu.VMEM((shards, width // shards, columns), BF),
                pltpu.VMEM((count, columns), BF),
                pltpu.VMEM((count, width), F32),
                pltpu.SemaphoreType.DMA((shards,)),
            ],
        ),
        out_shape=jax.ShapeDtypeStruct(tokens.shape, BF),
        compiler_params=pltpu.CompilerParams(vmem_limit_bytes=VMEM),
        cost_estimate=pl.CostEstimate(
            flops=2 * count * width * columns,
            bytes_accessed=2 * width * columns + 12 * count * width,
            transcendentals=count,
        ),
        name="home_backward",
    )(place, *args, *weights)


def collect_kernel(copies, late, own_weight, d_qkv, d_out, small, d_gain):
    rows = own_weight.shape[0]
    chunk = late.shape[2] - HEAD_COLS
    for head in range(HK):
        part = late[head * copies, :rows, :HEAD_COLS].astype(F32)
        for i in range(1, copies):
            part = part + late[head * copies + i, :rows, :HEAD_COLS].astype(F32)
        d_qkv[:, head * HEAD : (head + 1) * HEAD] = part[:, :HEAD]
        key = Q_COLS + head * HD
        d_qkv[:, key : key + HD] = part[:, HEAD : HEAD + HD]
        value = key + K_COLS
        d_qkv[:, value : value + HD] = part[:, HEAD + HD :]
    total = jnp.zeros((EXTRA, rows), F32)
    for span in range(late.shape[0]):
        d_out[:, span * chunk : (span + 1) * chunk] = late[span, :rows, HEAD_COLS:].astype(F32)
        total = total + late[span, rows:, :rows].astype(F32)
    small[...] = total
    d_gain[...] = jnp.sum(d_qkv[...] * own_weight[...].astype(F32), axis=1, keepdims=True)


def collected(late, own_weight, width, copies):
    rows, columns = own_weight.shape
    shapes = [
        jax.ShapeDtypeStruct((rows, columns), F32),
        jax.ShapeDtypeStruct((rows, width), F32),
        jax.ShapeDtypeStruct((EXTRA, rows), F32),
        jax.ShapeDtypeStruct((rows, 1), F32),
    ]
    return pl.pallas_call(
        functools.partial(collect_kernel, copies),
        grid=(1,),
        in_specs=[whole(late), whole(own_weight)],
        out_specs=[whole(shape) for shape in shapes],
        out_shape=shapes,
        compiler_params=pltpu.CompilerParams(vmem_limit_bytes=VMEM),
        name="collected",
    )(late, own_weight)


def picked_gates(second, router_t, chosen):
    logits = dot_t(router_t, second)
    ids = iota(logits.shape, 0)
    picked = (ids == chosen[0:1, :]) | (ids == chosen[1:2, :])
    logits = jnp.where(picked, logits, MASK_NEG)
    parts = jnp.where(picked, jnp.exp(logits - jnp.max(logits, axis=0, keepdims=True)), 0.0)
    return picked, parts / jnp.sum(parts, axis=0, keepdims=True)


def swiglu_grads(gate, up, d_hidden):
    sigma = 1.0 / (1.0 + jnp.exp(-gate))
    passed = gate * sigma
    d_gate = d_hidden * up * sigma * (1.0 + gate * (1.0 - sigma))
    return (passed * up).astype(BF), d_gate.astype(BF), (d_hidden * passed).astype(BF)


def near_kernel(shards, place, *refs):
    second, grads = refs[:shards], refs[shards : 2 * shards]
    router_t, w_gate, w_up, w_down = refs[2 * shards : 2 * shards + 4]
    branch_out = refs[2 * shards + 4 : 3 * shards + 4]
    back_out = refs[3 * shards + 4 : 4 * shards + 4]
    hot, rows, cots, d_outs, slot_gate, out_acc, row_acc, branch_acc, back_acc = refs[
        4 * shards + 4 :
    ]
    expert, tile = pl.program_id(0), pl.program_id(1)
    tokens = second[0].shape[0]
    width = second[0].shape[1]
    wanted = place[1] * pl.num_programs(0) + expert

    @pl.when(tile == 0)
    def _():
        before = (iota((tokens, tokens), 0) < iota((tokens, tokens), 1)).astype(BF)
        for f in range(shards):
            chosen = grads[f][tokens : tokens + EXTRA, :tokens].astype(F32).astype(jnp.int32)
            picked, gates = picked_gates(second[f][...], router_t[...], chosen)
            ranks = dot(picked.astype(BF), before)
            found = (iota(ranks.shape, 0) == wanted) & picked
            rank = jnp.sum(jnp.where(found, ranks + 1.0, 0.0), axis=0, keepdims=True)
            gate = jnp.sum(jnp.where(found, gates, 0.0), axis=0, keepdims=True)
            match = iota((CAP, tokens), 0).astype(F32) + 1.0 == rank
            one_hot = match.astype(BF)
            place = pl.ds(f * CAP, CAP)
            hot[f] = one_hot
            found_gate = jnp.sum(jnp.where(match, gate, 0.0), axis=1, keepdims=True)
            slot_gate[place, :] = jnp.broadcast_to(found_gate, (CAP, LANES))
            rows[place, :] = dot(one_hot, second[f][...]).astype(BF)
            cot = dot(one_hot, grads[f][:tokens, :])
            cots[place, :] = cot.astype(BF)
            d_outs[place, :] = (found_gate * cot).astype(BF)
        out_acc[...] = jnp.zeros_like(out_acc)
        row_acc[...] = jnp.zeros_like(row_acc)

    hidden, d_gate, d_up = swiglu_grads(
        dot(rows[...], w_gate[0]), dot(rows[...], w_up[0]), dot(d_outs[...], w_down[0])
    )
    out_acc[...] += dot_t(hidden, w_down[0])
    row_acc[...] += dot_t(d_gate, w_gate[0]) + dot_t(d_up, w_up[0])

    @pl.when(tile == pl.num_programs(1) - 1)
    def _():
        last = expert == pl.num_programs(0) - 1
        for f in range(shards):
            place = pl.ds(f * CAP, CAP)
            out = out_acc[place, :].astype(BF).astype(F32)
            d_gates = jnp.sum(cots[place, :].astype(F32) * out, axis=1, keepdims=True)
            gated = (slot_gate[place, 0:1] * out).astype(BF)
            lane = iota((CAP, LANES), 1)
            coarse = d_gates.astype(BF).astype(F32)
            extra = jnp.where(lane == wanted, coarse, 0.0)
            extra = extra + jnp.where(lane == EXPERTS + wanted, d_gates - coarse, 0.0)

            def add(acc, part, columns):
                @pl.when(expert == 0)
                def _():
                    acc[f, :, columns] = part

                @pl.when(expert > 0)
                def _():
                    acc[f, :, columns] += part

            add(branch_acc, t_dot(hot[f], gated), slice(0, width))
            add(back_acc, t_dot(hot[f], row_acc[place, :].astype(BF)), slice(0, width))
            add(back_acc, t_dot(hot[f], extra.astype(BF)), slice(width, width + LANES))

            @pl.when(last)
            def _():
                branch_out[f][...] = branch_acc[f].astype(BF)
                back_out[f][...] = back_acc[f].astype(BF)


def near_experts(place, second, grads, router_t, w_experts):
    shards = len(second)
    tokens, width = second[0].shape
    experts = w_experts.shape[0]
    slots = shards * CAP
    tiles = FF // TILE
    shapes = [jax.ShapeDtypeStruct((tokens, width), BF)] * shards
    shapes += [jax.ShapeDtypeStruct((tokens, width + LANES), BF)] * shards

    def weight(part):
        return pl.BlockSpec((1, width, TILE), lambda e, j, s: (e, 0, part * tiles + j))

    outs = pl.pallas_call(
        functools.partial(near_kernel, shards),
        grid_spec=pltpu.PrefetchScalarGridSpec(
            num_scalar_prefetch=1,
            grid=(experts, tiles),
            in_specs=[whole(a) for a in (*second, *grads, router_t)]
            + [weight(0), weight(1), weight(2)],
            out_specs=[whole(shape) for shape in shapes],
            scratch_shapes=[
                pltpu.VMEM((shards, CAP, tokens), BF),
                pltpu.VMEM((slots, width), BF),
                pltpu.VMEM((slots, width), BF),
                pltpu.VMEM((slots, width), BF),
                pltpu.VMEM((slots, LANES), F32),
                pltpu.VMEM((slots, width), F32),
                pltpu.VMEM((slots, width), F32),
                pltpu.VMEM((shards, tokens, width), F32),
                pltpu.VMEM((shards, tokens, width + LANES), F32),
            ],
        ),
        out_shape=shapes,
        compiler_params=pltpu.CompilerParams(vmem_limit_bytes=VMEM),
        cost_estimate=pl.CostEstimate(
            flops=12 * experts * slots * width * FF,
            bytes_accessed=w_experts.size * 2,
            transcendentals=experts * slots * FF,
        ),
        name="near_experts",
    )(place, *second, *grads, router_t, w_experts, w_experts, w_experts)
    return outs[:shards], outs[shards:]


def far_kernel(
    place,
    router_t,
    second_ref,
    grads_ref,
    w_gate,
    w_up,
    w_down,
    out_ref,
    rows,
    d_outs,
    act,
    fetched_rows,
    fetched_grads,
    tile_out,
    counts,
    fetch_sem,
    store_sem,
):
    experts = rows.shape[0]
    expert, tile = pl.program_id(0), pl.program_id(1)
    tiles = pl.num_programs(1)
    step = expert * tiles + tile
    slot = lax.rem(step, 2)
    groups = second_ref.shape[0] // JOINED
    tokens, width = second_ref.shape[1:]
    size = JOINED * tokens
    window = JOINED * CAP + 16

    def stores(which, e, j):
        return [
            pltpu.make_async_copy(
                tile_out.at[which, i],
                out_ref.at[e, :, pl.ds(pl.multiple_of(i * FF + j * TILE, TILE), TILE)],
                store_sem.at[which, i],
            )
            for i in range(3)
        ]

    def fetches(which, g):
        at = pl.ds(g * JOINED, JOINED)
        return [
            pltpu.make_async_copy(ref.at[at], buffer.at[which], fetch_sem.at[which, i])
            for i, (ref, buffer) in enumerate(
                ((second_ref, fetched_rows), (grads_ref, fetched_grads))
            )
        ]

    @pl.when(step == 0)
    def _():
        for copy in fetches(0, 0):
            copy.start()
        before = (iota((size, size), 0) < iota((size, size), 1)).astype(BF)

        def gather(g, starts):
            which = lax.rem(g, 2)
            for copy in fetches(which, g):
                copy.wait()

            @pl.when(g + 1 < groups)
            def _():
                for copy in fetches(1 - which, g + 1):
                    copy.start()

            second = fetched_rows[which].reshape(size, width)
            grads = fetched_grads[which, :, :tokens].reshape(size, width)
            chosen = jnp.concatenate(
                [fetched_grads[which, b, tokens : tokens + EXTRA, :LANES] for b in range(JOINED)],
                axis=1,
            )
            chosen = chosen.astype(F32).astype(jnp.int32)
            picked, gates = picked_gates(second, router_t[...], chosen)
            ranks = dot(picked.astype(BF), before)
            ids = iota(ranks.shape, 0)
            bases = [start // 16 * 16 for start in starts]
            matches, found_gates, ends = [], [], []
            for e in range(experts):
                found = (ids == place[1] * experts + e) & picked
                gate = jnp.sum(jnp.where(found, gates, 0.0), axis=0, keepdims=True)
                rank = jnp.sum(jnp.where(found, ranks + 1.0, 0.0), axis=0, keepdims=True)
                shift = (starts[e] - bases[e]).astype(F32)
                spot = jnp.where(rank > 0.0, rank + (shift - 1.0), -1.0)
                match = iota((window, size), 0).astype(F32) == spot
                matches.append(match.astype(BF))
                found_gates.append(
                    jnp.sum(jnp.where(match, gate, 0.0), axis=1, keepdims=True)
                )
                ends.append(starts[e] + jnp.sum((rank > 0.0).astype(jnp.int32)))
            one_hot = jnp.concatenate(matches, axis=0)
            new_rows = dot(one_hot, second).astype(BF)
            new_grads = (jnp.concatenate(found_gates, axis=0) * dot(one_hot, grads)).astype(BF)
            for e in range(experts):
                at = pl.ds(pl.multiple_of(bases[e], 16), 16)
                rest = pl.ds(pl.multiple_of(bases[e] + 16, 16), window - 16)
                held = iota((16, width), 0) < starts[e] - bases[e]
                for ref, new in ((rows, new_rows), (d_outs, new_grads)):
                    new = new[e * window : (e + 1) * window]
                    ref[e, at, :] = jnp.where(held, ref[e, at, :], new[:16])
                    ref[e, rest, :] = new[16:]
            return tuple(ends)

        ends = lax.fori_loop(0, groups, gather, (jnp.int32(0),) * experts)
        for e in range(experts):
            counts[e] = ends[e]
            spare = pl.ds(pl.multiple_of((ends[e] + 15) // 16 * 16, 16), CHUNK)
            rows[e, spare, :] = jnp.zeros((CHUNK, width), BF)
            d_outs[e, spare, :] = jnp.zeros((CHUNK, width), BF)

    chunks = jnp.maximum((counts[expert] + CHUNK - 1) // CHUNK, 1)

    @pl.loop(0, chunks)
    def _(i):
        at = pl.ds(pl.multiple_of(i * CHUNK, CHUNK), CHUNK)
        row, d_out = rows[expert, at, :], d_outs[expert, at, :]
        hidden, d_gate, d_up = swiglu_grads(
            dot(row, w_gate[0]), dot(row, w_up[0]), dot(d_out, w_down[0])
        )
        act[0, at, :] = d_gate
        act[1, at, :] = d_up
        act[2, at, :] = hidden

    @pl.when(step >= 2)
    def _():
        for copy in stores(slot, (step - 2) // tiles, lax.rem(step - 2, tiles)):
            copy.wait()

    most = act.shape[1] // CHUNK
    depths = [k for k in DEPTHS if k < most] + [most]
    for low, k in zip([0] + depths[:-1], depths):

        @pl.when((chunks > low) & (chunks <= k))
        def _():
            for extra in range(low + 1, k):

                @pl.when(chunks == extra)
                def _():
                    spare = slice(extra * CHUNK, k * CHUNK)
                    empty = jnp.zeros(((k - extra) * CHUNK, width), BF)
                    rows[expert, spare, :] = empty
                    d_outs[expert, spare, :] = empty
                    for i in range(3):
                        act[i, spare, :] = empty[:, :TILE]

            upto = k * CHUNK
            for i, left in enumerate((rows, rows, d_outs)):
                tile_out[slot, i] = t_dot(left[expert, :upto, :], act[i, :upto, :])

    for copy in stores(slot, expert, tile):
        copy.start()

    @pl.when(step == pl.num_programs(0) * tiles - 1)
    def _():
        for copy in stores(1 - slot, (step - 1) // tiles, lax.rem(step - 1, tiles)):
            copy.wait()
        for copy in stores(slot, expert, tile):
            copy.wait()


def far_weight_grads(place, router_t, second, grads, w_experts):
    experts, width = w_experts.shape[:2]
    blocks, tokens = second.shape[:2]
    tiles = FF // TILE
    most = blocks * CAP
    held = most + CHUNK + 16

    def weight(part):
        return pl.BlockSpec((1, width, TILE), lambda e, j, s: (e, 0, part * tiles + j))

    return pl.pallas_call(
        far_kernel,
        grid_spec=pltpu.PrefetchScalarGridSpec(
            num_scalar_prefetch=1,
            grid=(experts, tiles),
            in_specs=[
                whole(router_t),
                anywhere(),
                anywhere(),
                weight(0),
                weight(1),
                weight(2),
            ],
            out_specs=anywhere(),
            scratch_shapes=[
                pltpu.VMEM((experts, held, width), BF),
                pltpu.VMEM((experts, held, width), BF),
                pltpu.VMEM((3, most, TILE), BF),
                pltpu.VMEM((2, JOINED, tokens, width), BF),
                pltpu.VMEM((2, JOINED, tokens + EXTRA, width), BF),
                pltpu.VMEM((2, 3, width, TILE), F32),
                pltpu.SMEM((experts,), jnp.int32),
                pltpu.SemaphoreType.DMA((2, 2)),
                pltpu.SemaphoreType.DMA((2, 3)),
            ],
        ),
        out_shape=jax.ShapeDtypeStruct((experts, width, 3 * FF), F32),
        compiler_params=pltpu.CompilerParams(vmem_limit_bytes=VMEM),
        cost_estimate=pl.CostEstimate(
            flops=8 * experts * most * width * FF,
            bytes_accessed=w_experts.size * 6 + 4 * blocks * tokens * width,
            transcendentals=experts * most * FF,
        ),
        name="far_weight_grads",
    )(place, router_t, second, grads, w_experts, w_experts, w_experts)


def per_device(
    tokens,
    query_key_value_weight,
    output_weight,
    routing_weight,
    gain_attn,
    gain_moe,
    w_experts,
    doc_starts,
    routes,
    cotangent,
):
    spans = lax.axis_size("ctx")
    shards = lax.axis_size("fsdp")
    here = lax.axis_index("ctx")
    shard = lax.axis_index("fsdp")
    place = jnp.stack([here, shard]).astype(jnp.int32)
    x, grad = tokens[0], cotangent[0]
    tok_count, width = x.shape
    shard_rows = query_key_value_weight.shape[0]
    copies = spans // HK
    head = here // copies
    length = spans * tok_count
    blocks = spans * shards

    side = jnp.concatenate(
        [
            routing_weight.T,
            gain_attn[None],
            gain_moe[None],
            jnp.zeros((EXTRA - EXPERTS - 2, shard_rows), BF),
        ]
    )
    head_w = jnp.concatenate(
        [
            lax.dynamic_slice_in_dim(query_key_value_weight, head * HEAD, HEAD, 1),
            lax.dynamic_slice_in_dim(query_key_value_weight, Q_COLS + head * HD, HD, 1),
            lax.dynamic_slice_in_dim(query_key_value_weight, Q_COLS + K_COLS + head * HD, HD, 1),
        ],
        axis=1,
    )
    side = jnp.stack(near_blocks(side))
    side = jnp.take(side, jnp.arange(shards, dtype=jnp.int32) ^ shard, axis=0)
    side = side.swapaxes(0, 1).reshape(EXTRA, width)
    head_w = near_blocks(head_w)
    pieces = span_pieces(x)

    payload = jnp.concatenate(
        [grad, jnp.pad(routes[0].T.astype(BF), ((0, EXTRA - 2), (0, width - tok_count)))]
    )
    payload, output_weight = after((payload, output_weight), pieces)
    out_w = near_blocks(output_weight)
    grads_near = near_blocks(payload)
    grads_line = line_blocks(payload)
    grads_all = all_blocks(grads_line)

    normed, mixed, attended_low, attended, log_norm = stream_attention(
        place, doc_starts[0], pieces, head_w, side, copies
    )

    attended_low, grads_line = after((attended_low, grads_line), grads_near)
    own = to_all(attended_low, "ctx").reshape(spans, tok_count, HEAD)
    middle, second = home_forward(place, own, x, side, out_w, copies)
    second_near = near_blocks(second)
    second_line = line_blocks(second)
    second_all = all_blocks(second_line)

    branch, back = near_experts(place, second_near, grads_near, side, w_experts)
    back = after(back, second_line)
    later_qkv, attended_low = after((query_key_value_weight, attended_low), back)
    qkv_w = near_blocks(later_qkv)
    attended_pieces = span_pieces(attended_low)
    terms = after(near_terms(back), grads_all)
    branch_terms = near_terms(branch)
    output = sum((term.astype(F32) for term in branch_terms), middle).astype(BF)

    d_middle, sent, small = home_turn(
        place, terms, middle, second, grad, routes[0], side, out_w, spans
    )

    sent = to_all(sent.reshape(length, -1), "ctx")
    d_mixed, grads_out = stream_backward(
        place, doc_starts[0], attended_pieces, sent, mixed, attended, log_norm, normed, small, shards
    )
    late = near_terms([grads_out[r] for r in range(shards)])
    late = sum((term.astype(F32) for term in late[1:]), late[0].astype(F32)).astype(BF)
    late = lax.all_gather(after(late, second_all), "ctx", axis=0)

    d_home = to_all(d_mixed, "ctx").reshape(spans, tok_count, HEAD_COLS)
    d_tokens = home_backward(place, d_home, x, side, d_middle, qkv_w, copies)

    second_all = second_all.reshape(blocks, tok_count, width)
    grads_all = grads_all.reshape(blocks, tok_count + EXTRA, width)
    segment = min(blocks, SEGMENT)
    parts = [
        far_weight_grads(
            place, side, second_all[i : i + segment], grads_all[i : i + segment], w_experts
        )
        for i in range(0, blocks, segment)
    ]
    d_w_experts = sum(parts[1:], parts[0])

    d_qkv_w, d_out_w, small, d_gain_attn = collected(
        late, query_key_value_weight, width, copies
    )
    return (
        output[None],
        d_tokens[None],
        d_qkv_w,
        d_out_w,
        small[:EXPERTS].T,
        d_gain_attn[:, 0] / gain_attn.astype(F32),
        small[EXPERTS],
        d_w_experts,
    )


def solution(mesh):
    placed = (
        P("fsdp", "ctx", None),
        P("fsdp", None),
        P("fsdp", None),
        P("fsdp", None),
        P("fsdp"),
        P("fsdp"),
        P("fsdp", None, None),
        P("fsdp", None),
        P("fsdp", "ctx", None),
        P("fsdp", "ctx", None),
    )
    return jax.shard_map(
        per_device,
        mesh=mesh,
        in_specs=placed,
        out_specs=(
            P("fsdp", "ctx", None),
            P("fsdp", "ctx", None),
            P("fsdp", None),
            P("fsdp", None),
            P("fsdp", None),
            P("fsdp"),
            P("fsdp"),
            P("fsdp", None, None),
        ),
        check_vma=False,
    )
```

time: 767 us -> 649 us (0.85)
  the two profiles are of different devices: /device:TPU:0 before, /device:TPU:1 now
where the time goes in v4:
time: 649 us; the launch traced here: 640 us
  waiting for transfers between devices  295 us (45%)
  Pallas kernels  182 us (28%)
  starting transfers between devices  93.7 us (14%)
  local copies, waits for them, and re-layouts  22.2 us (3%)
  blocking collectives  16.8 us (3%)
  other arithmetic  15.1 us (2%)
  between operations  14.4 us (2%)
    ppermute x49, waiting for transfers between devices, exchanged(): return lax.ppermute(value, axis, [(i, i ^ distance) for i in range(count)])  295 us
    pallas_call x1, Pallas kernels, far_weight_grads(): pl.pallas_call(far_kernel, grid_spec=pltpu.PrefetchScalarGridSpec(num_sca...  90.9 us
    ppermute x49, starting transfers between devices, exchanged(): return lax.ppermute(value, axis, [(i, i ^ distance) for i in range(count)])  77.3 us
    pallas_call x1, Pallas kernels, near_experts(): pl.pallas_call(functools.partial(near_kernel, shards), grid_spec=pltpu.Pr...  28.5 us
    pallas_call x1, Pallas kernels, stream_backward(): pl.pallas_call(functools.partial(stream_grad_kernel, spans // HK), grid_s...  17.9 us
    pallas_call x1, Pallas kernels, stream_attention(): pl.pallas_call(functools.partial(stream_kernel, copies), grid_spec=pltpu....  16.9 us
    all_to_all x1, blocking collectives, to_all(): return lax.all_to_all(value, axis, 0, 0, tiled=True)  16.8 us
    all_to_all x2, starting transfers between devices, to_all(): return lax.all_to_all(value, axis, 0, 0, tiled=True)  16.2 us
  transfers between devices with their start and end apart: 54, of which 21 were waited for; matrix products, arithmetic and copies ran while one was open for 4% of the time, Pallas kernels for 27%

profile of v4, /device:TPU:1, one launch (start us, length us, event | category | flops | bytes accessed | tf_op | source)
XLA Modules:
  0.0 640.0 jit_solution(12621265198327743111)
XLA Ops:
  8.3 4.2 collective-permute-start.5
  12.9 3.2 collective-permute-start.2
  17.2 7.7 %collective-permute-start = (bf16[64,1536]{1,0:T(8,128)(2,1)S(1)}, bf16[64,1536]{1,0:T(8,128)(2,1)S(1)}, u32[]{:S(2)}, u32[]{:S(2)}) collective-permute-start(bf16[64,1536]{1,0:T(8,128)(2,1)S(1)} %get-tuple-element.91), channel_id=1, source_target_pairs={{0,8},{4,12},{8,0},{12,4},{16,24},{20,28},{24,16},{28,20},{1,9},{5... | collective-permute-start | bytes 589832 | tf_op jit(solution)/shard_map/ppermute | solution.py:70
  24.9 12.4 %collective-permute-done.4 = bf16[64,1536]{1,0:T(8,128)(2,1)S(1)} collective-permute-done((bf16[64,1536]{1,0:T(8,128)(2,1)S(1)}, bf16[64,1536]{1,0:T(8,128)(2,1)S(1)}, u32[]{:S(2)}, u32[]{:S(2)}) %collective-permute-start.4) | collective-permute-done | bytes 196640 | tf_op jit(solution)/shard_map/ppermute | solution.py:70
  38.7 7.0 %collective-permute-done.1 = bf16[64,1536]{1,0:T(8,128)(2,1)S(1)} collective-permute-done((bf16[64,1536]{1,0:T(8,128)(2,1)S(1)}, bf16[64,1536]{1,0:T(8,128)(2,1)S(1)}, u32[]{:S(2)}, u32[]{:S(2)}) %collective-permute-start.1) | collective-permute-done | bytes 196640 | tf_op jit(solution)/shard_map/ppermute | solution.py:70
  45.8 1.3 collective-permute-start.6
  47.4 6.8 %collective-permute-done.7.refs_3_ = bf16[4,64,1536]{2,1,0:T(8,128)(2,1)S(1)} collective-permute-done((bf16[4,64,1536]{2,1,0:T(8,128)(2,1)S(1)}, bf16[4,64,1536]{2,1,0:T(8,128)(2,1)S(1)}, u32[]{:S(2)}, u32[]{:S(2)}) %collective-permute-start.7) | collective-permute-done | bytes 786464 | tf_op jit(solution)/shard_map/ppermute | solution.py:70
  54.2 17.0 %collective-permute-done.6.refs_2_ = bf16[4,64,1536]{2,1,0:T(8,128)(2,1)} collective-permute-done((bf16[4,64,1536]{2,1,0:T(8,128)(2,1)S(1)}, bf16[4,64,1536]{2,1,0:T(8,128)(2,1)}, u32[]{:S(2)}, u32[]{:S(2)}) %collective-permute-start.6) | collective-permute-done | bytes 786464 | tf_op jit(solution)/shard_map/ppermute | solution.py:70
  71.1 1.4 collective-permute-start.16
  72.6 2.1 collective-permute-start.14
  74.7 6.8 %collective-permute-done.16 = bf16[144,1536]{1,0:T(8,128)(2,1)S(1)} collective-permute-done((bf16[144,1536]{1,0:T(8,128)(2,1)S(1)}, bf16[144,1536]{1,0:T(8,128)(2,1)S(1)}, u32[]{:S(2)}, u32[]{:S(2)}) %collective-permute-start.16) | collective-permute-done | bytes 442400 | tf_op jit(solution)/shard_map/ppermute | solution.py:70
  81.5 23.9 %collective-permute-done.15 = bf16[144,1536]{1,0:T(8,128)(2,1)S(1)} collective-permute-done((bf16[144,1536]{1,0:T(8,128)(2,1)S(1)}, bf16[144,1536]{1,0:T(8,128)(2,1)S(1)}, u32[]{:S(2)}, u32[]{:S(2)}) %collective-permute-start.15) | collective-permute-done | bytes 442400 | tf_op jit(solution)/shard_map/ppermute | solution.py:70
  105.4 1.4 pad_maximum_fusion
  110.7 5.1 collective-permute-start.8
  118.5 47.7 %collective-permute-done.12 = bf16[16,384]{1,0:T(8,128)(2,1)S(1)} collective-permute-done((bf16[16,384]{1,0:T(8,128)(2,1)S(1)}, bf16[16,384]{1,0:T(8,128)(2,1)S(1)}, u32[]{:S(2)}, u32[]{:S(2)}) %collective-permute-start.12) | collective-permute-done | bytes 12320 | tf_op jit(solution)/shard_map/ppermute | solution.py:70
  166.2 10.9 %collective-permute-start.13 = (bf16[16,384]{1,0:T(8,128)(2,1)S(1)}, bf16[16,384]{1,0:T(8,128)(2,1)S(1)}, u32[]{:S(2)}, u32[]{:S(2)}) collective-permute-start(bf16[16,384]{1,0:T(8,128)(2,1)S(1)} %collective-permute-done.12), channel_id=1, source_target_pairs={{0,1},{1,0},{2,3},{3,2},{4,5},{5,4},{6,7},{7,6},{8,9},{9,8},{10,11... | collective-permute-start | bytes 36872 | tf_op jit(solution)/shard_map/ppermute | solution.py:70
  180.2 16.9 %stream_attention.1 = (bf16[1024,1536]{1,0:T(8,128)(2,1)}, bf16[1024,320]{1,0:T(8,128)(2,1)}, bf16[1024,192]{1,0:T(8,128)(2,1)}, f32[1024,192]{1,0:T(8,128)}, f32[1024,128]{1,0:T(8,128)}) custom-call(s32[2]{0:T(128)} %pad_add_fusion.place, s32[8]{0:T(128)} %bitcast.105, bf16[4,64,1536]{2,1,0:T(8,128)(2,1)} %copy-done.10, bf16[4,64,1536]{2,1,0:T(8,128)(2,1)} %copy-done.9, ...), custom_call_target="tpu_custom_call" | custom-call | flops 1811939328 | bytes 12582912 | tf_op jit(solution)/shard_map/stream_attention/pallas_call | solution.py:225
  197.1 2.0 copy.25
  199.1 16.8 %all_to_all.26 = bf16[8,128,192]{1,2,0:T(8,128)(2,1)S(1)} all-to-all(bf16[8,128,192]{1,2,0:T(8,128)(2,1)} %copy.25), channel_id=1, replica_groups=mesh['ctx'=8,'fsdp'=4] {'ctx'}, dimensions={0} | all-to-all | bytes 786432 | tf_op jit(solution)/shard_map/all_to_all | solution.py:65
  216.9 5.3 home_forward.1
  222.2 1.5 collective-permute-start.31
  224.0 1.8 collective-permute-start.29
  225.8 7.3 %collective-permute-done.31 = bf16[128,1536]{1,0:T(8,128)(2,1)S(1)} collective-permute-done((bf16[128,1536]{1,0:T(8,128)(2,1)}, bf16[128,1536]{1,0:T(8,128)(2,1)S(1)}, u32[]{:S(2)}, u32[]{:S(2)}) %collective-permute-start.31) | collective-permute-done | bytes 393248 | tf_op jit(solution)/shard_map/ppermute | solution.py:70
  233.1 24.4 %collective-permute-done.30 = bf16[128,1536]{1,0:T(8,128)(2,1)S(1)} collective-permute-done((bf16[128,1536]{1,0:T(8,128)(2,1)}, bf16[128,1536]{1,0:T(8,128)(2,1)S(1)}, u32[]{:S(2)}, u32[]{:S(2)}) %collective-permute-start.30) | collective-permute-done | bytes 393248 | tf_op jit(solution)/shard_map/ppermute | solution.py:70
  257.5 2.4 pad_maximum_fusion.1
  259.9 2.3 collective-permute-start.24
  262.2 2.3 collective-permute-start.23
  264.5 5.0 collective-permute-done.24.refs_2_
  269.6 2.7 collective-permute-start.25
  272.3 1.3 collective-permute-done.25.refs_3_
  274.4 28.5 %near_experts.1 = (bf16[128,1536]{1,0:T(8,128)(2,1)}, bf16[128,1536]{1,0:T(8,128)(2,1)}, bf16[128,1536]{1,0:T(8,128)(2,1)}, bf16[128,1536]{1,0:T(8,128)(2,1)}, b...) custom-call(s32[2]{0:T(128)} %pad_add_fusion.place, ...), custom_call_target="tpu_custom_call" | custom-call | flops 9663676416 | bytes 18874368 | tf_op jit(solution)/shard_map/near_experts/pallas_call | solution.py:656
  303.4 1.5 collective-permute-done.41
  305.9 1.5 collective-permute-start.42
  307.5 19.3 %collective-permute-done.42.refs_2_ = bf16[128,1664]{1,0:T(8,128)(2,1)S(1)} collective-permute-done((bf16[128,1664]{1,0:T(8,128)(2,1)S(1)}, bf16[128,1664]{1,0:T(8,128)(2,1)S(1)}, u32[]{:S(2)}, u32[]{:S(2)}) %collective-permute-start.42) | collective-permute-done | bytes 426016 | tf_op jit(solution)/shard_map/ppermute | solution.py:70
  327.5 7.4 %home_turn.1 = (f32[128,1536]{1,0:T(8,128)}, bf16[8,128,384]{2,1,0:T(8,128)(2,1)}, f32[16,1536]{1,0:T(8,128)}) custom-call(s32[2]{0:T(128)} %pad_add_fusion.place, bf16[128,1664]{1,0:T(8,128)(2,1)} %get-tuple-element.64.refs_0_, bf16[128,1664]{1,0:T(8,128)(2,1)} %copy-done.13, bf16[128,1664]{1,0:T(8,128)(2,1)} %copy-done.14, ...), custom_call_target="tpu_custom_call" | custom-call | flops 603979776 | bytes 9437184 | tf_op jit(solution)/shard_map/home_turn/pallas_call | solution.py:352
  335.0 4.3 all-to-all-start.1
  339.5 2.3 collective-permute-start.36
  343.1 1.3 collective-permute-start.33
  344.4 2.1 collective-permute-start.32
  346.5 34.6 %collective-permute-done.36 = bf16[512,192]{1,0:T(8,128)(2,1)S(1)} collective-permute-done((bf16[512,192]{1,0:T(8,128)(2,1)S(1)}, bf16[512,192]{1,0:T(8,128)(2,1)S(1)}, u32[]{:S(2)}, u32[]{:S(2)}) %collective-permute-start.36) | collective-permute-done | bytes 196640 | tf_op jit(solution)/shard_map/ppermute | solution.py:70
  381.1 1.7 collective-permute-start.34
  383.0 1.3 copy.28
  384.3 1.9 collective-permute-start.39
  386.2 11.8 %collective-permute-done.33 = bf16[512,192]{1,0:T(8,128)(2,1)} collective-permute-done((bf16[512,192]{1,0:T(8,128)(2,1)S(1)}, bf16[512,192]{1,0:T(8,128)(2,1)}, u32[]{:S(2)}, u32[]{:S(2)}) %collective-permute-start.33) | collective-permute-done | bytes 196640 | tf_op jit(solution)/shard_map/ppermute | solution.py:70
  398.0 2.3 pad_maximum_fusion.2.pieces0
  400.4 2.2 copy.27
  402.5 1.4 collective-permute-start.38
  404.0 2.2 copy.30.pieces3
  406.2 12.4 %collective-permute-done.38 = bf16[4,512,192]{1,2,0:T(8,128)(2,1)S(1)} collective-permute-done((bf16[4,512,192]{1,2,0:T(8,128)(2,1)}, bf16[4,512,192]{1,2,0:T(8,128)(2,1)S(1)}, u32[]{:S(2)}, u32[]{:S(2)}) %collective-permute-start.38) | collective-permute-done | bytes 786464 | tf_op jit(solution)/shard_map/ppermute | solution.py:70
  418.6 1.7 copy.29.pieces2
  420.3 17.9 %stream_backward.1 = (bf16[1024,320]{1,0:T(8,128)(2,1)}, bf16[4,400,512]{2,1,0:T(8,128)(2,1)}) custom-call(s32[2]{0:T(128)} %pad_add_fusion.place, s32[8]{0:T(128)} %bitcast.106, bf16[4,512,192]{2,1,0:T(8,128)(2,1)} %pad_maximum_fusion.2.pieces0, bf16[4,512,192]{2,1,0:T(8,128)(2,1)} %copy-done.2, bf16[4,512,192]{2,1,0:T(8,128)(2,1)} %copy.29.pieces2, ...), custom_call_target="tpu_custom_call" | custom-call | flops 3623878656 | bytes 12582912 | tf_op jit(solution)/shard_map/stream_backward/pallas_call | solution.py:429
  438.2 1.3 slice_bitcast_fusion.1
  439.5 4.2 collective-permute-start.47
  443.7 1.4 collective-permute-start.44
  448.5 48.4 %collective-permute-done.48 = bf16[400,512]{1,0:T(8,128)(2,1)S(1)} collective-permute-done((bf16[400,512]{1,0:T(8,128)(2,1)S(1)}, bf16[400,512]{1,0:T(8,128)(2,1)S(1)}, u32[]{:S(2)}, u32[]{:S(2)}) %collective-permute-start.48) | collective-permute-done | bytes 409632 | tf_op jit(solution)/shard_map/ppermute | solution.py:70
  497.8 1.4 collective-permute-start.43
  499.2 6.2 collective-permute-done.28
  505.4 2.1 fusion.5
  509.5 11.9 %all-to-all-start.2 = ((bf16[8,128,320]{1,2,0:T(8,128)(2,1)}), bf16[8,128,320]{1,2,0:T(8,128)(2,1)S(1)}, u32[]{:S(2)}, u32[]{:S(2)}) async-start(bf16[8,128,320]{1,2,0:T(8,128)(2,1)} %copy.31), calls=%async_computation.2 | async-start | bytes 1310720 | tf_op jit(solution)/shard_map/all_to_all | solution.py:65
  521.4 90.9 %far_weight_grads.1 = f32[2,1536,3072]{2,1,0:T(8,128)} custom-call(s32[2]{0:T(128)} %pad_add_fusion.place, bf16[16,1536]{1,0:T(8,128)(2,1)} %bitcast.80, bf16[32,128,1536]{2,1,0:T(8,128)(2,1)} %all-gather.7.cloned.1.call-done.second_ref, bf16[32,144,1536]{2,1,0:T(8,128)(2,1)} %all-gather.5.cloned.1.call-done.grads_ref, bf16[2,1536,3072]{2,1,0:T(8,128)(2,1)} %w_down.1, ...), custom_call_target="tpu_custom_call" | custom-call | flops 51539607552 | bytes 81788928 | tf_op jit(solution)/shard_map/far_weight_grads/pallas_call | solution.py:856
  613.5 8.8 %home_backward.1 = bf16[128,1536]{1,0:T(8,128)(2,1)} custom-call(s32[2]{0:T(128)} %pad_add_fusion.place, bf16[8,128,320]{2,1,0:T(8,128)(2,1)} %copy.32.d_home, bf16[128,1536]{1,0:T(8,128)(2,1)} %bitcast.71, bf16[16,1536]{1,0:T(8,128)(2,1)} %bitcast.81, f32[128,1536]{1,0:T(8,128)} %get-tuple-element.74.d_middle, bf16[384,2560]{1,0:T(8,128)(2,1)} %own_weight.1, ...), custom_call_target="tpu_custom_call" | custom-call | flops 1006632960 | bytes 10223616 | tf_op jit(solution)/shard_map/home_backward/pallas_call | solution.py:490
  622.4 6.6 %collected.1 = (f32[384,2560]{1,0:T(8,128)}, f32[384,1536]{1,0:T(8,128)}, f32[16,384]{1,0:T(8,128)}, f32[384,1]{1,0:T(8,128)}) custom-call(bf16[8,400,512]{2,1,0:T(8,128)(2,1)} %bitcast.72, bf16[384,2560]{1,0:T(8,128)(2,1)} %own_weight.1), custom_call_target="tpu_custom_call" | custom-call | tf_op jit(solution)/shard_map/collected/pallas_call | solution.py:543
  629.0 1.3 slice_reduce_fusion
  630.3 1.3 slice_bitcast_fusion.2
  (153 shorter events, 29.2 us)
Async XLA Ops:
  7.2 319.6 %all-gather.5.cloned.1.call-start = ((), (), s32[]{:S(2)}) async-start(), calls=%async_computation.3 | async-start | bytes 15925248 | tf_op jit(solution)/shard_map/all_gather | solution.py:118
  8.3 38.8 %copy-start.21 = (s32[1,128,2]{1,2,0:T(2,128)S(1)}, s32[1,128,2]{1,2,0:T(2,128)}, u32[]{:S(2)}) copy-start(s32[1,128,2]{1,2,0:T(2,128)} %param.18) | copy-start | bytes 3076
  8.3 39.0 %copy-start.8 = (bf16[1,128,1536]{2,1,0:T(8,128)(2,1)S(1)}, bf16[1,128,1536]{2,1,0:T(8,128)(2,1)}, u32[]{:S(2)}) copy-start(bf16[1,128,1536]{2,1,0:T(8,128)(2,1)} %param.19) | copy-start | bytes 1179652
  8.3 8.9 %collective-permute-start.5 = (bf16[64,1536]{1,0:T(8,128)(2,1)S(1)}, bf16[64,1536]{1,0:T(8,128)(2,1)S(1)}, u32[]{:S(2)}, u32[]{:S(2)}) collective-permute-start(bf16[64,1536]{1,0:T(8,128)(2,1)S(1)} %get-tuple-element.92), channel_id=1, source_target_pairs={{0,24},{4,28},{8,16},{12,20},{16,8},{20,12},{24,0},{28,4},{1,25},{... | collective-permute-start | bytes 589832 | tf_op jit(solution)/shard_map/ppermute | solution.py:70
  12.5 24.7 %collective-permute-start.4 = (bf16[64,1536]{1,0:T(8,128)(2,1)S(1)}, bf16[64,1536]{1,0:T(8,128)(2,1)S(1)}, u32[]{:S(2)}, u32[]{:S(2)}) collective-permute-start(bf16[64,1536]{1,0:T(8,128)(2,1)S(1)} %get-tuple-element.92), channel_id=1, source_target_pairs={{0,16},{4,20},{8,24},{12,28},{16,0},{20,4},{24,8},{28,12},{1,17},{... | collective-permute-start | bytes 589832 | tf_op jit(solution)/shard_map/ppermute | solution.py:70
  12.5 24.7 %collective-permute-start.3 = (bf16[64,1536]{1,0:T(8,128)(2,1)S(1)}, bf16[64,1536]{1,0:T(8,128)(2,1)S(1)}, u32[]{:S(2)}, u32[]{:S(2)}) collective-permute-start(bf16[64,1536]{1,0:T(8,128)(2,1)S(1)} %get-tuple-element.92), channel_id=1, source_target_pairs={{0,8},{4,12},{8,0},{12,4},{16,24},{20,28},{24,16},{28,20},{1,9},{5... | collective-permute-start | bytes 589832 | tf_op jit(solution)/shard_map/ppermute | solution.py:70
  12.9 25.7 %collective-permute-start.2 = (bf16[64,1536]{1,0:T(8,128)(2,1)S(1)}, bf16[64,1536]{1,0:T(8,128)(2,1)S(1)}, u32[]{:S(2)}, u32[]{:S(2)}) collective-permute-start(bf16[64,1536]{1,0:T(8,128)(2,1)S(1)} %get-tuple-element.91), channel_id=1, source_target_pairs={{0,24},{4,28},{8,16},{12,20},{16,8},{20,12},{24,0},{28,4},{1,25},{... | collective-permute-start | bytes 589832 | tf_op jit(solution)/shard_map/ppermute | solution.py:70
  16.1 29.6 %collective-permute-start.1 = (bf16[64,1536]{1,0:T(8,128)(2,1)S(1)}, bf16[64,1536]{1,0:T(8,128)(2,1)S(1)}, u32[]{:S(2)}, u32[]{:S(2)}) collective-permute-start(bf16[64,1536]{1,0:T(8,128)(2,1)S(1)} %get-tuple-element.91), channel_id=1, source_target_pairs={{0,16},{4,20},{8,24},{12,28},{16,0},{20,4},{24,8},{28,12},{1,17},{... | collective-permute-start | bytes 589832 | tf_op jit(solution)/shard_map/ppermute | solution.py:70
  17.2 28.5 %collective-permute-start = (bf16[64,1536]{1,0:T(8,128)(2,1)S(1)}, bf16[64,1536]{1,0:T(8,128)(2,1)S(1)}, u32[]{:S(2)}, u32[]{:S(2)}) collective-permute-start(bf16[64,1536]{1,0:T(8,128)(2,1)S(1)} %get-tuple-element.91), channel_id=1, source_target_pairs={{0,8},{4,12},{8,0},{12,4},{16,24},{20,28},{24,16},{28,20},{1,9},{5... | collective-permute-start | bytes 589832 | tf_op jit(solution)/shard_map/ppermute | solution.py:70
  37.4 68.0 %copy-start.9 = (bf16[4,64,1536]{2,1,0:T(8,128)(2,1)}, bf16[4,64,1536]{2,1,0:T(8,128)(2,1)S(1)}, u32[]{:S(2)}) copy-start(bf16[4,64,1536]{2,1,0:T(8,128)(2,1)S(1)} %pad_maximum_fusion.5.refs_1_) | copy-start | bytes 2359300
  37.4 16.8 %collective-permute-start.7 = (bf16[4,64,1536]{2,1,0:T(8,128)(2,1)S(1)}, bf16[4,64,1536]{2,1,0:T(8,128)(2,1)S(1)}, u32[]{:S(2)}, u32[]{:S(2)}) collective-permute-start(bf16[4,64,1536]{2,1,0:T(8,128)(2,1)S(1)} %pad_maximum_fusion.5.refs_1_), channel_id=1, source_target_pairs={{0,4},{4,0},{8,12},{12,8},{16,20},{20,16},{24,28},{28,24},{1,5},{5... | collective-permute-start | bytes 2359304 | tf_op jit(solution)/shard_map/ppermute | solution.py:70
  45.8 59.6 %copy-start.10 = (bf16[4,64,1536]{2,1,0:T(8,128)(2,1)}, bf16[4,64,1536]{2,1,0:T(8,128)(2,1)S(1)}, u32[]{:S(2)}) copy-start(bf16[4,64,1536]{2,1,0:T(8,128)(2,1)S(1)} %pad_maximum_fusion.4.refs_0_) | copy-start | bytes 2359300
  45.8 25.3 %collective-permute-start.6 = (bf16[4,64,1536]{2,1,0:T(8,128)(2,1)S(1)}, bf16[4,64,1536]{2,1,0:T(8,128)(2,1)}, u32[]{:S(2)}, u32[]{:S(2)}) collective-permute-start(bf16[4,64,1536]{2,1,0:T(8,128)(2,1)S(1)} %pad_maximum_fusion.4.refs_0_), channel_id=1, source_target_pairs={{0,4},{4,0},{8,12},{12,8},{16,20},{20,16},{24,28},{28,24},{1,5},{5... | collective-permute-start | bytes 2359304 | tf_op jit(solution)/shard_map/ppermute | solution.py:70
  47.2 58.2 %copy-start.12 = (s32[1,128,2]{2,1,0:T(8,128)}, s32[1,128,2]{2,1,0:T(8,128)S(1)}, u32[]{:S(2)}) copy-start(s32[1,128,2]{2,1,0:T(8,128)S(1)} %copy.23) | copy-start | bytes 3076
  47.3 58.1 %copy-start.3 = (bf16[144,1536]{1,0:T(8,128)(2,1)}, bf16[144,1536]{1,0:T(8,128)(2,1)S(1)}, u32[]{:S(2)}) copy-start(bf16[144,1536]{1,0:T(8,128)(2,1)S(1)} %fusion.4.refs_4_) | copy-start | bytes 1327108
  54.2 51.3 %copy-start.23 = (bf16[4,64,1536]{2,1,0:T(8,128)(2,1)}, bf16[4,64,1536]{2,1,0:T(8,128)(2,1)S(1)}, u32[]{:S(2)}) copy-start(bf16[4,64,1536]{2,1,0:T(8,128)(2,1)S(1)} %collective-permute-done.7.refs_3_) | copy-start | bytes 2359300
  71.1 10.4 %collective-permute-start.16 = (bf16[144,1536]{1,0:T(8,128)(2,1)S(1)}, bf16[144,1536]{1,0:T(8,128)(2,1)S(1)}, u32[]{:S(2)}, u32[]{:S(2)}) collective-permute-start(bf16[144,1536]{1,0:T(8,128)(2,1)S(1)} %fusion.4.refs_4_), channel_id=1, source_target_pairs={{0,24},{4,28},{8,16},{12,20},{16,8},{20,12},{24,0},{28,4},{1,25},{... | collective-permute-start | bytes 1327112 | tf_op jit(solution)/shard_map/ppermute | solution.py:70
  72.6 32.8 %collective-permute-start.15 = (bf16[144,1536]{1,0:T(8,128)(2,1)S(1)}, bf16[144,1536]{1,0:T(8,128)(2,1)S(1)}, u32[]{:S(2)}, u32[]{:S(2)}) collective-permute-start(bf16[144,1536]{1,0:T(8,128)(2,1)S(1)} %fusion.4.refs_4_), channel_id=1, source_target_pairs={{0,16},{4,20},{8,24},{12,28},{16,0},{20,4},{24,8},{28,12},{1,17},{... | collective-permute-start | bytes 1327112 | tf_op jit(solution)/shard_map/ppermute | solution.py:70
  72.6 32.8 %collective-permute-start.14 = (bf16[144,1536]{1,0:T(8,128)(2,1)S(1)}, bf16[144,1536]{1,0:T(8,128)(2,1)S(1)}, u32[]{:S(2)}, u32[]{:S(2)}) collective-permute-start(bf16[144,1536]{1,0:T(8,128)(2,1)S(1)} %fusion.4.refs_4_), channel_id=1, source_target_pairs={{0,8},{4,12},{8,0},{12,4},{16,24},{20,28},{24,16},{28,20},{1,9},{5... | collective-permute-start | bytes 1327112 | tf_op jit(solution)/shard_map/ppermute | solution.py:70
  106.9 390.9 %all-gather.7.cloned.1.call-start = ((), (), s32[]{:S(2)}) async-start(), calls=%async_computation.4 | async-start | bytes 14155776 | tf_op jit(solution)/shard_map/all_gather | solution.py:118
  108.1 70.6 %collective-permute-start.21 = (bf16[384,1536]{1,0:T(8,128)(2,1)S(1)}, bf16[384,1536]{1,0:T(8,128)(2,1)}, u32[]{:S(2)}, u32[]{:S(2)}) collective-permute-start(bf16[384,1536]{1,0:T(8,128)(2,1)S(1)} %copy-done.1), channel_id=1, source_target_pairs={{0,2},{1,3},{2,0},{3,1},{4,6},{5,7},{6,4},{7,5},{8,10},{9,11},{10,... | collective-permute-start | bytes 3538952 | tf_op jit(solution)/shard_map/ppermute | solution.py:70
  110.5 67.2 %collective-permute-start.9 = (bf16[384,320]{1,0:T(8,128)(2,1)}, bf16[384,320]{1,0:T(8,128)(2,1)}, u32[]{:S(2)}, u32[]{:S(2)}) collective-permute-start(bf16[384,320]{1,0:T(8,128)(2,1)} %pad_maximum_fusion.6.refs_4_), channel_id=1, source_target_pairs={{0,2},{1,3},{2,0},{3,1},{4,6},{5,7},{6,4},{7,5},{8,10},{9,11},{10,... | collective-permute-start | bytes 737288 | tf_op jit(solution)/shard_map/ppermute | solution.py:70
  110.7 67.5 %collective-permute-start.8 = (bf16[384,320]{1,0:T(8,128)(2,1)}, bf16[384,320]{1,0:T(8,128)(2,1)}, u32[]{:S(2)}, u32[]{:S(2)}) collective-permute-start(bf16[384,320]{1,0:T(8,128)(2,1)} %pad_maximum_fusion.6.refs_4_), channel_id=1, source_target_pairs={{0,1},{1,0},{2,3},{3,2},{4,5},{5,4},{6,7},{7,6},{8,9},{9,8},{10,11... | collective-permute-start | bytes 737288 | tf_op jit(solution)/shard_map/ppermute | solution.py:70
  116.0 1.4 collective-permute-start.11
  116.1 62.3 %collective-permute-start.18 = (bf16[144,1536]{1,0:T(8,128)(2,1)}, bf16[144,1536]{1,0:T(8,128)(2,1)}, u32[]{:S(2)}, u32[]{:S(2)}) collective-permute-start(bf16[144,1536]{1,0:T(8,128)(2,1)} %copy-done.3), channel_id=1, source_target_pairs={{0,2},{1,3},{2,0},{3,1},{4,6},{5,7},{6,4},{7,5},{8,10},{9,11},{10,... | collective-permute-start | bytes 1327112 | tf_op jit(solution)/shard_map/ppermute | solution.py:70
  117.4 48.8 %collective-permute-start.12 = (bf16[16,384]{1,0:T(8,128)(2,1)S(1)}, bf16[16,384]{1,0:T(8,128)(2,1)S(1)}, u32[]{:S(2)}, u32[]{:S(2)}) collective-permute-start(bf16[16,384]{1,0:T(8,128)(2,1)S(1)} %maximum_maximum_fusion), channel_id=1, source_target_pairs={{0,2},{1,3},{2,0},{3,1},{4,6},{5,7},{6,4},{7,5},{8,10},{9,11},{10,... | collective-permute-start | bytes 36872 | tf_op jit(solution)/shard_map/ppermute | solution.py:70
  166.2 11.7 %collective-permute-start.13 = (bf16[16,384]{1,0:T(8,128)(2,1)S(1)}, bf16[16,384]{1,0:T(8,128)(2,1)S(1)}, u32[]{:S(2)}, u32[]{:S(2)}) collective-permute-start(bf16[16,384]{1,0:T(8,128)(2,1)S(1)} %collective-permute-done.12), channel_id=1, source_target_pairs={{0,1},{1,0},{2,3},{3,2},{4,5},{5,4},{6,7},{7,6},{8,9},{9,8},{10,11... | collective-permute-start | bytes 36872 | tf_op jit(solution)/shard_map/ppermute | solution.py:70
  177.7 2.6 collective-permute-start.10
  177.9 19.2 %collective-permute-start.17 = (bf16[144,1536]{1,0:T(8,128)(2,1)}, bf16[144,1536]{1,0:T(8,128)(2,1)}, u32[]{:S(2)}, u32[]{:S(2)}) collective-permute-start(bf16[144,1536]{1,0:T(8,128)(2,1)} %copy-done.3), channel_id=1, source_target_pairs={{0,1},{1,0},{2,3},{3,2},{4,5},{5,4},{6,7},{7,6},{8,9},{9,8},{10,11... | collective-permute-start | bytes 1327112 | tf_op jit(solution)/shard_map/ppermute | solution.py:70
  178.2 38.7 %collective-permute-start.20 = (bf16[384,1536]{1,0:T(8,128)(2,1)S(1)}, bf16[384,1536]{1,0:T(8,128)(2,1)}, u32[]{:S(2)}, u32[]{:S(2)}) collective-permute-start(bf16[384,1536]{1,0:T(8,128)(2,1)S(1)} %copy-done.1), channel_id=1, source_target_pairs={{0,1},{1,0},{2,3},{3,2},{4,5},{5,4},{6,7},{7,6},{8,9},{9,8},{10,11... | collective-permute-start | bytes 3538952 | tf_op jit(solution)/shard_map/ppermute | solution.py:70
  178.4 18.7 %collective-permute-start.19 = (bf16[144,1536]{1,0:T(8,128)(2,1)}, bf16[144,1536]{1,0:T(8,128)(2,1)}, u32[]{:S(2)}, u32[]{:S(2)}) collective-permute-start(bf16[144,1536]{1,0:T(8,128)(2,1)} %collective-permute-done.18.refs_6_), channel_id=1, source_target_pairs={{0,1},{1,0},{2,3},{3,2},{4,5},{5,4},{6,7},{7,6},{8,9},{9,8},{10,11... | collective-permute-start | bytes 1327112 | tf_op jit(solution)/shard_map/ppermute | solution.py:70
  178.8 38.2 %collective-permute-start.22 = (bf16[384,1536]{1,0:T(8,128)(2,1)}, bf16[384,1536]{1,0:T(8,128)(2,1)}, u32[]{:S(2)}, u32[]{:S(2)}) collective-permute-start(bf16[384,1536]{1,0:T(8,128)(2,1)} %collective-permute-done.21.refs_2_.refs_10_), channel_id=1, source_target_pairs={{0,1},{1,0},{2,3},{3,2},{4,5},{5,4},{6,7},{7,6},{8,9},{9,8},{10,11... | collective-permute-start | bytes 3538952 | tf_op jit(solution)/shard_map/ppermute | solution.py:70
  222.2 10.9 %collective-permute-start.31 = (bf16[128,1536]{1,0:T(8,128)(2,1)}, bf16[128,1536]{1,0:T(8,128)(2,1)S(1)}, u32[]{:S(2)}, u32[]{:S(2)}) collective-permute-start(bf16[128,1536]{1,0:T(8,128)(2,1)} %get-tuple-element.50.refs_0_.refs_4_), channel_id=1, source_target_pairs={{0,24},{4,28},{8,16},{12,20},{16,8},{20,12},{24,0},{28,4},{1,25},{... | collective-permute-start | bytes 1179656 | tf_op jit(solution)/shard_map/ppermute | solution.py:70
  223.7 33.7 %collective-permute-start.30 = (bf16[128,1536]{1,0:T(8,128)(2,1)}, bf16[128,1536]{1,0:T(8,128)(2,1)S(1)}, u32[]{:S(2)}, u32[]{:S(2)}) collective-permute-start(bf16[128,1536]{1,0:T(8,128)(2,1)} %get-tuple-element.50.refs_0_.refs_4_), channel_id=1, source_target_pairs={{0,16},{4,20},{8,24},{12,28},{16,0},{20,4},{24,8},{28,12},{1,17},{... | collective-permute-start | bytes 1179656 | tf_op jit(solution)/shard_map/ppermute | solution.py:70
  224.0 33.5 %collective-permute-start.29 = (bf16[128,1536]{1,0:T(8,128)(2,1)}, bf16[128,1536]{1,0:T(8,128)(2,1)S(1)}, u32[]{:S(2)}, u32[]{:S(2)}) collective-permute-start(bf16[128,1536]{1,0:T(8,128)(2,1)} %get-tuple-element.50.refs_0_.refs_4_), channel_id=1, source_target_pairs={{0,8},{4,12},{8,0},{12,4},{16,24},{20,28},{24,16},{28,20},{1,9},{5... | collective-permute-start | bytes 1179656 | tf_op jit(solution)/shard_map/ppermute | solution.py:70
  259.9 9.6 %collective-permute-start.24 = (bf16[128,1536]{1,0:T(8,128)(2,1)S(1)}, bf16[128,1536]{1,0:T(8,128)(2,1)S(1)}, u32[]{:S(2)}, u32[]{:S(2)}) collective-permute-start(bf16[128,1536]{1,0:T(8,128)(2,1)S(1)} %copy-done.4), channel_id=1, source_target_pairs={{0,2},{1,3},{2,0},{3,1},{4,6},{5,7},{6,4},{7,5},{8,10},{9,11},{10,... | collective-permute-start | bytes 1179656 | tf_op jit(solution)/shard_map/ppermute | solution.py:70
  262.2 10.1 %collective-permute-start.23 = (bf16[128,1536]{1,0:T(8,128)(2,1)S(1)}, bf16[128,1536]{1,0:T(8,128)(2,1)S(1)}, u32[]{:S(2)}, u32[]{:S(2)}) collective-permute-start(bf16[128,1536]{1,0:T(8,128)(2,1)S(1)} %copy-done.4), channel_id=1, source_target_pairs={{0,1},{1,0},{2,3},{3,2},{4,5},{5,4},{6,7},{7,6},{8,9},{9,8},{10,11... | collective-permute-start | bytes 1179656 | tf_op jit(solution)/shard_map/ppermute | solution.py:70
  269.6 4.1 collective-permute-start.25
  302.8 2.0 collective-permute-start.41
  303.2 4.2 collective-permute-start.40
  305.9 20.8 %collective-permute-start.42 = (bf16[128,1664]{1,0:T(8,128)(2,1)S(1)}, bf16[128,1664]{1,0:T(8,128)(2,1)S(1)}, u32[]{:S(2)}, u32[]{:S(2)}) collective-permute-start(bf16[128,1664]{1,0:T(8,128)(2,1)S(1)} %add_convert_fusion), channel_id=1, source_target_pairs={{0,2},{1,3},{2,0},{3,1},{4,6},{5,7},{6,4},{7,5},{8,10},{9,11},{10,... | collective-permute-start | bytes 1277960 | tf_op jit(solution)/shard_map/ppermute | solution.py:70
  307.5 19.3 %copy-start.13 = (bf16[128,1664]{1,0:T(8,128)(2,1)}, bf16[128,1664]{1,0:T(8,128)(2,1)S(1)}, u32[]{:S(2)}) copy-start(bf16[128,1664]{1,0:T(8,128)(2,1)S(1)} %collective-permute-done.40.refs_1_) | copy-start | bytes 1277956
  335.0 85.3 %all-to-all-start.1 = ((bf16[8,128,384]{2,1,0:T(8,128)(2,1)}), bf16[8,128,384]{2,1,0:T(8,128)(2,1)}, u32[]{:S(2)}, u32[]{:S(2)}) async-start(bf16[8,128,384]{2,1,0:T(8,128)(2,1)} %get-tuple-element.67), calls=%async_computation.1 | async-start | bytes 1572864 | tf_op jit(solution)/shard_map/all_to_all | solution.py:65
  339.3 283.0 %all-gather.9.cloned.1.call-start = ((), (), s32[]{:S(2)}) async-start(), calls=%async_computation.5 | async-start | bytes 3686400 | tf_op jit(solution)/shard_map/all_gather | solution.py:979
  339.5 41.6 %collective-permute-start.36 = (bf16[512,192]{1,0:T(8,128)(2,1)S(1)}, bf16[512,192]{1,0:T(8,128)(2,1)S(1)}, u32[]{:S(2)}, u32[]{:S(2)}) collective-permute-start(bf16[512,192]{1,0:T(8,128)(2,1)S(1)} %get-tuple-element.88), channel_id=1, source_target_pairs={{0,16},{4,20},{8,24},{12,28},{16,0},{20,4},{24,8},{28,12},{1,17},{... | collective-permute-start | bytes 589832 | tf_op jit(solution)/shard_map/ppermute | solution.py:70
  341.7 41.1 %collective-permute-start.35 = (bf16[512,192]{1,0:T(8,128)(2,1)S(1)}, bf16[512,192]{1,0:T(8,128)(2,1)S(1)}, u32[]{:S(2)}, u32[]{:S(2)}) collective-permute-start(bf16[512,192]{1,0:T(8,128)(2,1)S(1)} %get-tuple-element.88), channel_id=1, source_target_pairs={{0,8},{4,12},{8,0},{12,4},{16,24},{20,28},{24,16},{28,20},{1,9},{5... | collective-permute-start | bytes 589832 | tf_op jit(solution)/shard_map/ppermute | solution.py:70
  342.9 39.9 %collective-permute-start.37 = (bf16[512,192]{1,0:T(8,128)(2,1)S(1)}, bf16[512,192]{1,0:T(8,128)(2,1)S(1)}, u32[]{:S(2)}, u32[]{:S(2)}) collective-permute-start(bf16[512,192]{1,0:T(8,128)(2,1)S(1)} %get-tuple-element.88), channel_id=1, source_target_pairs={{0,24},{4,28},{8,16},{12,20},{16,8},{20,12},{24,0},{28,4},{1,25},{... | collective-permute-start | bytes 589832 | tf_op jit(solution)/shard_map/ppermute | solution.py:70
  343.1 55.0 %collective-permute-start.33 = (bf16[512,192]{1,0:T(8,128)(2,1)S(1)}, bf16[512,192]{1,0:T(8,128)(2,1)}, u32[]{:S(2)}, u32[]{:S(2)}) collective-permute-start(bf16[512,192]{1,0:T(8,128)(2,1)S(1)} %get-tuple-element.89), channel_id=1, source_target_pairs={{0,16},{4,20},{8,24},{12,28},{16,0},{20,4},{24,8},{28,12},{1,17},{... | collective-permute-start | bytes 589832 | tf_op jit(solution)/shard_map/ppermute | solution.py:70
  344.4 53.7 %collective-permute-start.32 = (bf16[512,192]{1,0:T(8,128)(2,1)S(1)}, bf16[512,192]{1,0:T(8,128)(2,1)}, u32[]{:S(2)}, u32[]{:S(2)}) collective-permute-start(bf16[512,192]{1,0:T(8,128)(2,1)S(1)} %get-tuple-element.89), channel_id=1, source_target_pairs={{0,8},{4,12},{8,0},{12,4},{16,24},{20,28},{24,16},{28,20},{1,9},{5... | collective-permute-start | bytes 589832 | tf_op jit(solution)/shard_map/ppermute | solution.py:70
  381.1 17.0 %collective-permute-start.34 = (bf16[512,192]{1,0:T(8,128)(2,1)S(1)}, bf16[512,192]{1,0:T(8,128)(2,1)}, u32[]{:S(2)}, u32[]{:S(2)}) collective-permute-start(bf16[512,192]{1,0:T(8,128)(2,1)S(1)} %get-tuple-element.89), channel_id=1, source_target_pairs={{0,24},{4,28},{8,16},{12,20},{16,8},{20,12},{24,0},{28,4},{1,25},{... | collective-permute-start | bytes 589832 | tf_op jit(solution)/shard_map/ppermute | solution.py:70
  384.3 19.7 %collective-permute-start.39 = (bf16[4,512,192]{1,2,0:T(8,128)(2,1)}, bf16[4,512,192]{1,2,0:T(8,128)(2,1)}, u32[]{:S(2)}, u32[]{:S(2)}) collective-permute-start(bf16[4,512,192]{1,2,0:T(8,128)(2,1)} %copy.28), channel_id=1, source_target_pairs={{0,4},{4,0},{8,12},{12,8},{16,20},{20,16},{24,28},{28,24},{1,5},{5... | collective-permute-start | bytes 2359304 | tf_op jit(solution)/shard_map/ppermute | solution.py:70
  402.5 16.0 %collective-permute-start.38 = (bf16[4,512,192]{1,2,0:T(8,128)(2,1)}, bf16[4,512,192]{1,2,0:T(8,128)(2,1)S(1)}, u32[]{:S(2)}, u32[]{:S(2)}) collective-permute-start(bf16[4,512,192]{1,2,0:T(8,128)(2,1)} %copy.27), channel_id=1, source_target_pairs={{0,4},{4,0},{8,12},{12,8},{16,20},{20,16},{24,28},{28,24},{1,5},{5... | collective-permute-start | bytes 2359304 | tf_op jit(solution)/shard_map/ppermute | solution.py:70
  420.3 24.8 %copy-start.24 = (bf16[128,1536]{1,0:T(8,128)(2,1)S(1)}, bf16[128,1536]{1,0:T(8,128)(2,1)}, u32[]{:S(2)}) copy-start(bf16[128,1536]{1,0:T(8,128)(2,1)} %get-tuple-element.54) | copy-start | bytes 1179652
  439.5 6.5 %collective-permute-start.47 = (bf16[400,512]{1,0:T(8,128)(2,1)S(1)}, bf16[400,512]{1,0:T(8,128)(2,1)S(1)}, u32[]{:S(2)}, u32[]{:S(2)}) collective-permute-start(bf16[400,512]{1,0:T(8,128)(2,1)S(1)} %get-tuple-element.85), channel_id=1, source_target_pairs={{0,1},{1,0},{2,3},{3,2},{4,5},{5,4},{6,7},{7,6},{8,9},{9,8},{10,11... | collective-permute-start | bytes 1228808 | tf_op jit(solution)/shard_map/ppermute | solution.py:70
  443.7 63.9 %collective-permute-start.44 = (bf16[384,2560]{1,0:T(8,128)(2,1)S(1)}, bf16[384,2560]{1,0:T(8,128)(2,1)}, u32[]{:S(2)}, u32[]{:S(2)}) collective-permute-start(bf16[384,2560]{1,0:T(8,128)(2,1)S(1)} %copy-done), channel_id=1, source_target_pairs={{0,2},{1,3},{2,0},{3,1},{4,6},{5,7},{6,4},{7,5},{8,10},{9,11},{10,... | collective-permute-start | bytes 5898248 | tf_op jit(solution)/shard_map/ppermute | solution.py:70
  445.1 1.7 collective-permute-start.27
  445.5 53.7 %collective-permute-start.26 = (bf16[128,1536]{1,0:T(8,128)(2,1)}, bf16[128,1536]{1,0:T(8,128)(2,1)}, u32[]{:S(2)}, u32[]{:S(2)}) collective-permute-start(bf16[128,1536]{1,0:T(8,128)(2,1)} %get-tuple-element.52), channel_id=1, source_target_pairs={{0,1},{1,0},{2,3},{3,2},{4,5},{5,4},{6,7},{7,6},{8,9},{9,8},{10,11... | collective-permute-start | bytes 1179656 | tf_op jit(solution)/shard_map/ppermute | solution.py:70
  445.6 2.8 collective-permute-start.46
  446.1 59.3 %copy-start.5 = (f32[128,1536]{1,0:T(8,128)S(1)}, f32[128,1536]{1,0:T(8,128)}, u32[]{:S(2)}) copy-start(f32[128,1536]{1,0:T(8,128)} %get-tuple-element.49.refs_3_) | copy-start | bytes 2359300
  446.1 50.8 %collective-permute-start.48 = (bf16[400,512]{1,0:T(8,128)(2,1)S(1)}, bf16[400,512]{1,0:T(8,128)(2,1)S(1)}, u32[]{:S(2)}, u32[]{:S(2)}) collective-permute-start(bf16[400,512]{1,0:T(8,128)(2,1)S(1)} %fusion.1), channel_id=1, source_target_pairs={{0,2},{1,3},{2,0},{3,1},{4,6},{5,7},{6,4},{7,5},{8,10},{9,11},{10,... | collective-permute-start | bytes 1228808 | tf_op jit(solution)/shard_map/ppermute | solution.py:70
  447.7 57.7 %collective-permute-start.28 = (bf16[128,1536]{1,0:T(8,128)(2,1)}, bf16[128,1536]{1,0:T(8,128)(2,1)}, u32[]{:S(2)}, u32[]{:S(2)}) collective-permute-start(bf16[128,1536]{1,0:T(8,128)(2,1)} %add_convert_fusion.2), channel_id=1, source_target_pairs={{0,2},{1,3},{2,0},{3,1},{4,6},{5,7},{6,4},{7,5},{8,10},{9,11},{10,... | collective-permute-start | bytes 1179656 | tf_op jit(solution)/shard_map/ppermute | solution.py:70
  497.8 115.7 %collective-permute-start.43 = (bf16[384,2560]{1,0:T(8,128)(2,1)S(1)}, bf16[384,2560]{1,0:T(8,128)(2,1)}, u32[]{:S(2)}, u32[]{:S(2)}) collective-permute-start(bf16[384,2560]{1,0:T(8,128)(2,1)S(1)} %copy-done), channel_id=1, source_target_pairs={{0,1},{1,0},{2,3},{3,2},{4,5},{5,4},{6,7},{7,6},{8,9},{9,8},{10,11... | collective-permute-start | bytes 5898248 | tf_op jit(solution)/shard_map/ppermute | solution.py:70
  507.6 105.9 %collective-permute-start.45 = (bf16[384,2560]{1,0:T(8,128)(2,1)}, bf16[384,2560]{1,0:T(8,128)(2,1)}, u32[]{:S(2)}, u32[]{:S(2)}) collective-permute-start(bf16[384,2560]{1,0:T(8,128)(2,1)} %collective-permute-done.44.refs_2_), channel_id=1, source_target_pairs={{0,1},{1,0},{2,3},{3,2},{4,5},{5,4},{6,7},{7,6},{8,9},{9,8},{10,11... | collective-permute-start | bytes 5898248 | tf_op jit(solution)/shard_map/ppermute | solution.py:70
  509.5 102.8 %all-to-all-start.2 = ((bf16[8,128,320]{1,2,0:T(8,128)(2,1)}), bf16[8,128,320]{1,2,0:T(8,128)(2,1)S(1)}, u32[]{:S(2)}, u32[]{:S(2)}) async-start(bf16[8,128,320]{1,2,0:T(8,128)(2,1)} %copy.31), calls=%async_computation.2 | async-start | bytes 1310720 | tf_op jit(solution)/shard_map/all_to_all | solution.py:65
  (15 other events, 90.5 us)
Sparse Core Ops, SparseCore 0:
  107.0 104.5 all-gather.4
  260.0 82.9 all-gather.6
  497.9 79.2 all-gather.8

commit v5 on v4

--- a/solution.py
+++ b/solution.py
@@ -65,6 +65,10 @@
     return lax.all_to_all(value, axis, 0, 0, tiled=True)
 
 
+def gathered(value, axis):
+    return lax.all_gather(value, axis, axis=0, tiled=True)
+
+
 def exchanged(value, axis, distance):
     count = lax.axis_size(axis)
     return lax.ppermute(value, axis, [(i, i ^ distance) for i in range(count)])
@@ -103,9 +107,10 @@
     return jnp.stack([own] + [exchanged(own, "ctx", d) for d in range(2, spans, 2)])
 
 
-def span_pieces(own):
+def span_pieces(own, *others):
     half = own.shape[0] // 2
     same = [line_blocks(part) for part in (own[:half], own[half:])]
+    same = after(same, *others)
     return same + [exchanged(part, "ctx", 1) for part in same]
 
 
@@ -120,6 +125,10 @@
 
 def after(values, *others):
     return lax.optimization_barrier((values, others))[0]
+
+
+def time_of(microseconds):
+    return pl.CostEstimate(flops=0, bytes_accessed=microseconds * 3_600_000, transcendentals=0)
 
 
 def whole(array):
@@ -251,62 +260,43 @@
             )
         ],
         compiler_params=pltpu.CompilerParams(vmem_limit_bytes=VMEM),
-        cost_estimate=pl.CostEstimate(
-            flops=2 * length * width * HEAD_COLS + 4 * length * length * HEAD,
-            bytes_accessed=8 * length * width,
-            transcendentals=GROUP * length * length,
-        ),
+        cost_estimate=time_of(16),
         name="stream_attention",
     )(place, starts, *pieces, *head_weights, side)
 
 
-def home_kernel(copies, place, own, tokens, side, *refs):
-    weights, (middle, second) = refs[:-2], refs[-2:]
-    shards = len(weights)
-    heads = HK // shards
+def home_kernel(copies, own, tokens, side, weight, middle, second):
     total = tokens[...].astype(F32)
-    for r, weight in enumerate(weights):
-        first = (place[1] ^ r) * heads
-        for h in range(heads):
-            part = own[(first + h) * copies]
-            for i in range(1, copies):
-                part = part + own[(first + h) * copies + i]
-            total = total + dot(part, weight[h * HEAD : (h + 1) * HEAD, :])
+    for head in range(HK):
+        part = own[head * copies]
+        for i in range(1, copies):
+            part = part + own[head * copies + i]
+        total = total + dot(part, weight[head * HEAD : (head + 1) * HEAD, :])
     middle[...] = total
     gain = side[EXPERTS + 1 : EXPERTS + 2, :].astype(F32)
     second[...] = (total * rms_factor(total) * gain).astype(BF)
 
 
-def home_forward(place, own, tokens, side, weights, copies):
-    args = (own, tokens, side, *weights)
+def home_forward(own, tokens, side, weight, copies):
+    args = (own, tokens, side, weight)
     return pl.pallas_call(
         functools.partial(home_kernel, copies),
-        grid_spec=pltpu.PrefetchScalarGridSpec(
-            num_scalar_prefetch=1,
-            grid=(1,),
-            in_specs=[whole(a) for a in args],
-            out_specs=[whole(tokens)] * 2,
-        ),
+        grid=(1,),
+        in_specs=[whole(a) for a in args],
+        out_specs=[whole(tokens)] * 2,
         out_shape=[
             jax.ShapeDtypeStruct(tokens.shape, F32),
             jax.ShapeDtypeStruct(tokens.shape, BF),
         ],
         compiler_params=pltpu.CompilerParams(vmem_limit_bytes=VMEM),
-        cost_estimate=pl.CostEstimate(
-            flops=2 * tokens.size * tokens.shape[1],
-            bytes_accessed=8 * tokens.size + 2 * tokens.shape[1] ** 2,
-            transcendentals=tokens.shape[0],
-        ),
+        cost_estimate=time_of(5),
         name="home_forward",
-    )(place, *args)
-
-
-def turn_kernel(copies, term_count, place, *refs):
+    )(*args)
+
+
+def turn_kernel(copies, term_count, *refs):
     terms, refs = refs[:term_count], refs[term_count:]
-    middle_ref, second_ref, grad, routes, side, *weights = refs[:-3]
-    d_middle_out, sent, small = refs[-3:]
-    shards = len(weights)
-    heads = HK // shards
+    middle_ref, second_ref, grad, routes, side, weight, d_middle_out, sent, small = refs
     width = middle_ref.shape[1]
     back = terms[0][...].astype(F32)
     for term in terms[1:]:
@@ -330,19 +320,17 @@
     d_middle = grad[...].astype(F32) + rms_input_grad(middle, factor, gain, d_second)
     d_middle_out[...] = d_middle
     d_proj = d_middle.astype(BF)
-    for r, weight in enumerate(weights):
-        d_heads = dot_t(d_proj, weight[...]).astype(BF)
-        for h in range(heads):
-            for i in range(copies):
-                spot = ((place[1] ^ r) * heads + h) * copies + i
-                sent[spot, :, :HEAD] = d_heads[:, h * HEAD : (h + 1) * HEAD]
+    for head in range(HK):
+        d_head = dot_t(d_proj, weight[head * HEAD : (head + 1) * HEAD, :]).astype(BF)
+        for i in range(copies):
+            sent[head * copies + i, :, :HEAD] = d_head
     chunk = sent.shape[2] - HEAD
     for span in range(sent.shape[0]):
         sent[span, :, HEAD:] = d_proj[:, span * chunk : (span + 1) * chunk]
 
 
-def home_turn(place, terms, middle, second, grad, routes, side, weights, spans):
-    args = (*terms, middle, second, grad, routes, side, *weights)
+def home_turn(terms, middle, second, grad, routes, side, weight, spans):
+    args = (*terms, middle, second, grad, routes, side, weight)
     tokens, width = middle.shape
     shapes = [
         jax.ShapeDtypeStruct((tokens, width), F32),
@@ -351,21 +339,14 @@
     ]
     return pl.pallas_call(
         functools.partial(turn_kernel, spans // HK, len(terms)),
-        grid_spec=pltpu.PrefetchScalarGridSpec(
-            num_scalar_prefetch=1,
-            grid=(1,),
-            in_specs=[whole(a) for a in args],
-            out_specs=[whole(shape) for shape in shapes],
-        ),
+        grid=(1,),
+        in_specs=[whole(a) for a in args],
+        out_specs=[whole(shape) for shape in shapes],
         out_shape=shapes,
         compiler_params=pltpu.CompilerParams(vmem_limit_bytes=VMEM),
-        cost_estimate=pl.CostEstimate(
-            flops=2 * tokens * width * width,
-            bytes_accessed=24 * tokens * width + 2 * width * width,
-            transcendentals=tokens,
-        ),
+        cost_estimate=time_of(7),
         name="home_turn",
-    )(place, *args)
+    )(*args)
 
 
 def stream_grad_kernel(
@@ -441,24 +422,12 @@
         ),
         out_shape=shapes,
         compiler_params=pltpu.CompilerParams(vmem_limit_bytes=VMEM),
-        cost_estimate=pl.CostEstimate(
-            flops=2 * length * width * (HEAD_COLS + width // spans) + 10 * length * length * HEAD,
-            bytes_accessed=8 * length * width,
-            transcendentals=GROUP * length * length,
-        ),
+        cost_estimate=time_of(17),
         name="stream_backward",
     )(place, starts, *pieces, *args)
 
 
-def home_grad_kernel(copies, place, d_home, tokens, side, d_middle, *refs):
-    weight_refs, (d_tokens, weight, mixed, d_normed, sems) = refs[:-5], refs[-5:]
-    shards = len(weight_refs)
-    loading = [
-        pltpu.make_async_copy(ref, weight.at[place[1] ^ r], sems.at[r])
-        for r, ref in enumerate(weight_refs)
-    ]
-    for copy in loading:
-        copy.start()
+def home_grad_kernel(copies, d_home, tokens, side, d_middle, weight, d_tokens, mixed):
     for head in range(HK):
         part = d_home[head * copies]
         if copies > 1:
@@ -471,45 +440,26 @@
         mixed[:, key : key + HD] = part[:, HEAD : HEAD + HD]
         value = key + K_COLS
         mixed[:, value : value + HD] = part[:, HEAD + HD :]
-    for copy in loading:
-        copy.wait()
-    rows = weight.shape[1]
-    for f in range(shards):
-        d_normed[:, f * rows : (f + 1) * rows] = dot_t(mixed[...], weight[f])
+    d_normed = dot_t(mixed[...], weight[...])
     x = tokens[...].astype(F32)
     gain = side[EXPERTS : EXPERTS + 1, :].astype(F32)
-    d_x = rms_input_grad(x, rms_factor(x), gain, d_normed[...])
+    d_x = rms_input_grad(x, rms_factor(x), gain, d_normed)
     d_tokens[...] = (d_middle[...] + d_x).astype(BF)
 
 
-def home_backward(place, d_home, tokens, side, d_middle, weights, copies):
-    args = (d_home, tokens, side, d_middle)
-    count, width = tokens.shape
-    shards = len(weights)
-    columns = Q_COLS + 2 * K_COLS
+def home_backward(d_home, tokens, side, d_middle, weight, copies):
+    args = (d_home, tokens, side, d_middle, weight)
     return pl.pallas_call(
         functools.partial(home_grad_kernel, copies),
-        grid_spec=pltpu.PrefetchScalarGridSpec(
-            num_scalar_prefetch=1,
-            grid=(1,),
-            in_specs=[whole(a) for a in args] + [anywhere()] * shards,
-            out_specs=whole(tokens),
-            scratch_shapes=[
-                pltpu.VMEM((shards, width // shards, columns), BF),
-                pltpu.VMEM((count, columns), BF),
-                pltpu.VMEM((count, width), F32),
-                pltpu.SemaphoreType.DMA((shards,)),
-            ],
-        ),
+        grid=(1,),
+        in_specs=[whole(a) for a in args],
+        out_specs=whole(tokens),
+        scratch_shapes=[pltpu.VMEM((tokens.shape[0], Q_COLS + 2 * K_COLS), BF)],
         out_shape=jax.ShapeDtypeStruct(tokens.shape, BF),
         compiler_params=pltpu.CompilerParams(vmem_limit_bytes=VMEM),
-        cost_estimate=pl.CostEstimate(
-            flops=2 * count * width * columns,
-            bytes_accessed=2 * width * columns + 12 * count * width,
-            transcendentals=count,
-        ),
+        cost_estimate=time_of(8),
         name="home_backward",
-    )(place, *args, *weights)
+    )(*args)
 
 
 def collect_kernel(copies, late, own_weight, d_qkv, d_out, small, d_gain):
@@ -547,6 +497,7 @@
         out_specs=[whole(shape) for shape in shapes],
         out_shape=shapes,
         compiler_params=pltpu.CompilerParams(vmem_limit_bytes=VMEM),
+        cost_estimate=time_of(7),
         name="collected",
     )(late, own_weight)
 
@@ -675,11 +626,7 @@
         ),
         out_shape=shapes,
         compiler_params=pltpu.CompilerParams(vmem_limit_bytes=VMEM),
-        cost_estimate=pl.CostEstimate(
-            flops=12 * experts * slots * width * FF,
-            bytes_accessed=w_experts.size * 2,
-            transcendentals=experts * slots * FF,
-        ),
+        cost_estimate=time_of(26),
         name="near_experts",
     )(place, *second, *grads, router_t, w_experts, w_experts, w_experts)
     return outs[:shards], outs[shards:]
@@ -881,11 +828,7 @@
         ),
         out_shape=jax.ShapeDtypeStruct((experts, width, 3 * FF), F32),
         compiler_params=pltpu.CompilerParams(vmem_limit_bytes=VMEM),
-        cost_estimate=pl.CostEstimate(
-            flops=8 * experts * most * width * FF,
-            bytes_accessed=w_experts.size * 6 + 4 * blocks * tokens * width,
-            transcendentals=experts * most * FF,
-        ),
+        cost_estimate=time_of(80),
         name="far_weight_grads",
     )(place, router_t, second, grads, w_experts, w_experts, w_experts)
 
@@ -935,13 +878,14 @@
     side = jnp.take(side, jnp.arange(shards, dtype=jnp.int32) ^ shard, axis=0)
     side = side.swapaxes(0, 1).reshape(EXTRA, width)
     head_w = near_blocks(head_w)
-    pieces = span_pieces(x)
+    out_w = gathered(output_weight, "fsdp")
+    qkv_w = gathered(after(query_key_value_weight, out_w), "fsdp")
+    pieces = span_pieces(x, side, head_w)
 
     payload = jnp.concatenate(
         [grad, jnp.pad(routes[0].T.astype(BF), ((0, EXTRA - 2), (0, width - tok_count)))]
     )
-    payload, output_weight = after((payload, output_weight), pieces)
-    out_w = near_blocks(output_weight)
+    payload = after(payload, pieces)
     grads_near = near_blocks(payload)
     grads_line = line_blocks(payload)
     grads_all = all_blocks(grads_line)
@@ -950,24 +894,22 @@
         place, doc_starts[0], pieces, head_w, side, copies
     )
 
-    attended_low, grads_line = after((attended_low, grads_line), grads_near)
+    attended_low = after(attended_low, grads_line, grads_near)
     own = to_all(attended_low, "ctx").reshape(spans, tok_count, HEAD)
-    middle, second = home_forward(place, own, x, side, out_w, copies)
+    middle, second = home_forward(own, x, side, out_w, copies)
     second_near = near_blocks(second)
     second_line = line_blocks(second)
     second_all = all_blocks(second_line)
 
     branch, back = near_experts(place, second_near, grads_near, side, w_experts)
-    back = after(back, second_line)
-    later_qkv, attended_low = after((query_key_value_weight, attended_low), back)
-    qkv_w = near_blocks(later_qkv)
-    attended_pieces = span_pieces(attended_low)
+    attended_pieces = span_pieces(after(attended_low, second_line), back)
+    back = after(back, attended_pieces[:2])
     terms = after(near_terms(back), grads_all)
     branch_terms = near_terms(branch)
     output = sum((term.astype(F32) for term in branch_terms), middle).astype(BF)
 
     d_middle, sent, small = home_turn(
-        place, terms, middle, second, grad, routes[0], side, out_w, spans
+        terms, middle, second, grad, routes[0], side, out_w, spans
     )
 
     sent = to_all(sent.reshape(length, -1), "ctx")
@@ -979,7 +921,7 @@
     late = lax.all_gather(after(late, second_all), "ctx", axis=0)
 
     d_home = to_all(d_mixed, "ctx").reshape(spans, tok_count, HEAD_COLS)
-    d_tokens = home_backward(place, d_home, x, side, d_middle, qkv_w, copies)
+    d_tokens = home_backward(d_home, x, side, d_middle, qkv_w, copies)
 
     second_all = second_all.reshape(blocks, tok_count, width)
     grads_all = grads_all.reshape(blocks, tok_count + EXTRA, width)

time: 649 us -> 600 us (0.924)
  the two profiles are of different devices: /device:TPU:1 before, /device:TPU:31 now
where the time goes in v5:
time: 600 us; the launch traced here: 590 us
  waiting for transfers between devices  246 us (41%)
  Pallas kernels  196 us (33%)
  starting transfers between devices  73.4 us (12%)
  local copies, waits for them, and re-layouts  34 us (6%)
  blocking collectives  15.3 us (3%)
  between operations  14.7 us (2%)
  other arithmetic  10.9 us (2%)
    ppermute x43, waiting for transfers between devices, exchanged(): return lax.ppermute(value, axis, [(i, i ^ distance) for i in range(count)])  227 us
    pallas_call x1, Pallas kernels, far_weight_grads(): pl.pallas_call(far_kernel, grid_spec=pltpu.PrefetchScalarGridSpec(num_sca...  107 us
    ppermute x43, starting transfers between devices, exchanged(): return lax.ppermute(value, axis, [(i, i ^ distance) for i in range(count)])  47.1 us
    pallas_call x1, Pallas kernels, near_experts(): pl.pallas_call(functools.partial(near_kernel, shards), grid_spec=pltpu.Pr...  28.5 us
    all_to_all x2, starting transfers between devices, to_all(): return lax.all_to_all(value, axis, 0, 0, tiled=True)  25.8 us
    all_to_all x2, waiting for transfers between devices, to_all(): return lax.all_to_all(value, axis, 0, 0, tiled=True)  18 us
    pallas_call x1, Pallas kernels, stream_backward(): pl.pallas_call(functools.partial(stream_grad_kernel, spans // HK), grid_s...  17.7 us
    pallas_call x1, Pallas kernels, stream_attention(): pl.pallas_call(functools.partial(stream_kernel, copies), grid_spec=pltpu....  16.9 us
  transfers between devices with their start and end apart: 50, of which 23 were waited for; matrix products, arithmetic and copies ran while one was open for 6% of the time, Pallas kernels for 32%

profile of v5, /device:TPU:31, one launch (start us, length us, event | category | flops | bytes accessed | tf_op | source)
XLA Modules:
  0.0 590.4 jit_solution(6118991354826859629)
XLA Ops:
  13.4 1.3 collective-permute-start.10
  15.9 1.5 collective-permute-start.1
  17.4 2.2 collective-permute-start
  20.8 3.1 collective-permute-done.2
  23.9 14.8 %collective-permute-done.1 = bf16[64,1536]{1,0:T(8,128)(2,1)S(1)} collective-permute-done((bf16[64,1536]{1,0:T(8,128)(2,1)S(1)}, bf16[64,1536]{1,0:T(8,128)(2,1)S(1)}, u32[]{:S(2)}, u32[]{:S(2)}) %collective-permute-start.1) | collective-permute-done | bytes 196640 | tf_op jit(solution)/shard_map/ppermute | solution.py:74
  38.8 1.3 collective-permute-start.3
  40.2 1.8 collective-permute-start.11
  42.0 9.4 %collective-permute-done.4 = bf16[64,1536]{1,0:T(8,128)(2,1)S(1)} collective-permute-done((bf16[64,1536]{1,0:T(8,128)(2,1)S(1)}, bf16[64,1536]{1,0:T(8,128)(2,1)S(1)}, u32[]{:S(2)}, u32[]{:S(2)}) %collective-permute-start.4) | collective-permute-done | bytes 196640 | tf_op jit(solution)/shard_map/ppermute | solution.py:74
  51.9 1.2 collective-permute-start.13
  53.4 16.6 %collective-permute-done.12.refs_2_ = bf16[4,64,1536]{2,1,0:T(8,128)(2,1)} collective-permute-done((bf16[4,64,1536]{2,1,0:T(8,128)(2,1)S(1)}, bf16[4,64,1536]{2,1,0:T(8,128)(2,1)}, u32[]{:S(2)}, u32[]{:S(2)}) %collective-permute-start.12) | collective-permute-done | bytes 786464 | tf_op jit(solution)/shard_map/ppermute | solution.py:74
  70.0 16.9 %collective-permute-done.13.refs_3_ = bf16[4,64,1536]{2,1,0:T(8,128)(2,1)} collective-permute-done((bf16[4,64,1536]{2,1,0:T(8,128)(2,1)S(1)}, bf16[4,64,1536]{2,1,0:T(8,128)(2,1)}, u32[]{:S(2)}, u32[]{:S(2)}) %collective-permute-start.13) | collective-permute-done | bytes 786464 | tf_op jit(solution)/shard_map/ppermute | solution.py:74
  87.9 2.5 collective-permute-start.14
  90.4 8.4 %collective-permute-done.16 = bf16[144,1536]{1,0:T(8,128)(2,1)S(1)} collective-permute-done((bf16[144,1536]{1,0:T(8,128)(2,1)S(1)}, bf16[144,1536]{1,0:T(8,128)(2,1)S(1)}, u32[]{:S(2)}, u32[]{:S(2)}) %collective-permute-start.16) | collective-permute-done | bytes 442400 | tf_op jit(solution)/shard_map/ppermute | solution.py:74
  98.8 24.5 %collective-permute-done.15 = bf16[144,1536]{1,0:T(8,128)(2,1)S(1)} collective-permute-done((bf16[144,1536]{1,0:T(8,128)(2,1)S(1)}, bf16[144,1536]{1,0:T(8,128)(2,1)S(1)}, u32[]{:S(2)}, u32[]{:S(2)}) %collective-permute-start.15) | collective-permute-done | bytes 442400 | tf_op jit(solution)/shard_map/ppermute | solution.py:74
  123.3 1.4 pad_maximum_fusion
  125.1 2.9 collective-permute-start.17
  128.0 6.0 %collective-permute-done.18.refs_6_ = bf16[144,1536]{1,0:T(8,128)(2,1)S(1)} collective-permute-done((bf16[144,1536]{1,0:T(8,128)(2,1)S(1)}, bf16[144,1536]{1,0:T(8,128)(2,1)S(1)}, u32[]{:S(2)}, u32[]{:S(2)}) %collective-permute-start.18) | collective-permute-done | bytes 442400 | tf_op jit(solution)/shard_map/ppermute | solution.py:74
  133.9 3.5 collective-permute-start.19
  138.0 16.9 %stream_attention.1 = (bf16[1024,1536]{1,0:T(8,128)(2,1)}, bf16[1024,320]{1,0:T(8,128)(2,1)}, bf16[1024,192]{1,0:T(8,128)(2,1)}, f32[1024,192]{1,0:T(8,128)}, f32[1024,128]{1,0:T(8,128)}) custom-call(s32[2]{0:T(128)} %pad_add_fusion.place, s32[8]{0:T(128)} %bitcast.109, bf16[4,64,1536]{2,1,0:T(8,128)(2,1)} %copy-done.5, bf16[4,64,1536]{2,1,0:T(8,128)(2,1)} %copy-done.6, ...), custom_call_target="tpu_custom_call" | custom-call | bytes 57600000 | tf_op jit(solution)/shard_map/stream_attention/pallas_call | solution.py:234
  155.8 1.3 copy.25
  157.1 15.3 %all_to_all.26 = bf16[8,128,192]{1,2,0:T(8,128)(2,1)S(1)} all-to-all(bf16[8,128,192]{1,2,0:T(8,128)(2,1)S(1)} %copy.25), channel_id=1, replica_groups=mesh['ctx'=8,'fsdp'=4] {'ctx'}, dimensions={0} | all-to-all | bytes 786432 | tf_op jit(solution)/shard_map/all_to_all | solution.py:65
  173.4 4.7 home_forward.1
  178.0 1.5 collective-permute-start.28
  179.6 2.0 collective-permute-start.26
  181.6 8.7 %collective-permute-done.28 = bf16[128,1536]{1,0:T(8,128)(2,1)S(1)} collective-permute-done((bf16[128,1536]{1,0:T(8,128)(2,1)}, bf16[128,1536]{1,0:T(8,128)(2,1)S(1)}, u32[]{:S(2)}, u32[]{:S(2)}) %collective-permute-start.28) | collective-permute-done | bytes 393248 | tf_op jit(solution)/shard_map/ppermute | solution.py:74
  190.3 22.8 %collective-permute-done.27 = bf16[128,1536]{1,0:T(8,128)(2,1)S(1)} collective-permute-done((bf16[128,1536]{1,0:T(8,128)(2,1)}, bf16[128,1536]{1,0:T(8,128)(2,1)S(1)}, u32[]{:S(2)}, u32[]{:S(2)}) %collective-permute-start.27) | collective-permute-done | bytes 393248 | tf_op jit(solution)/shard_map/ppermute | solution.py:74
  213.1 2.3 pad_maximum_fusion.1
  216.8 3.5 collective-permute-start.34
  220.3 2.5 collective-permute-start.20
  222.8 2.9 collective-permute-done.21.refs_2_
  225.7 2.3 collective-permute-start.22
  229.7 3.0 collective-permute-done.34
  232.8 3.6 collective-permute-start.31
  236.6 19.4 %collective-permute-done.30 = bf16[512,192]{1,0:T(8,128)(2,1)S(1)} collective-permute-done((bf16[512,192]{1,0:T(8,128)(2,1)S(1)}, bf16[512,192]{1,0:T(8,128)(2,1)S(1)}, u32[]{:S(2)}, u32[]{:S(2)}) %collective-permute-start.30) | collective-permute-done | bytes 196640 | tf_op jit(solution)/shard_map/ppermute | solution.py:74
  257.8 28.5 %near_experts.1 = (bf16[128,1536]{1,0:T(8,128)(2,1)}, bf16[128,1536]{1,0:T(8,128)(2,1)}, bf16[128,1536]{1,0:T(8,128)(2,1)}, bf16[128,1536]{1,0:T(8,128)(2,1)}, b...) custom-call(s32[2]{0:T(128)} %pad_add_fusion.place, ...), custom_call_target="tpu_custom_call" | custom-call | bytes 93600000 | tf_op jit(solution)/shard_map/near_experts/pallas_call | solution.py:607
  286.3 2.4 collective-permute-start.38
  288.9 1.5 collective-permute-done.38
  291.5 1.3 collective-permute-start.39
  292.8 10.4 %collective-permute-done.39.refs_2_ = bf16[128,1664]{1,0:T(8,128)(2,1)S(1)} collective-permute-done((bf16[128,1664]{1,0:T(8,128)(2,1)S(1)}, bf16[128,1664]{1,0:T(8,128)(2,1)S(1)}, u32[]{:S(2)}, u32[]{:S(2)}) %collective-permute-start.39) | collective-permute-done | bytes 426016 | tf_op jit(solution)/shard_map/ppermute | solution.py:74
  304.0 6.9 %home_turn.1 = (f32[128,1536]{1,0:T(8,128)}, bf16[8,128,384]{2,1,0:T(8,128)(2,1)}, f32[16,1536]{1,0:T(8,128)}) custom-call(bf16[128,1664]{1,0:T(8,128)(2,1)} %get-tuple-element.70.refs_0_, bf16[128,1664]{1,0:T(8,128)(2,1)} %copy-done.18, bf16[128,1664]{1,0:T(8,128)(2,1)} %copy-done.19, f32[128,1536]{1,0:T(8,128)} %get-tuple-element.53.refs_3_, ...), custom_call_target="tpu_custom_call" | custom-call | bytes 25200000 | tf_op jit(solution)/shard_map/home_turn/pallas_call | solution.py:340
  310.9 19.8 %all-to-all-start.1 = ((bf16[8,128,384]{2,1,0:T(8,128)(2,1)}), bf16[8,128,384]{2,1,0:T(8,128)(2,1)S(1)}, u32[]{:S(2)}, u32[]{:S(2)}) async-start(bf16[8,128,384]{2,1,0:T(8,128)(2,1)} %get-tuple-element.73), calls=%async_computation.1 | async-start | bytes 1572864 | tf_op jit(solution)/shard_map/all_to_all | solution.py:65
  330.7 1.3 copy.28
  332.3 1.2 copy.27
  333.5 1.2 collective-permute-start.35
  334.7 22.8 %collective-permute-done.36 = bf16[4,512,192]{1,2,0:T(8,128)(2,1)} collective-permute-done((bf16[4,512,192]{1,2,0:T(8,128)(2,1)}, bf16[4,512,192]{1,2,0:T(8,128)(2,1)}, u32[]{:S(2)}, u32[]{:S(2)}) %collective-permute-start.36) | collective-permute-done | bytes 786464 | tf_op jit(solution)/shard_map/ppermute | solution.py:74
  357.5 2.2 copy.30.pieces3
  359.7 14.5 %collective-permute-done.35 = bf16[4,512,192]{1,2,0:T(8,128)(2,1)S(1)} collective-permute-done((bf16[4,512,192]{1,2,0:T(8,128)(2,1)}, bf16[4,512,192]{1,2,0:T(8,128)(2,1)S(1)}, u32[]{:S(2)}, u32[]{:S(2)}) %collective-permute-start.35) | collective-permute-done | bytes 786464 | tf_op jit(solution)/shard_map/ppermute | solution.py:74
  374.2 11.2 %copy.29.pieces2 = bf16[4,512,192]{2,1,0:T(8,128)(2,1)} copy(bf16[4,512,192]{1,2,0:T(8,128)(2,1)S(1)} %collective-permute-done.35) | data formatting | bytes 1572864 | tf_op jit(solution)/shard_map/ppermute | solution.py:74
  386.3 17.7 %stream_backward.1 = (bf16[1024,320]{1,0:T(8,128)(2,1)}, bf16[4,400,512]{2,1,0:T(8,128)(2,1)}) custom-call(s32[2]{0:T(128)} %pad_add_fusion.place, s32[8]{0:T(128)} %bitcast.110, bf16[4,512,192]{2,1,0:T(8,128)(2,1)} %copy-done.1, bf16[4,512,192]{2,1,0:T(8,128)(2,1)} %copy-done, bf16[4,512,192]{2,1,0:T(8,128)(2,1)} %copy.29.pieces2, ...), custom_call_target="tpu_custom_call" | custom-call | bytes 61200000 | tf_op jit(solution)/shard_map/stream_backward/pallas_call | solution.py:410
  404.0 1.3 slice_bitcast_fusion.1
  406.0 1.3 collective-permute-done.41
  407.4 1.2 collective-permute-start.42
  408.6 9.5 %collective-permute-done.42 = bf16[400,512]{1,0:T(8,128)(2,1)S(1)} collective-permute-done((bf16[400,512]{1,0:T(8,128)(2,1)S(1)}, bf16[400,512]{1,0:T(8,128)(2,1)S(1)}, u32[]{:S(2)}, u32[]{:S(2)}) %collective-permute-start.42) | collective-permute-done | bytes 409632 | tf_op jit(solution)/shard_map/ppermute | solution.py:74
  419.1 1.3 collective-permute-start.24
  421.5 6.0 %all-to-all-start.2 = ((bf16[8,128,320]{1,2,0:T(8,128)(2,1)}), bf16[8,128,320]{1,2,0:T(8,128)(2,1)S(1)}, u32[]{:S(2)}, u32[]{:S(2)}) async-start(bf16[8,128,320]{1,2,0:T(8,128)(2,1)} %copy.31), calls=%async_computation.2 | async-start | bytes 1310720 | tf_op jit(solution)/shard_map/all_to_all | solution.py:65
  427.7 1.2 collective-permute-start.25
  428.9 8.6 %collective-permute-done.25 = bf16[128,1536]{1,0:T(8,128)(2,1)S(1)} collective-permute-done((bf16[128,1536]{1,0:T(8,128)(2,1)S(1)}, bf16[128,1536]{1,0:T(8,128)(2,1)S(1)}, u32[]{:S(2)}, u32[]{:S(2)}) %collective-permute-start.25) | collective-permute-done | bytes 393248 | tf_op jit(solution)/shard_map/ppermute | solution.py:74
  438.4 18.0 %all-to-all-done.2 = bf16[8,128,320]{1,2,0:T(8,128)(2,1)S(1)} async-done(((bf16[8,128,320]{1,2,0:T(8,128)(2,1)}), bf16[8,128,320]{1,2,0:T(8,128)(2,1)S(1)}, u32[]{:S(2)}, u32[]{:S(2)}) %all-to-all-start.2) | async-done | bytes 655392 | tf_op jit(solution)/shard_map/all_to_all | solution.py:65
  456.4 1.2 copy.32.d_home
  457.6 7.5 %home_backward.1 = bf16[128,1536]{1,0:T(8,128)(2,1)} custom-call(bf16[8,128,320]{2,1,0:T(8,128)(2,1)} %copy.32.d_home, bf16[128,1536]{1,0:T(8,128)(2,1)} %bitcast.71, bf16[16,1536]{1,0:T(8,128)(2,1)} %bitcast.78, f32[128,1536]{1,0:T(8,128)} %get-tuple-element.80.d_middle, bf16[1536,2560]{1,0:T(8,128)(2,1)} %all-gather.11.cloned.1.call-done.weight), custom_call_target="tpu_custom_call" | custom-call | bytes 28800000 | tf_op jit(solution)/shard_map/home_backward/pallas_call | solution.py:452
  465.0 107.5 %far_weight_grads.1 = f32[2,1536,3072]{2,1,0:T(8,128)} custom-call(s32[2]{0:T(128)} %pad_add_fusion.place, bf16[16,1536]{1,0:T(8,128)(2,1)} %bitcast.79, bf16[32,128,1536]{2,1,0:T(8,128)(2,1)} %all-gather.13.cloned.1.call-done.second_ref, bf16[32,144,1536]{2,1,0:T(8,128)(2,1)} %all-gather.9.cloned.1.call-done.grads_ref, bf16[2,1536,3072]{2,1,0:T(8,128)(2,1)} %w_down.1, ...), custom_call_target="tpu_custom_call" | custom-call | bytes 288000000 | tf_op jit(solution)/shard_map/far_weight_grads/pallas_call | solution.py:803
  572.5 6.7 %collected.1 = (f32[384,2560]{1,0:T(8,128)}, f32[384,1536]{1,0:T(8,128)}, f32[16,384]{1,0:T(8,128)}, f32[384,1]{1,0:T(8,128)}) custom-call(bf16[8,400,512]{2,1,0:T(8,128)(2,1)} %bitcast.72, bf16[384,2560]{1,0:T(8,128)(2,1)} %own_weight.1), custom_call_target="tpu_custom_call" | custom-call | bytes 25200000 | tf_op jit(solution)/shard_map/collected/pallas_call | solution.py:493
  579.2 1.3 slice_reduce_fusion
  580.5 1.3 slice_bitcast_fusion.2
  (161 shorter events, 27.1 us)
Async XLA Ops:
  7.2 166.2 %all-gather.7.cloned.1.call-start = ((), (), s32[]{:S(2)}) async-start(), calls=%async_computation.3 | async-start | bytes 5898240 | tf_op jit(solution)/shard_map/all_gather | solution.py:69
  7.9 295.3 %all-gather.9.cloned.1.call-start = ((), (), s32[]{:S(2)}) async-start(), calls=%async_computation.4 | async-start | bytes 15925248 | tf_op jit(solution)/shard_map/all_gather | solution.py:123
  10.2 5.7 collective-permute-start.6
  10.9 4.7 collective-permute-start.7
  13.4 38.1 %copy-start.12 = (bf16[384,320]{1,0:T(8,128)(2,1)}, bf16[384,320]{1,0:T(8,128)(2,1)S(1)}, u32[]{:S(2)}) copy-start(bf16[384,320]{1,0:T(8,128)(2,1)S(1)} %pad_maximum_fusion.6.refs_4_) | copy-start | bytes 737284
  13.4 26.8 %collective-permute-start.10 = (bf16[384,320]{1,0:T(8,128)(2,1)S(1)}, bf16[384,320]{1,0:T(8,128)(2,1)S(1)}, u32[]{:S(2)}, u32[]{:S(2)}) collective-permute-start(bf16[384,320]{1,0:T(8,128)(2,1)S(1)} %pad_maximum_fusion.6.refs_4_), channel_id=1, source_target_pairs={{0,2},{1,3},{2,0},{3,1},{4,6},{5,7},{6,4},{7,5},{8,10},{9,11},{10,... | collective-permute-start | bytes 737288 | tf_op jit(solution)/shard_map/ppermute | solution.py:74
  14.7 36.8 %collective-permute-start.9 = (bf16[384,320]{1,0:T(8,128)(2,1)S(1)}, bf16[384,320]{1,0:T(8,128)(2,1)S(1)}, u32[]{:S(2)}, u32[]{:S(2)}) collective-permute-start(bf16[384,320]{1,0:T(8,128)(2,1)S(1)} %pad_maximum_fusion.6.refs_4_), channel_id=1, source_target_pairs={{0,1},{1,0},{2,3},{3,2},{4,5},{5,4},{6,7},{7,6},{8,9},{9,8},{10,11... | collective-permute-start | bytes 737288 | tf_op jit(solution)/shard_map/ppermute | solution.py:74
  15.4 8.5 %collective-permute-start.2 = (bf16[64,1536]{1,0:T(8,128)(2,1)S(1)}, bf16[64,1536]{1,0:T(8,128)(2,1)S(1)}, u32[]{:S(2)}, u32[]{:S(2)}) collective-permute-start(bf16[64,1536]{1,0:T(8,128)(2,1)S(1)} %get-tuple-element.97), channel_id=1, source_target_pairs={{0,24},{4,28},{8,16},{12,20},{16,8},{20,12},{24,0},{28,4},{1,25},{... | collective-permute-start | bytes 589832 | tf_op jit(solution)/shard_map/ppermute | solution.py:74
  15.6 1.7 collective-permute-start.8
  15.9 22.9 %collective-permute-start.1 = (bf16[64,1536]{1,0:T(8,128)(2,1)S(1)}, bf16[64,1536]{1,0:T(8,128)(2,1)S(1)}, u32[]{:S(2)}, u32[]{:S(2)}) collective-permute-start(bf16[64,1536]{1,0:T(8,128)(2,1)S(1)} %get-tuple-element.97), channel_id=1, source_target_pairs={{0,16},{4,20},{8,24},{12,28},{16,0},{20,4},{24,8},{28,12},{1,17},{... | collective-permute-start | bytes 589832 | tf_op jit(solution)/shard_map/ppermute | solution.py:74
  17.4 21.4 %collective-permute-start = (bf16[64,1536]{1,0:T(8,128)(2,1)S(1)}, bf16[64,1536]{1,0:T(8,128)(2,1)S(1)}, u32[]{:S(2)}, u32[]{:S(2)}) collective-permute-start(bf16[64,1536]{1,0:T(8,128)(2,1)S(1)} %get-tuple-element.97), channel_id=1, source_target_pairs={{0,8},{4,12},{8,0},{12,4},{16,24},{20,28},{24,16},{28,20},{1,9},{5... | collective-permute-start | bytes 589832 | tf_op jit(solution)/shard_map/ppermute | solution.py:74
  19.5 33.5 %copy-start.30 = (s32[1,128,2]{1,2,0:T(2,128)S(1)}, s32[1,128,2]{1,2,0:T(2,128)}, u32[]{:S(2)}) copy-start(s32[1,128,2]{1,2,0:T(2,128)} %param.18) | copy-start | bytes 3076
  20.1 33.2 %copy-start.11 = (bf16[1,128,1536]{2,1,0:T(8,128)(2,1)S(1)}, bf16[1,128,1536]{2,1,0:T(8,128)(2,1)}, u32[]{:S(2)}) copy-start(bf16[1,128,1536]{2,1,0:T(8,128)(2,1)} %param.19) | copy-start | bytes 1179652
  23.9 18.1 %collective-permute-start.5 = (bf16[64,1536]{1,0:T(8,128)(2,1)S(1)}, bf16[64,1536]{1,0:T(8,128)(2,1)S(1)}, u32[]{:S(2)}, u32[]{:S(2)}) collective-permute-start(bf16[64,1536]{1,0:T(8,128)(2,1)S(1)} %get-tuple-element.98), channel_id=1, source_target_pairs={{0,24},{4,28},{8,16},{12,20},{16,8},{20,12},{24,0},{28,4},{1,25},{... | collective-permute-start | bytes 589832 | tf_op jit(solution)/shard_map/ppermute | solution.py:74
  38.7 12.6 %collective-permute-start.4 = (bf16[64,1536]{1,0:T(8,128)(2,1)S(1)}, bf16[64,1536]{1,0:T(8,128)(2,1)S(1)}, u32[]{:S(2)}, u32[]{:S(2)}) collective-permute-start(bf16[64,1536]{1,0:T(8,128)(2,1)S(1)} %get-tuple-element.98), channel_id=1, source_target_pairs={{0,16},{4,20},{8,24},{12,28},{16,0},{20,4},{24,8},{28,12},{1,17},{... | collective-permute-start | bytes 589832 | tf_op jit(solution)/shard_map/ppermute | solution.py:74
  38.8 12.6 %collective-permute-start.3 = (bf16[64,1536]{1,0:T(8,128)(2,1)S(1)}, bf16[64,1536]{1,0:T(8,128)(2,1)S(1)}, u32[]{:S(2)}, u32[]{:S(2)}) collective-permute-start(bf16[64,1536]{1,0:T(8,128)(2,1)S(1)} %get-tuple-element.98), channel_id=1, source_target_pairs={{0,8},{4,12},{8,0},{12,4},{16,24},{20,28},{24,16},{28,20},{1,9},{5... | collective-permute-start | bytes 589832 | tf_op jit(solution)/shard_map/ppermute | solution.py:74
  40.2 84.5 %copy-start.5 = (bf16[4,64,1536]{2,1,0:T(8,128)(2,1)}, bf16[4,64,1536]{2,1,0:T(8,128)(2,1)S(1)}, u32[]{:S(2)}) copy-start(bf16[4,64,1536]{2,1,0:T(8,128)(2,1)S(1)} %pad_maximum_fusion.4.refs_0_) | copy-start | bytes 2359300
  40.2 11.3 %collective-permute-start.11 = (bf16[384,320]{1,0:T(8,128)(2,1)S(1)}, bf16[384,320]{1,0:T(8,128)(2,1)S(1)}, u32[]{:S(2)}, u32[]{:S(2)}) collective-permute-start(bf16[384,320]{1,0:T(8,128)(2,1)S(1)} %collective-permute-done.10.refs_6_), channel_id=1, source_target_pairs={{0,1},{1,0},{2,3},{3,2},{4,5},{5,4},{6,7},{7,6},{8,9},{9,8},{10,11... | collective-permute-start | bytes 737288 | tf_op jit(solution)/shard_map/ppermute | solution.py:74
  51.5 73.2 %copy-start.6 = (bf16[4,64,1536]{2,1,0:T(8,128)(2,1)}, bf16[4,64,1536]{2,1,0:T(8,128)(2,1)S(1)}, u32[]{:S(2)}) copy-start(bf16[4,64,1536]{2,1,0:T(8,128)(2,1)S(1)} %pad_maximum_fusion.5.refs_1_) | copy-start | bytes 2359300
  51.5 73.2 %copy-start.26 = (bf16[384,320]{1,0:T(8,128)(2,1)}, bf16[384,320]{1,0:T(8,128)(2,1)S(1)}, u32[]{:S(2)}) copy-start(bf16[384,320]{1,0:T(8,128)(2,1)S(1)} %collective-permute-done.9.refs_5_) | copy-start | bytes 737284
  51.6 18.5 %collective-permute-start.12 = (bf16[4,64,1536]{2,1,0:T(8,128)(2,1)S(1)}, bf16[4,64,1536]{2,1,0:T(8,128)(2,1)}, u32[]{:S(2)}, u32[]{:S(2)}) collective-permute-start(bf16[4,64,1536]{2,1,0:T(8,128)(2,1)S(1)} %pad_maximum_fusion.4.refs_0_), channel_id=1, source_target_pairs={{0,4},{4,0},{8,12},{12,8},{16,20},{20,16},{24,28},{28,24},{1,5},{5... | collective-permute-start | bytes 2359304 | tf_op jit(solution)/shard_map/ppermute | solution.py:74
  51.9 35.0 %collective-permute-start.13 = (bf16[4,64,1536]{2,1,0:T(8,128)(2,1)S(1)}, bf16[4,64,1536]{2,1,0:T(8,128)(2,1)}, u32[]{:S(2)}, u32[]{:S(2)}) collective-permute-start(bf16[4,64,1536]{2,1,0:T(8,128)(2,1)S(1)} %pad_maximum_fusion.5.refs_1_), channel_id=1, source_target_pairs={{0,4},{4,0},{8,12},{12,8},{16,20},{20,16},{24,28},{28,24},{1,5},{5... | collective-permute-start | bytes 2359304 | tf_op jit(solution)/shard_map/ppermute | solution.py:74
  53.2 71.5 %copy-start.14 = (s32[1,128,2]{2,1,0:T(8,128)}, s32[1,128,2]{2,1,0:T(8,128)S(1)}, u32[]{:S(2)}) copy-start(s32[1,128,2]{2,1,0:T(8,128)S(1)} %copy.23) | copy-start | bytes 3076
  53.4 71.7 %copy-start.2 = (bf16[144,1536]{1,0:T(8,128)(2,1)}, bf16[144,1536]{1,0:T(8,128)(2,1)S(1)}, u32[]{:S(2)}) copy-start(bf16[144,1536]{1,0:T(8,128)(2,1)S(1)} %fusion.4.refs_4_) | copy-start | bytes 1327108
  86.9 11.9 %collective-permute-start.16 = (bf16[144,1536]{1,0:T(8,128)(2,1)S(1)}, bf16[144,1536]{1,0:T(8,128)(2,1)S(1)}, u32[]{:S(2)}, u32[]{:S(2)}) collective-permute-start(bf16[144,1536]{1,0:T(8,128)(2,1)S(1)} %fusion.4.refs_4_), channel_id=1, source_target_pairs={{0,24},{4,28},{8,16},{12,20},{16,8},{20,12},{24,0},{28,4},{1,25},{... | collective-permute-start | bytes 1327112 | tf_op jit(solution)/shard_map/ppermute | solution.py:74
  87.9 35.3 %collective-permute-start.15 = (bf16[144,1536]{1,0:T(8,128)(2,1)S(1)}, bf16[144,1536]{1,0:T(8,128)(2,1)S(1)}, u32[]{:S(2)}, u32[]{:S(2)}) collective-permute-start(bf16[144,1536]{1,0:T(8,128)(2,1)S(1)} %fusion.4.refs_4_), channel_id=1, source_target_pairs={{0,16},{4,20},{8,24},{12,28},{16,0},{20,4},{24,8},{28,12},{1,17},{... | collective-permute-start | bytes 1327112 | tf_op jit(solution)/shard_map/ppermute | solution.py:74
  87.9 35.3 %collective-permute-start.14 = (bf16[144,1536]{1,0:T(8,128)(2,1)S(1)}, bf16[144,1536]{1,0:T(8,128)(2,1)S(1)}, u32[]{:S(2)}, u32[]{:S(2)}) collective-permute-start(bf16[144,1536]{1,0:T(8,128)(2,1)S(1)} %fusion.4.refs_4_), channel_id=1, source_target_pairs={{0,8},{4,12},{8,0},{12,4},{16,24},{20,28},{24,16},{28,20},{1,9},{5... | collective-permute-start | bytes 1327112 | tf_op jit(solution)/shard_map/ppermute | solution.py:74
  124.7 294.3 %all-gather.13.cloned.1.call-start = ((), (), s32[]{:S(2)}) async-start(), calls=%async_computation.6 | async-start | bytes 14155776 | tf_op jit(solution)/shard_map/all_gather | solution.py:123
  124.8 9.1 %collective-permute-start.18 = (bf16[144,1536]{1,0:T(8,128)(2,1)S(1)}, bf16[144,1536]{1,0:T(8,128)(2,1)S(1)}, u32[]{:S(2)}, u32[]{:S(2)}) collective-permute-start(bf16[144,1536]{1,0:T(8,128)(2,1)S(1)} %fusion.4.refs_4_), channel_id=1, source_target_pairs={{0,2},{1,3},{2,0},{3,1},{4,6},{5,7},{6,4},{7,5},{8,10},{9,11},{10,... | collective-permute-start | bytes 1327112 | tf_op jit(solution)/shard_map/ppermute | solution.py:74
  125.1 29.8 %collective-permute-start.17 = (bf16[144,1536]{1,0:T(8,128)(2,1)S(1)}, bf16[144,1536]{1,0:T(8,128)(2,1)S(1)}, u32[]{:S(2)}, u32[]{:S(2)}) collective-permute-start(bf16[144,1536]{1,0:T(8,128)(2,1)S(1)} %fusion.4.refs_4_), channel_id=1, source_target_pairs={{0,1},{1,0},{2,3},{3,2},{4,5},{5,4},{6,7},{7,6},{8,9},{9,8},{10,11... | collective-permute-start | bytes 1327112 | tf_op jit(solution)/shard_map/ppermute | solution.py:74
  133.9 21.0 %copy-start.15 = (bf16[144,1536]{1,0:T(8,128)(2,1)}, bf16[144,1536]{1,0:T(8,128)(2,1)S(1)}, u32[]{:S(2)}) copy-start(bf16[144,1536]{1,0:T(8,128)(2,1)S(1)} %collective-permute-done.18.refs_6_) | copy-start | bytes 1327108
  133.9 21.0 %collective-permute-start.19 = (bf16[144,1536]{1,0:T(8,128)(2,1)S(1)}, bf16[144,1536]{1,0:T(8,128)(2,1)S(1)}, u32[]{:S(2)}, u32[]{:S(2)}) collective-permute-start(bf16[144,1536]{1,0:T(8,128)(2,1)S(1)} %collective-permute-done.18.refs_6_), channel_id=1, source_target_pairs={{0,1},{1,0},{2,3},{3,2},{4,5},{5,4},{6,7},{7,6},{8,9},{9,8},{10,11... | collective-permute-start | bytes 1327112 | tf_op jit(solution)/shard_map/ppermute | solution.py:74
  154.9 23.1 %copy-start.16 = (bf16[144,1536]{1,0:T(8,128)(2,1)}, bf16[144,1536]{1,0:T(8,128)(2,1)S(1)}, u32[]{:S(2)}) copy-start(bf16[144,1536]{1,0:T(8,128)(2,1)S(1)} %collective-permute-done.17.refs_5_) | copy-start | bytes 1327108
  178.0 12.3 %collective-permute-start.28 = (bf16[128,1536]{1,0:T(8,128)(2,1)}, bf16[128,1536]{1,0:T(8,128)(2,1)S(1)}, u32[]{:S(2)}, u32[]{:S(2)}) collective-permute-start(bf16[128,1536]{1,0:T(8,128)(2,1)} %get-tuple-element.54.refs_0_.refs_4_), channel_id=1, source_target_pairs={{0,24},{4,28},{8,16},{12,20},{16,8},{20,12},{24,0},{28,4},{1,25},{... | collective-permute-start | bytes 1179656 | tf_op jit(solution)/shard_map/ppermute | solution.py:74
  179.6 33.5 %collective-permute-start.27 = (bf16[128,1536]{1,0:T(8,128)(2,1)}, bf16[128,1536]{1,0:T(8,128)(2,1)S(1)}, u32[]{:S(2)}, u32[]{:S(2)}) collective-permute-start(bf16[128,1536]{1,0:T(8,128)(2,1)} %get-tuple-element.54.refs_0_.refs_4_), channel_id=1, source_target_pairs={{0,16},{4,20},{8,24},{12,28},{16,0},{20,4},{24,8},{28,12},{1,17},{... | collective-permute-start | bytes 1179656 | tf_op jit(solution)/shard_map/ppermute | solution.py:74
  179.6 33.5 %collective-permute-start.26 = (bf16[128,1536]{1,0:T(8,128)(2,1)}, bf16[128,1536]{1,0:T(8,128)(2,1)S(1)}, u32[]{:S(2)}, u32[]{:S(2)}) collective-permute-start(bf16[128,1536]{1,0:T(8,128)(2,1)} %get-tuple-element.54.refs_0_.refs_4_), channel_id=1, source_target_pairs={{0,8},{4,12},{8,0},{12,4},{16,24},{20,28},{24,16},{28,20},{1,9},{5... | collective-permute-start | bytes 1179656 | tf_op jit(solution)/shard_map/ppermute | solution.py:74
  215.5 242.1 %all-gather.11.cloned.1.call-start = ((), (), s32[]{:S(2)}) async-start(), calls=%async_computation.5 | async-start | bytes 9830400 | tf_op jit(solution)/shard_map/all_gather | solution.py:69
  216.4 9.3 %collective-permute-start.21 = (bf16[128,1536]{1,0:T(8,128)(2,1)S(1)}, bf16[128,1536]{1,0:T(8,128)(2,1)S(1)}, u32[]{:S(2)}, u32[]{:S(2)}) collective-permute-start(bf16[128,1536]{1,0:T(8,128)(2,1)S(1)} %copy-done.3), channel_id=1, source_target_pairs={{0,2},{1,3},{2,0},{3,1},{4,6},{5,7},{6,4},{7,5},{8,10},{9,11},{10,... | collective-permute-start | bytes 1179656 | tf_op jit(solution)/shard_map/ppermute | solution.py:74
  216.7 12.0 %collective-permute-start.33 = (bf16[512,192]{1,0:T(8,128)(2,1)S(1)}, bf16[512,192]{1,0:T(8,128)(2,1)S(1)}, u32[]{:S(2)}, u32[]{:S(2)}) collective-permute-start(bf16[512,192]{1,0:T(8,128)(2,1)S(1)} %get-tuple-element.94), channel_id=1, source_target_pairs={{0,16},{4,20},{8,24},{12,28},{16,0},{20,4},{24,8},{28,12},{1,17},{... | collective-permute-start | bytes 589832 | tf_op jit(solution)/shard_map/ppermute | solution.py:74
  216.8 13.0 %collective-permute-start.32 = (bf16[512,192]{1,0:T(8,128)(2,1)S(1)}, bf16[512,192]{1,0:T(8,128)(2,1)S(1)}, u32[]{:S(2)}, u32[]{:S(2)}) collective-permute-start(bf16[512,192]{1,0:T(8,128)(2,1)S(1)} %get-tuple-element.94), channel_id=1, source_target_pairs={{0,8},{4,12},{8,0},{12,4},{16,24},{20,28},{24,16},{28,20},{1,9},{5... | collective-permute-start | bytes 589832 | tf_op jit(solution)/shard_map/ppermute | solution.py:74
  216.8 15.9 %collective-permute-start.34 = (bf16[512,192]{1,0:T(8,128)(2,1)S(1)}, bf16[512,192]{1,0:T(8,128)(2,1)S(1)}, u32[]{:S(2)}, u32[]{:S(2)}) collective-permute-start(bf16[512,192]{1,0:T(8,128)(2,1)S(1)} %get-tuple-element.94), channel_id=1, source_target_pairs={{0,24},{4,28},{8,16},{12,20},{16,8},{20,12},{24,0},{28,4},{1,25},{... | collective-permute-start | bytes 589832 | tf_op jit(solution)/shard_map/ppermute | solution.py:74
  220.3 36.0 %collective-permute-start.20 = (bf16[128,1536]{1,0:T(8,128)(2,1)S(1)}, bf16[128,1536]{1,0:T(8,128)(2,1)S(1)}, u32[]{:S(2)}, u32[]{:S(2)}) collective-permute-start(bf16[128,1536]{1,0:T(8,128)(2,1)S(1)} %copy-done.3), channel_id=1, source_target_pairs={{0,1},{1,0},{2,3},{3,2},{4,5},{5,4},{6,7},{7,6},{8,9},{9,8},{10,11... | collective-permute-start | bytes 1179656 | tf_op jit(solution)/shard_map/ppermute | solution.py:74
  225.7 30.5 %copy-start.20 = (bf16[128,1536]{1,0:T(8,128)(2,1)}, bf16[128,1536]{1,0:T(8,128)(2,1)S(1)}, u32[]{:S(2)}) copy-start(bf16[128,1536]{1,0:T(8,128)(2,1)S(1)} %collective-permute-done.21.refs_2_) | copy-start | bytes 1179652
  225.7 30.6 %collective-permute-start.22 = (bf16[128,1536]{1,0:T(8,128)(2,1)S(1)}, bf16[128,1536]{1,0:T(8,128)(2,1)S(1)}, u32[]{:S(2)}, u32[]{:S(2)}) collective-permute-start(bf16[128,1536]{1,0:T(8,128)(2,1)S(1)} %collective-permute-done.21.refs_2_), channel_id=1, source_target_pairs={{0,1},{1,0},{2,3},{3,2},{4,5},{5,4},{6,7},{7,6},{8,9},{9,8},{10,11... | collective-permute-start | bytes 1179656 | tf_op jit(solution)/shard_map/ppermute | solution.py:74
  228.7 27.3 %collective-permute-start.30 = (bf16[512,192]{1,0:T(8,128)(2,1)S(1)}, bf16[512,192]{1,0:T(8,128)(2,1)S(1)}, u32[]{:S(2)}, u32[]{:S(2)}) collective-permute-start(bf16[512,192]{1,0:T(8,128)(2,1)S(1)} %get-tuple-element.95), channel_id=1, source_target_pairs={{0,16},{4,20},{8,24},{12,28},{16,0},{20,4},{24,8},{28,12},{1,17},{... | collective-permute-start | bytes 589832 | tf_op jit(solution)/shard_map/ppermute | solution.py:74
  229.7 26.3 %collective-permute-start.29 = (bf16[512,192]{1,0:T(8,128)(2,1)S(1)}, bf16[512,192]{1,0:T(8,128)(2,1)S(1)}, u32[]{:S(2)}, u32[]{:S(2)}) collective-permute-start(bf16[512,192]{1,0:T(8,128)(2,1)S(1)} %get-tuple-element.95), channel_id=1, source_target_pairs={{0,8},{4,12},{8,0},{12,4},{16,24},{20,28},{24,16},{28,20},{1,9},{5... | collective-permute-start | bytes 589832 | tf_op jit(solution)/shard_map/ppermute | solution.py:74
  232.8 23.2 %collective-permute-start.31 = (bf16[512,192]{1,0:T(8,128)(2,1)S(1)}, bf16[512,192]{1,0:T(8,128)(2,1)S(1)}, u32[]{:S(2)}, u32[]{:S(2)}) collective-permute-start(bf16[512,192]{1,0:T(8,128)(2,1)S(1)} %get-tuple-element.95), channel_id=1, source_target_pairs={{0,24},{4,28},{8,16},{12,20},{16,8},{20,12},{24,0},{28,4},{1,25},{... | collective-permute-start | bytes 589832 | tf_op jit(solution)/shard_map/ppermute | solution.py:74
  236.6 94.2 %copy-start = (bf16[4,512,192]{2,1,0:T(8,128)(2,1)}, bf16[4,512,192]{2,1,0:T(8,128)(2,1)S(1)}, u32[]{:S(2)}) copy-start(bf16[4,512,192]{2,1,0:T(8,128)(2,1)S(1)} %pad_maximum_fusion.3.pieces1) | copy-start | bytes 2359300
  256.3 76.0 %copy-start.1 = (bf16[4,512,192]{2,1,0:T(8,128)(2,1)}, bf16[4,512,192]{2,1,0:T(8,128)(2,1)S(1)}, u32[]{:S(2)}) copy-start(bf16[4,512,192]{2,1,0:T(8,128)(2,1)S(1)} %pad_maximum_fusion.2.pieces0) | copy-start | bytes 2359300
  286.3 4.0 collective-permute-start.38
  288.8 4.0 collective-permute-start.37
  291.5 11.7 %collective-permute-start.39 = (bf16[128,1664]{1,0:T(8,128)(2,1)S(1)}, bf16[128,1664]{1,0:T(8,128)(2,1)S(1)}, u32[]{:S(2)}, u32[]{:S(2)}) collective-permute-start(bf16[128,1664]{1,0:T(8,128)(2,1)S(1)} %add_convert_fusion), channel_id=1, source_target_pairs={{0,2},{1,3},{2,0},{3,1},{4,6},{5,7},{6,4},{7,5},{8,10},{9,11},{10,... | collective-permute-start | bytes 1277960 | tf_op jit(solution)/shard_map/ppermute | solution.py:74
  310.9 74.5 %all-to-all-start.1 = ((bf16[8,128,384]{2,1,0:T(8,128)(2,1)}), bf16[8,128,384]{2,1,0:T(8,128)(2,1)S(1)}, u32[]{:S(2)}, u32[]{:S(2)}) async-start(bf16[8,128,384]{2,1,0:T(8,128)(2,1)} %get-tuple-element.73), calls=%async_computation.1 | async-start | bytes 1572864 | tf_op jit(solution)/shard_map/all_to_all | solution.py:65
  330.7 241.8 %all-gather.15.cloned.1.call-start = ((), (), s32[]{:S(2)}) async-start(), calls=%async_computation.7 | async-start | bytes 3686400 | tf_op jit(solution)/shard_map/all_gather | solution.py:921
  332.0 25.5 %collective-permute-start.36 = (bf16[4,512,192]{1,2,0:T(8,128)(2,1)}, bf16[4,512,192]{1,2,0:T(8,128)(2,1)}, u32[]{:S(2)}, u32[]{:S(2)}) collective-permute-start(bf16[4,512,192]{1,2,0:T(8,128)(2,1)} %copy.28), channel_id=1, source_target_pairs={{0,4},{4,0},{8,12},{12,8},{16,20},{20,16},{24,28},{28,24},{1,5},{5... | collective-permute-start | bytes 2359304 | tf_op jit(solution)/shard_map/ppermute | solution.py:74
  333.5 40.7 %collective-permute-start.35 = (bf16[4,512,192]{1,2,0:T(8,128)(2,1)}, bf16[4,512,192]{1,2,0:T(8,128)(2,1)S(1)}, u32[]{:S(2)}, u32[]{:S(2)}) collective-permute-start(bf16[4,512,192]{1,2,0:T(8,128)(2,1)} %copy.27), channel_id=1, source_target_pairs={{0,4},{4,0},{8,12},{12,8},{16,20},{20,16},{24,28},{28,24},{1,5},{5... | collective-permute-start | bytes 2359304 | tf_op jit(solution)/shard_map/ppermute | solution.py:74
  405.4 1.9 collective-permute-start.41
  405.9 2.7 collective-permute-start.40
  407.4 10.7 %collective-permute-start.42 = (bf16[400,512]{1,0:T(8,128)(2,1)S(1)}, bf16[400,512]{1,0:T(8,128)(2,1)S(1)}, u32[]{:S(2)}, u32[]{:S(2)}) collective-permute-start(bf16[400,512]{1,0:T(8,128)(2,1)S(1)} %fusion.1), channel_id=1, source_target_pairs={{0,2},{1,3},{2,0},{3,1},{4,6},{5,7},{6,4},{7,5},{8,10},{9,11},{10,... | collective-permute-start | bytes 1228808 | tf_op jit(solution)/shard_map/ppermute | solution.py:74
  419.1 8.5 %collective-permute-start.24 = (bf16[128,1536]{1,0:T(8,128)(2,1)}, bf16[128,1536]{1,0:T(8,128)(2,1)S(1)}, u32[]{:S(2)}, u32[]{:S(2)}) collective-permute-start(bf16[128,1536]{1,0:T(8,128)(2,1)} %get-tuple-element.58), channel_id=1, source_target_pairs={{0,1},{1,0},{2,3},{3,2},{4,5},{5,4},{6,7},{7,6},{8,9},{9,8},{10,11... | collective-permute-start | bytes 1179656 | tf_op jit(solution)/shard_map/ppermute | solution.py:74
  420.3 8.6 %collective-permute-start.23 = (bf16[128,1536]{1,0:T(8,128)(2,1)S(1)}, bf16[128,1536]{1,0:T(8,128)(2,1)S(1)}, u32[]{:S(2)}, u32[]{:S(2)}) collective-permute-start(bf16[128,1536]{1,0:T(8,128)(2,1)S(1)} %copy-done.31), channel_id=1, source_target_pairs={{0,1},{1,0},{2,3},{3,2},{4,5},{5,4},{6,7},{7,6},{8,9},{9,8},{10,11... | collective-permute-start | bytes 1179656 | tf_op jit(solution)/shard_map/ppermute | solution.py:74
  420.4 17.1 %copy-start.23 = (bf16[128,1536]{1,0:T(8,128)(2,1)S(1)}, bf16[128,1536]{1,0:T(8,128)(2,1)}, u32[]{:S(2)}) copy-start(bf16[128,1536]{1,0:T(8,128)(2,1)} %get-tuple-element.55) | copy-start | bytes 1179652
  421.5 34.9 %all-to-all-start.2 = ((bf16[8,128,320]{1,2,0:T(8,128)(2,1)}), bf16[8,128,320]{1,2,0:T(8,128)(2,1)S(1)}, u32[]{:S(2)}, u32[]{:S(2)}) async-start(bf16[8,128,320]{1,2,0:T(8,128)(2,1)} %copy.31), calls=%async_computation.2 | async-start | bytes 1310720 | tf_op jit(solution)/shard_map/all_to_all | solution.py:65
  427.7 9.8 %collective-permute-start.25 = (bf16[128,1536]{1,0:T(8,128)(2,1)S(1)}, bf16[128,1536]{1,0:T(8,128)(2,1)S(1)}, u32[]{:S(2)}, u32[]{:S(2)}) collective-permute-start(bf16[128,1536]{1,0:T(8,128)(2,1)S(1)} %add_convert_fusion.2), channel_id=1, source_target_pairs={{0,2},{1,3},{2,0},{3,1},{4,6},{5,7},{6,4},{7,5},{8,10},{9,11},{10,... | collective-permute-start | bytes 1179656 | tf_op jit(solution)/shard_map/ppermute | solution.py:74
  (18 other events, 115.8 us)
Sparse Core Ops, SparseCore 0:
  9.6 39.9 all-gather.6
  124.9 82.9 all-gather.8
  215.6 73.5 all-gather.12
  290.6 56.7 all-gather.10
  419.2 73.0 all-gather.14
